TPU v7x, 256 devices: a whole 4x4x8 slice. The times are simulated.
256 devices in a mesh: section: 16 (over y, z_hi), tensor: 16 (over z_lo, x, core).
Axes of the slice: x: 4, y: 4, z: 8 (z_hi: 4, z_lo: 2; z = z_hi * 2 + z_lo), core: 2. Of those that a mesh axis runs over, the one named last changes fastest.
Arguments:
- entering_streams: bfloat16 [16, 4, 128, 5120], P('section', None, 'tensor'), may hold values from -6 to 6
- entering_grads: bfloat16 [16, 4, 128, 5120], P('section', None, 'tensor'), may hold values from -6 to 6
- fresh_streams: bfloat16 [1, 4, 128, 5120], P(None, None, 'tensor'), may hold values from -6 to 6
- loss_grads: bfloat16 [1, 4, 128, 5120], P(None, None, 'tensor'), may hold values from -6 to 6
- stashed: bfloat16 [2, 16, 4, 128, 5120], P(None, 'section', None, 'tensor'), may hold values from -6 to 6
- slot_order: int32 [16, 2], replicated, may hold values from 0 to 1, each once within a row
- q_weight: bfloat16 [16, 5120, 6144], P('section', None, 'tensor'), may hold values from -0.078125 to 0.078125
- kv_weight: bfloat16 [16, 2, 5120, 1024], P('section', None, None, 'tensor'), may hold values from -0.078125 to 0.078125
- out_weight: bfloat16 [16, 6144, 5120], P('section', 'tensor'), may hold values from -0.15625 to 0.15625
- norm_gain: float32 [16, 5120], P('section'), may hold values from 0.1 to 1.9
- head_gains: float32 [16, 2, 128], P('section'), may hold values from 0.6 to 1.8
- stream_in: float32 [16, 4], P('section'), may hold values from 0.1 to 0.6
- stream_out: float32 [16, 4], P('section'), may hold values from 0.5 to 1.5
- stream_mix: float32 [16, 4, 4], P('section'), may hold values from -0.2 to 0.6
Outputs:
- leaving_streams: bfloat16 [16, 4, 128, 5120], P('section', None, 'tensor')
- leaving_grads: bfloat16 [16, 4, 128, 5120], P('section', None, 'tensor')
- evicted: bfloat16 [2, 16, 4, 128, 5120], P(None, 'section', None, 'tensor')
Inputs may be any that keep to these rules, and one draw needn't show every extreme that they name: Each row of slot_order is a permutation of 0 to 1.
All inputs are finite; a program needn't handle non-finite values.
Results may differ from a plain program's by a relative error of at most 0.04.
Values may be sent and summed in bfloat16 or wider, within the bound.
No kernel may reach another device: no remote copies, remote signals or barrier semaphores. Data moves between devices by JAX's collectives and lax.ppermute only.
A program may use at most 128 MiB of HBM per device.

v0:
```python
import math

import jax
import jax.numpy as jnp
from jax import lax
from jax.sharding import PartitionSpec as P

EPSILON = 1e-06
ROPE_BASE = 1000000.0


def swapped(value, axis, stride):
    mask = 2**stride
    pairs = [(source, source ^ mask) for source in range(lax.axis_size(axis))]
    return lax.ppermute(value, axis, pairs)


def passed_along(value, axis, by):
    size = lax.axis_size(axis)
    pairs = [(i, i + by) for i in range(size) if 0 <= i + by < size]
    return lax.ppermute(value, axis, pairs)


def rope_tables(row_count, head_width):
    half_width = head_width // 2
    position = jnp.arange(row_count, dtype=jnp.float32)[:, None]
    frequency = ROPE_BASE ** (-jnp.arange(half_width, dtype=jnp.float32) / half_width)
    angles = position * frequency[None, :]
    return (jnp.cos(angles), jnp.sin(angles))


def rotate_half(values, cosine, sine_table):
    half_width = values.shape[-1] // 2
    first_half = values[..., :half_width]
    second_half = values[..., half_width:]
    cos_rows = cosine[:, None, :]
    sin_rows = sine_table[:, None, :]
    return jnp.concatenate(
        [
            first_half * cos_rows - second_half * sin_rows,
            second_half * cos_rows + first_half * sin_rows,
        ],
        axis=-1,
    )


def head_norm(values, scaling):
    return values * lax.rsqrt(jnp.mean(values * values, axis=-1, keepdims=True) + EPSILON) * scaling


def attend_group(queries, key_rows, value_rows, head_gains):
    row_count = queries.shape[0]
    head_width = key_rows.shape[1]
    head_count = queries.shape[1] // head_width
    cosine, sine_table = rope_tables(row_count, head_width)
    query_heads = rotate_half(
        head_norm(queries.reshape(row_count, head_count, head_width), head_gains[0]),
        cosine,
        sine_table,
    )
    key_heads = rotate_half(
        head_norm(key_rows.reshape(row_count, 1, head_width), head_gains[1]), cosine, sine_table
    )[:, 0]
    scores = jnp.einsum("qhc,kc->hqk", query_heads, key_heads) / math.sqrt(head_width)
    causal = jnp.arange(row_count)[:, None] >= jnp.arange(row_count)[None, :]
    scores = jnp.where(causal[None], scores, -1e30)
    scores = scores - lax.stop_gradient(jnp.max(scores, axis=-1, keepdims=True))
    exp_scores = jnp.exp(scores)
    probability = exp_scores / jnp.sum(exp_scores, axis=-1, keepdims=True)
    rounded = lax.optimization_barrier(probability.astype(jnp.bfloat16)).astype(jnp.float32)
    context = jnp.einsum("hqk,kc->qhc", rounded, value_rows)
    return context.reshape(row_count, head_count * head_width)


def mixed_input(streams_now, stream_in, norm_gain):
    combined = jnp.sum(stream_in[:, None, None] * streams_now, axis=0)
    return (
        combined
        * lax.rsqrt(jnp.mean(combined * combined, axis=-1, keepdims=True) + EPSILON)
        * norm_gain
    )


def order_halves(own_part, other_part, parity):
    return jnp.where(
        parity == 0,
        jnp.concatenate([own_part, other_part], axis=-1),
        jnp.concatenate([other_part, own_part], axis=-1),
    )


def project_rows(normed, joined_w, query_width, parity):
    projected = jnp.dot(
        lax.all_gather(normed, "tensor", axis=0, tiled=True),
        joined_w,
        preferred_element_type=jnp.float32,
    ).astype(jnp.bfloat16)
    kv_width = (projected.shape[1] - query_width) // 2
    queries = projected[:, :query_width]
    key_rows = projected[:, query_width : query_width + kv_width]
    value_rows = projected[:, query_width + kv_width :]
    stacked = jnp.stack([key_rows, value_rows])
    received = swapped(stacked, "tensor", 0)
    stacked = order_halves(stacked, received, parity)
    key_rows = stacked[0]
    value_rows = stacked[1]
    return (queries, key_rows, value_rows)


def on_device(
    entering_streams,
    entering_grads,
    fresh_streams,
    loss_grads,
    stashed,
    slot_order,
    q_weight,
    kv_weight,
    out_weight,
    norm_gain,
    head_gains,
    stream_in,
    stream_out,
    stream_mix,
):
    section_count = lax.axis_size("section")
    section_here = lax.axis_index("section")
    pair_bit = section_count.bit_length() - 2
    partner = (section_here + section_count // 2) % section_count
    parity = lax.axis_index("tensor") % 2
    queries_w = q_weight[0]
    halves_w = kv_weight[0]
    output_w = out_weight[0]
    gain_row = norm_gain[0]
    norm_gains = head_gains[0]
    mix_in = stream_in[0]
    mix_out = stream_out[0]
    mix_streams = stream_mix[0]
    query_width = queries_w.shape[1]
    half_width = halves_w.shape[2]
    joined_w = jnp.concatenate([queries_w, halves_w[0], halves_w[1]], axis=1)

    def pre_layer(streams_now):
        return mixed_input(streams_now, mix_in, gain_row)

    def forward_front(streams):
        streams_f = streams.astype(jnp.float32)
        normed = pre_layer(streams_f).astype(jnp.bfloat16)
        queries, key_rows, value_rows = project_rows(normed, joined_w, query_width, parity)
        context = attend_group(
            queries.astype(jnp.float32),
            key_rows.astype(jnp.float32),
            value_rows.astype(jnp.float32),
            norm_gains,
        ).astype(jnp.bfloat16)

        def output_terms(start, count):
            return jnp.dot(context, output_w, preferred_element_type=jnp.float32)

        return (streams_f, output_terms)

    def backward_front(saved, grads):
        streams_f = saved.astype(jnp.float32)
        grads_f = grads.astype(jnp.float32)
        normed_f, pre_back = jax.vjp(pre_layer, streams_f)
        queries, key_rows, value_rows = project_rows(
            normed_f.astype(jnp.bfloat16), joined_w, query_width, parity
        )
        out_grad = jnp.tensordot(mix_out, grads_f, axes=1, precision=lax.Precision.HIGHEST).astype(
            jnp.bfloat16
        )
        context_grad = jnp.einsum(
            "rd,cd->rc",
            lax.all_gather(out_grad, "tensor", axis=0, tiled=True),
            output_w,
            preferred_element_type=jnp.float32,
        )

        def attend_inputs(query_in, key_in, value_in):
            return attend_group(query_in, key_in, value_in, norm_gains)

        _, attend_back = jax.vjp(
            attend_inputs,
            queries.astype(jnp.float32),
            key_rows.astype(jnp.float32),
            value_rows.astype(jnp.float32),
        )
        query_grad, key_grad, value_grad = attend_back(context_grad)
        query_grad = query_grad.astype(jnp.bfloat16)
        kv_grads = jnp.stack([key_grad, value_grad]).astype(jnp.bfloat16)
        own_part = jnp.where(parity == 0, kv_grads[..., :half_width], kv_grads[..., half_width:])
        other_part = jnp.where(parity == 0, kv_grads[..., half_width:], kv_grads[..., :half_width])
        received = swapped(other_part, "tensor", 0)
        term_pairs = [(own_part, halves_w), (received, halves_w)]

        def input_terms(start, count):
            total = jnp.einsum(
                "rc,dc->rd", query_grad, queries_w, preferred_element_type=jnp.float32
            )
            for grads_part, weight_part in term_pairs:
                total = total + jnp.einsum(
                    "krc,kdc->rd", grads_part, weight_part, preferred_element_type=jnp.float32
                )
            return total

        return (grads_f, pre_back, input_terms)

    stash_here = stashed[:, 0]
    tick_count = stash_here.shape[0]
    forward_now = entering_streams[0]
    backward_now = entering_grads[0]
    inputs_list = []
    forward_out = forward_now
    backward_out = backward_now
    for step_index in range(tick_count):
        held_slot = slot_order[partner, step_index]
        held_piece = lax.dynamic_index_in_dim(stash_here, held_slot, 0, keepdims=False)
        evicted_piece, saved = swapped((forward_now, held_piece), "section", pair_bit)
        inputs_list.append(evicted_piece)
        row_count = forward_now.shape[1]
        run_streams_f, run_output_terms = forward_front(forward_now)
        run_grads_f, run_pre_back, run_input_terms = backward_front(saved, backward_now)
        run_output_rows = lax.psum_scatter(
            run_output_terms(jnp.int32(0), lax.axis_size("tensor") * row_count).astype(
                jnp.bfloat16
            ),
            "tensor",
            scatter_dimension=0,
            tiled=True,
        ).astype(jnp.float32)
        run_normed_grad = lax.psum_scatter(
            run_input_terms(jnp.int32(0), lax.axis_size("tensor") * row_count).astype(jnp.bfloat16),
            "tensor",
            scatter_dimension=0,
            tiled=True,
        ).astype(jnp.float32)
        mixed = (
            jnp.tensordot(mix_streams, run_streams_f, axes=1, precision=lax.Precision.HIGHEST)
            + mix_out[:, None, None] * run_output_rows[None]
        )
        forward_out = mixed.astype(jnp.bfloat16)
        streams_grad = (
            jnp.tensordot(mix_streams.T, run_grads_f, axes=1, precision=lax.Precision.HIGHEST)
            + run_pre_back(run_normed_grad)[0]
        )
        backward_out = streams_grad.astype(jnp.bfloat16)
        if step_index + 1 < tick_count:
            from_previous = passed_along(forward_out, "section", 1)
            from_following = passed_along(backward_out, "section", -1)
            forward_now = jnp.where(section_here == 0, fresh_streams[step_index], from_previous)
            backward_now = jnp.where(
                section_here == section_count - 1, loss_grads[step_index], from_following
            )
    stacked_inputs = jnp.stack(inputs_list)
    return (forward_out[None], backward_out[None], stacked_inputs[:, None])


def solution(mesh):
    return jax.shard_map(
        on_device,
        mesh=mesh,
        in_specs=(
            P("section", None, "tensor", None),
            P("section", None, "tensor", None),
            P(None, None, "tensor", None),
            P(None, None, "tensor", None),
            P(None, "section", None, "tensor", None),
            P(),
            P("section", None, "tensor"),
            P("section", None, None, "tensor"),
            P("section", "tensor", None),
            P("section", None),
            P("section", None, None),
            P("section", None),
            P("section", None),
            P("section", None, None),
        ),
        out_specs=(
            P("section", None, "tensor", None),
            P("section", None, "tensor", None),
            P(None, "section", None, "tensor", None),
        ),
        check_vma=False,
    )
```

profile of v0, /device:TPU:1, one launch (start us, length us, event | category | flops | bytes accessed | tf_op | source)
XLA Modules:
  0.0 584.1 jit_solution(9128281016580400197)
XLA Ops:
  14.4 35.8 %all-gather.7.cloned.1.call-done = bf16[128,5120]{1,0:T(8,128)(2,1)} async-done(((bf16[8,5120]{1,0:T(8,128)(2,1)}), bf16[128,5120]{1,0:T(8,128)(2,1)}) %all-gather.7.cloned.1.call-update) | async-done | bytes 1310736 | tf_op jit(solution)/shard_map/all_gather | solution.py:94
  50.2 3.9 convolution_convert_fusion.5
  57.1 4.1 convolution_convert_fusion.1
  66.2 2.9 collective-permute-start.3
  69.6 53.1 %reduce-scatter.5.cloned.1.call-done = bf16[8,5120]{1,0:T(8,128)(2,1)} async-done(((bf16[128,5120]{1,0:T(8,128)(2,1)}), bf16[8,5120]{1,0:T(8,128)(2,1)}) %reduce-scatter.5.cloned.1.call-update) | async-done | bytes 81936 | tf_op jit(solution)/shard_map/reduce_scatter | solution.py:223
  124.4 4.0 collective-permute-start.1
  129.8 3.5 collective-permute-done.1
  138.3 29.8 %all-gather.11.cloned.1.call-done = bf16[128,5120]{1,0:T(8,128)(2,1)} async-done(((bf16[8,5120]{1,0:T(8,128)(2,1)}), bf16[128,5120]{1,0:T(8,128)(2,1)}) %all-gather.11.cloned.1.call-update) | async-done | bytes 1310736 | tf_op jit(solution)/shard_map/all_gather | solution.py:174
  168.1 3.9 fusion.30
  172.1 31.6 %all-gather.13.cloned.1.call-done = bf16[128,5120]{1,0:T(8,128)(2,1)} async-done(((bf16[8,5120]{1,0:T(8,128)(2,1)}), bf16[128,5120]{1,0:T(8,128)(2,1)}) %all-gather.13.cloned.1.call-update) | async-done | bytes 1310736 | tf_op jit(solution)/shard_map/all_gather | solution.py:94
  203.7 3.9 convolution_convert_fusion.3
  207.8 33.5 %all-gather.9.cloned.1.call-done = bf16[128,5120]{1,0:T(8,128)(2,1)} async-done(((bf16[8,5120]{1,0:T(8,128)(2,1)}), bf16[128,5120]{1,0:T(8,128)(2,1)}) %all-gather.9.cloned.1.call-update) | async-done | bytes 1310736 | tf_op jit(solution)/shard_map/all_gather | solution.py:94
  241.4 3.9 convolution_convert_fusion.4
  245.6 32.9 %all-gather.17.cloned.1.call-done = bf16[128,5120]{1,0:T(8,128)(2,1)} async-done(((bf16[8,5120]{1,0:T(8,128)(2,1)}), bf16[128,5120]{1,0:T(8,128)(2,1)}) %all-gather.17.cloned.1.call-update) | async-done | bytes 1310736 | tf_op jit(solution)/shard_map/all_gather | solution.py:94
  278.5 4.3 convolution_convert_fusion.2
  287.7 1.9 fusion.165
  298.6 2.1 convolution_bitcast_fusion.3
  301.9 4.3 convolution_add_fusion.1
  308.2 60.7 %reduce-scatter.9.cloned.1.call-done = bf16[8,5120]{1,0:T(8,128)(2,1)} async-done(((bf16[128,5120]{1,0:T(8,128)(2,1)}), bf16[8,5120]{1,0:T(8,128)(2,1)}) %reduce-scatter.9.cloned.1.call-update) | async-done | bytes 81936 | tf_op jit(solution)/shard_map/reduce_scatter | solution.py:231
  370.9 1.9 fusion.12
  374.1 16.3 %collective-permute-done.6 = bf16[4,8,5120]{2,0,1:T(4,128)(2,1)} collective-permute-done((bf16[4,8,5120]{2,0,1:T(4,128)(2,1)}, bf16[4,8,5120]{2,0,1:T(4,128)(2,1)}, u32[]{:S(2)}, u32[]{:S(2)}) %collective-permute-start.6) | collective-permute-done | bytes 327712 | tf_op jit(solution)/shard_map/ppermute | solution.py:21
  390.4 1.8 fusion.109
  393.1 2.8 collective-permute-start.2
  398.2 34.4 %all-gather.15.cloned.1.call-done = bf16[128,5120]{1,0:T(8,128)(2,1)} async-done(((bf16[8,5120]{1,0:T(8,128)(2,1)}), bf16[128,5120]{1,0:T(8,128)(2,1)}) %all-gather.15.cloned.1.call-update) | async-done | bytes 1310736 | tf_op jit(solution)/shard_map/all_gather | solution.py:174
  432.6 3.8 fusion.33
  442.3 4.1 convolution_convert_fusion
  454.0 2.9 collective-permute-start.10
  457.3 7.4 %collective-permute-done.10 = bf16[4,8,5120]{2,0,1:T(4,128)(2,1)S(1)} collective-permute-done((bf16[4,8,5120]{2,0,1:T(4,128)(2,1)S(1)}, bf16[4,8,5120]{2,0,1:T(4,128)(2,1)S(1)}, u32[]{:S(2)}, u32[]{:S(2)}) %collective-permute-start.10) | collective-permute-done | bytes 327712 | tf_op jit(solution)/shard_map/ppermute | solution.py:15
  464.6 7.0 %collective-permute-done.11 = bf16[4,8,5120]{2,0,1:T(4,128)(2,1)S(1)} collective-permute-done((bf16[4,8,5120]{2,0,1:T(4,128)(2,1)S(1)}, bf16[4,8,5120]{2,0,1:T(4,128)(2,1)S(1)}, u32[]{:S(2)}, u32[]{:S(2)}) %collective-permute-start.11) | collective-permute-done | bytes 327712 | tf_op jit(solution)/shard_map/ppermute | solution.py:15
  473.1 34.5 %reduce-scatter.7.cloned.1.call-done = bf16[8,5120]{1,0:T(8,128)(2,1)} async-done(((bf16[128,5120]{1,0:T(8,128)(2,1)}), bf16[8,5120]{1,0:T(8,128)(2,1)}) %reduce-scatter.7.cloned.1.call-update) | async-done | bytes 81936 | tf_op jit(solution)/shard_map/reduce_scatter | solution.py:223
  510.1 62.2 %reduce-scatter.11.cloned.1.call-done = bf16[8,5120]{1,0:T(8,128)(2,1)} async-done(((bf16[128,5120]{1,0:T(8,128)(2,1)}), bf16[8,5120]{1,0:T(8,128)(2,1)}) %reduce-scatter.11.cloned.1.call-update) | async-done | bytes 81936 | tf_op jit(solution)/shard_map/reduce_scatter | solution.py:231
  574.4 1.8 fusion.14
  (275 shorter events, 63.7 us)
Async XLA Ops:
  7.2 121.2 %copy-start = (bf16[1,4,8,5120]{3,2,1,0:T(8,128)(2,1)S(1)}, bf16[1,4,8,5120]{3,2,1,0:T(8,128)(2,1)}, u32[]{:S(2)}) copy-start(bf16[1,4,8,5120]{3,2,1,0:T(8,128)(2,1)} %param.15) | copy-start | bytes 983044
  7.2 43.0 %all-gather.7.cloned.1.call-start = ((), (), s32[]{:S(2)}) async-start(), calls=%async_computation.4 | async-start | bytes 1392640 | tf_op jit(solution)/shard_map/all_gather | solution.py:94
  10.5 112.2 %reduce-scatter.5.cloned.1.call-start = ((), (), s32[]{:S(2)}) async-start(), calls=%async_computation.5 | async-start | bytes 1392640 | tf_op jit(solution)/shard_map/reduce_scatter | solution.py:223
  54.5 1.3 collective-permute-start
  61.3 106.9 %all-gather.11.cloned.1.call-start = ((), (), s32[]{:S(2)}) async-start(), calls=%async_computation.8 | async-start | bytes 1392640 | tf_op jit(solution)/shard_map/all_gather | solution.py:174
  66.2 63.6 %collective-permute-start.3 = (bf16[4,8,5120]{2,0,1:T(4,128)(2,1)S(1)}, bf16[4,8,5120]{2,0,1:T(4,128)(2,1)S(1)}, u32[]{:S(2)}, u32[]{:S(2)}) collective-permute-start(bf16[4,8,5120]{2,0,1:T(4,128)(2,1)S(1)} %bitcast.416), channel_id=1, source_target_pairs={{0,128},{16,144},{32,160},{48,176},{64,192},{80,208},{96,224},{112... | collective-permute-start | bytes 983048 | tf_op jit(solution)/shard_map/ppermute | solution.py:15
  69.3 60.5 %collective-permute-start.7 = (bf16[4,8,5120]{2,0,1:T(4,128)(2,1)S(1)}, bf16[4,8,5120]{2,0,1:T(4,128)(2,1)S(1)}, u32[]{:S(2)}, u32[]{:S(2)}) collective-permute-start(bf16[4,8,5120]{2,0,1:T(4,128)(2,1)S(1)} %bitcast.417), channel_id=1, source_target_pairs={{0,128},{16,144},{32,160},{48,176},{64,192},{80,208},{96,224},{112... | collective-permute-start | bytes 983048 | tf_op jit(solution)/shard_map/ppermute | solution.py:15
  124.4 9.0 %collective-permute-start.1 = (bf16[4,8,5120]{2,0,1:T(4,128)(2,1)S(1)}, bf16[4,8,5120]{2,0,1:T(4,128)(2,1)S(1)}, u32[]{:S(2)}, u32[]{:S(2)}) collective-permute-start(bf16[4,8,5120]{2,0,1:T(4,128)(2,1)S(1)} %fusion.10), channel_id=1, source_target_pairs={{0,16},{16,32},{32,48},{48,64},{64,80},{80,96},{96,112},{112,128},... | collective-permute-start | bytes 983048 | tf_op jit(solution)/shard_map/ppermute | solution.py:21
  129.7 73.9 %all-gather.13.cloned.1.call-start = ((), (), s32[]{:S(2)}) async-start(), calls=%async_computation.9 | async-start | bytes 1392640 | tf_op jit(solution)/shard_map/all_gather | solution.py:94
  136.6 104.7 %all-gather.9.cloned.1.call-start = ((), (), s32[]{:S(2)}) async-start(), calls=%async_computation.6 | async-start | bytes 1392640 | tf_op jit(solution)/shard_map/all_gather | solution.py:94
  137.2 141.3 %all-gather.17.cloned.1.call-start = ((), (), s32[]{:S(2)}) async-start(), calls=%async_computation.12 | async-start | bytes 1392640 | tf_op jit(solution)/shard_map/all_gather | solution.py:94
  137.8 231.1 %reduce-scatter.9.cloned.1.call-start = ((), (), s32[]{:S(2)}) async-start(), calls=%async_computation.10 | async-start | bytes 1392640 | tf_op jit(solution)/shard_map/reduce_scatter | solution.py:231
  283.9 12.1 %collective-permute-start.8 = (bf16[2,128,64]{2,1,0:T(8,128)(2,1)}, bf16[2,128,64]{2,1,0:T(8,128)(2,1)}, u32[]{:S(2)}, u32[]{:S(2)}) collective-permute-start(bf16[2,128,64]{2,1,0:T(8,128)(2,1)} %pad_maximum_fusion.8), channel_id=1, source_target_pairs={{0,1},{1,0},{2,3},{3,2},{4,5},{5,4},{6,7},{7,6},{8,9},{9,8},{10,11... | collective-permute-start | bytes 98312 | tf_op jit(solution)/shard_map/ppermute | solution.py:15
  284.2 1.6 collective-permute-start.4
  301.6 4.7 collective-permute-start.5
  307.9 82.5 %copy-start.50 = (f32[1,4]{1,0:T(1,128)S(1)}, f32[1,4]{1,0:T(1,128)}, u32[]{:S(2)}) copy-start(f32[1,4]{1,0:T(1,128)} %param.26) | copy-start | bytes 52
  307.9 85.0 %copy-start.11 = (bf16[128,512]{1,0:T(8,128)(2,1)S(1)}, bf16[128,512]{1,0:T(8,128)(2,1)}, u32[]{:S(2)}) copy-start(bf16[128,512]{1,0:T(8,128)(2,1)} %copy-done.10) | copy-start | bytes 393220
  307.9 89.9 %copy-start.12 = (bf16[128,3,64]{2,0,1:T(8,128)(2,1)S(1)}, bf16[128,3,64]{2,0,1:T(8,128)(2,1)}, u32[]{:S(2)}) copy-start(bf16[128,3,64]{2,0,1:T(8,128)(2,1)} %get-tuple-element.37) | copy-start | bytes 147460
  308.0 89.9 %copy-start.13 = (bf16[128,3,64]{2,0,1:T(8,128)(2,1)S(1)}, bf16[128,3,64]{2,0,1:T(8,128)(2,1)}, u32[]{:S(2)}) copy-start(bf16[128,3,64]{2,0,1:T(8,128)(2,1)} %get-tuple-element.38) | copy-start | bytes 147460
  308.0 89.9 %copy-start.23 = (pred[128,128]{0,1:T(8,128)(4,1)S(1)}, pred[128,128]{0,1:T(8,128)(4,1)}, u32[]{:S(2)}) copy-start(pred[128,128]{0,1:T(8,128)(4,1)} %copy-done.22) | copy-start | bytes 49156
  308.0 124.6 %all-gather.15.cloned.1.call-start = ((), (), s32[]{:S(2)}) async-start(), calls=%async_computation.11 | async-start | bytes 1392640 | tf_op jit(solution)/shard_map/all_gather | solution.py:174
  372.8 17.6 %collective-permute-start.6 = (bf16[4,8,5120]{2,0,1:T(4,128)(2,1)}, bf16[4,8,5120]{2,0,1:T(4,128)(2,1)}, u32[]{:S(2)}, u32[]{:S(2)}) collective-permute-start(bf16[4,8,5120]{2,0,1:T(4,128)(2,1)} %fusion.12), channel_id=1, source_target_pairs={{16,0},{32,16},{48,32},{64,48},{80,64},{96,80},{112,96},{128,112},... | collective-permute-start | bytes 983048 | tf_op jit(solution)/shard_map/ppermute | solution.py:21
  392.9 114.8 %reduce-scatter.7.cloned.1.call-start = ((), (), s32[]{:S(2)}) async-start(), calls=%async_computation.7 | async-start | bytes 1392640 | tf_op jit(solution)/shard_map/reduce_scatter | solution.py:223
  393.1 3.7 collective-permute-start.2
  446.4 125.9 %reduce-scatter.11.cloned.1.call-start = ((), (), s32[]{:S(2)}) async-start(), calls=%async_computation.13 | async-start | bytes 1392640 | tf_op jit(solution)/shard_map/reduce_scatter | solution.py:231
  448.8 3.2 collective-permute-start.9
  453.7 119.7 %copy-start.40 = (f32[8]{0:T(128)S(1)}, f32[8]{0:T(128)}, u32[]{:S(2)}) copy-start(f32[8]{0:T(128)} %copy-done.39) | copy-start | bytes 100
  453.7 119.7 %copy-start.31 = (f32[8]{0:T(128)S(1)}, f32[8]{0:T(128)}, u32[]{:S(2)}) copy-start(f32[8]{0:T(128)} %copy-done.30) | copy-start | bytes 100
  454.0 120.4 %copy-start.36 = (f32[1,4]{1,0:T(1,128)S(1)}, f32[1,4]{1,0:T(1,128)}, u32[]{:S(2)}) copy-start(f32[1,4]{1,0:T(1,128)} %param.25) | copy-start | bytes 52
  454.0 120.4 %copy-start.45 = (bf16[1,4,8,5120]{3,2,1,0:T(8,128)(2,1)S(1)}, bf16[1,4,8,5120]{3,2,1,0:T(8,128)(2,1)}, u32[]{:S(2)}) copy-start(bf16[1,4,8,5120]{3,2,1,0:T(8,128)(2,1)} %param.17) | copy-start | bytes 983044
  454.0 10.6 %collective-permute-start.10 = (bf16[4,8,5120]{2,0,1:T(4,128)(2,1)S(1)}, bf16[4,8,5120]{2,0,1:T(4,128)(2,1)S(1)}, u32[]{:S(2)}, u32[]{:S(2)}) collective-permute-start(bf16[4,8,5120]{2,0,1:T(4,128)(2,1)S(1)} %bitcast.418), channel_id=1, source_target_pairs={{0,128},{16,144},{32,160},{48,176},{64,192},{80,208},{96,224},{112... | collective-permute-start | bytes 983048 | tf_op jit(solution)/shard_map/ppermute | solution.py:15
  456.9 14.8 %collective-permute-start.11 = (bf16[4,8,5120]{2,0,1:T(4,128)(2,1)S(1)}, bf16[4,8,5120]{2,0,1:T(4,128)(2,1)S(1)}, u32[]{:S(2)}, u32[]{:S(2)}) collective-permute-start(bf16[4,8,5120]{2,0,1:T(4,128)(2,1)S(1)} %copy-done.9), channel_id=1, source_target_pairs={{0,128},{16,144},{32,160},{48,176},{64,192},{80,208},{96,224},{112... | collective-permute-start | bytes 983048 | tf_op jit(solution)/shard_map/ppermute | solution.py:15
  (42 other events, 1151.2 us)
Sparse Core Ops, SparseCore 0:
  10.6 39.5 all-gather.6
  61.4 61.2 reduce-scatter.4
  129.9 38.2 all-gather.10
  170.4 33.2 all-gather.12
  206.0 35.3 all-gather.8
  243.1 35.3 all-gather.16
  308.1 60.7 reduce-scatter.8
  393.0 39.5 all-gather.14
  446.5 61.0 reduce-scatter.6
  510.0 62.2 reduce-scatter.10
where the time goes:
time: 595 us; the launch traced here: 584 us
  waiting for transfers between devices  446 us (75%)
  matrix products  61.6 us (10%)
  other arithmetic  25.3 us (4%)
  between operations  19.6 us (3%)
  starting transfers between devices  17.1 us (3%)
  local copies, waits for them, and re-layouts  14.9 us (3%)
    all_gather x4, waiting for transfers between devices, project_rows(): lax.all_gather(normed, 'tensor', axis=0, tiled=True)  134 us
    reduce_scatter x2, waiting for transfers between devices, on_device(): lax.psum_scatter(run_input_terms(jnp.int32(0), lax.axis_size('tensor') *...  123 us
    reduce_scatter x2, waiting for transfers between devices, on_device(): lax.psum_scatter(run_output_terms(jnp.int32(0), lax.axis_size('tensor') *...  87.6 us
    all_gather x2, waiting for transfers between devices, backward_front(): lax.all_gather(out_grad, 'tensor', axis=0, tiled=True)  64.2 us
    ppermute x2, waiting for transfers between devices, passed_along(): return lax.ppermute(value, axis, pairs)  19.8 us
    ppermute x10, waiting for transfers between devices, swapped(): return lax.ppermute(value, axis, pairs)  16 us
    dot_general x4, matrix products, project_rows(): jnp.dot(lax.all_gather(normed, 'tensor', axis=0, tiled=True), joined_w, p...  15.8 us
  transfers between devices with their start and end apart: 22, of which 16 were waited for; matrix products, arithmetic and copies ran while one was open for 8% of the time, Pallas kernels for 0%

commit v1 on v0

v1 whole, which is shorter than its diff:
```python
import math

import jax
import jax.numpy as jnp
import numpy as np
from jax import lax
from jax.experimental import pallas as pl
from jax.experimental.pallas import tpu as pltpu
from jax.sharding import PartitionSpec as P

EPSILON = 1e-06
ROPE_BASE = 1000000.0
ROWS = 128
LOCAL = 8
HEAD = 128
WIDTH = 5120
CHUNK = 1280
STEPS = WIDTH // CHUNK
QUERY = 384
BOTH = 256
GROUPS = [[core + 2 * chip for chip in range(8)] for core in range(2)]


def other_core(value):
    return lax.ppermute(value, "tensor", [(i, i ^ 1) for i in range(16)])


def to_partner(value):
    return lax.ppermute(value, "section", [(i, i ^ 8) for i in range(16)])


def shifted(value, by):
    return lax.ppermute(value, "section", [(i, (i + by) % 16) for i in range(16)])


def token_order(parity):
    own = [2 * chip + parity for chip in range(8)]
    other = [2 * chip + 1 - parity for chip in range(8)]
    return np.concatenate([np.arange(LOCAL) + LOCAL * block for block in own + other])


def rope_of(order):
    half = HEAD // 2
    position = jnp.asarray(order, jnp.float32)[:, None]
    frequency = ROPE_BASE ** (-jnp.arange(half, dtype=jnp.float32) / half)
    angles = position * frequency[None, :]
    return jnp.stack([jnp.cos(angles), jnp.sin(angles)])


def dot(left, right):
    return jnp.dot(left, right, preferred_element_type=jnp.float32)


def dot_nt(left, right):
    return lax.dot_general(left, right, (((1,), (1,)), ((), ())), preferred_element_type=jnp.float32)


def dot_tn(left, right):
    return lax.dot_general(left, right, (((0,), (0,)), ((), ())), preferred_element_type=jnp.float32)


def rope(values, cosine, sine):
    return values * cosine + pltpu.roll(values, HEAD // 2, 1) * sine


def rope_back(grads, cosine, sine):
    return grads * cosine - pltpu.roll(grads, HEAD // 2, 1) * sine


def norm_scale(values):
    return lax.rsqrt(jnp.mean(values * values, axis=-1, keepdims=True) + EPSILON)


def head_back(grads, values, scale, gain):
    weighted = grads * gain
    inner = jnp.mean(values * weighted, axis=-1, keepdims=True)
    return scale * weighted - values * (scale * scale * scale * inner)


def softmax_of(query_head, key_head, mask):
    scores = dot_nt(query_head, key_head) * (1.0 / math.sqrt(HEAD)) + mask
    scores = scores - jnp.max(scores, axis=-1, keepdims=True)
    weights = jnp.exp(scores)
    return weights / jnp.sum(weights, axis=-1, keepdims=True)


def attend(projected, gains, cosine, sine, mask):
    bf16, f32 = jnp.bfloat16, jnp.float32
    keys = projected[:, QUERY : QUERY + HEAD].astype(f32)
    key_head = rope(keys * norm_scale(keys) * gains[1:2], cosine, sine).astype(bf16)
    values = projected[:, QUERY + HEAD :]
    context = []
    for head in range(QUERY // HEAD):
        queries = projected[:, head * HEAD : (head + 1) * HEAD].astype(f32)
        query_head = rope(queries * norm_scale(queries) * gains[0:1], cosine, sine).astype(bf16)
        weights = softmax_of(query_head, key_head, mask)
        context.append(dot(weights.astype(bf16), values).astype(bf16))
    return jnp.concatenate(context, axis=1)


def attend_back(projected, context_grad, gains, cosine, sine, mask):
    bf16, f32 = jnp.bfloat16, jnp.float32
    root = 1.0 / math.sqrt(HEAD)
    keys = projected[:, QUERY : QUERY + HEAD].astype(f32)
    key_scale = norm_scale(keys)
    key_head = rope(keys * key_scale * gains[1:2], cosine, sine).astype(bf16)
    values = projected[:, QUERY + HEAD :]
    query_grads = []
    key_total = jnp.zeros((ROWS, HEAD), f32)
    value_total = jnp.zeros((ROWS, HEAD), f32)
    for head in range(QUERY // HEAD):
        queries = projected[:, head * HEAD : (head + 1) * HEAD].astype(f32)
        query_scale = norm_scale(queries)
        query_head = rope(queries * query_scale * gains[0:1], cosine, sine).astype(bf16)
        weights = softmax_of(query_head, key_head, mask)
        upstream = context_grad[:, head * HEAD : (head + 1) * HEAD].astype(bf16)
        value_total = value_total + dot_tn(weights.astype(bf16), upstream)
        weights_grad = dot_nt(upstream, values).astype(bf16).astype(f32)
        inner = jnp.sum(weights * weights_grad, axis=-1, keepdims=True)
        scores_grad = (weights * (weights_grad - inner) * root).astype(bf16)
        key_total = key_total + dot_tn(scores_grad, query_head)
        turned = rope_back(dot(scores_grad, key_head), cosine, sine)
        query_grads.append(head_back(turned, queries, query_scale, gains[0:1]).astype(bf16))
    key_grad = head_back(rope_back(key_total, cosine, sine), keys, key_scale, gains[1:2])
    both = jnp.concatenate([key_grad.astype(bf16), value_total.astype(bf16)], axis=1)
    return jnp.concatenate(query_grads, axis=1), both


def forward_kernel(
    own, other, queries_w, keys_values_w, output_w, gains, cosine, sine, mask, out, total, context
):
    step = pl.program_id(0)

    @pl.when(step == 0)
    def _():
        total[...] = jnp.zeros_like(total)

    @pl.when(step < STEPS)
    def _():
        rows = jnp.concatenate([own[...], other[...]], axis=0)
        total[:, :QUERY] += dot(rows, queries_w[...])
        total[:, QUERY:] += dot_nt(rows, keys_values_w[...])

    @pl.when(step == STEPS - 1)
    def _():
        projected = total[...].astype(jnp.bfloat16)
        context[...] = attend(projected, gains[...], cosine[...], sine[...], mask[...])

    @pl.when(step >= STEPS)
    def _():
        out[...] = dot(context[...], output_w[...]).astype(out.dtype)


def project_kernel(rows, queries_w, keys_values_w, turn, out, total):
    step = pl.program_id(0)

    @pl.when(step == 0)
    def _():
        total[...] = jnp.zeros_like(total)

    total[:, :QUERY] += dot(rows[...], queries_w[...])
    total[:, QUERY:] += dot_nt(rows[...], keys_values_w[...])

    @pl.when(step == STEPS - 1)
    def _():
        out[...] = dot(turn[...], total[...].astype(jnp.bfloat16)).astype(out.dtype)


def backward_kernel(
    own, other, projected, queries_w, keys_values_w, output_w, gains, cosine, sine, mask, out, total, query_grad, both_grad
):
    step = pl.program_id(0)

    @pl.when(step == 0)
    def _():
        total[...] = jnp.zeros_like(total)

    @pl.when(step < STEPS)
    def _():
        rows = jnp.concatenate([own[...], other[...]], axis=0)
        total[...] += dot_nt(rows, output_w[...])

    @pl.when(step == STEPS - 1)
    def _():
        query_part, both_part = attend_back(
            projected[...], total[...], gains[...], cosine[...], sine[...], mask[...]
        )
        query_grad[...] = query_part
        both_grad[...] = both_part

    @pl.when(step >= STEPS)
    def _():
        part = dot_nt(query_grad[...], queries_w[...]) + dot(both_grad[...], keys_values_w[...])
        out[...] = part.astype(out.dtype)


def first_phase(step):
    return jnp.minimum(step, STEPS - 1)


def second_phase(step):
    return jnp.maximum(step - STEPS, 0)


def whole(shape):
    return pl.BlockSpec(shape, lambda step: (0,) * len(shape))


PARAMS = pltpu.CompilerParams(vmem_limit_bytes=40 * 2**20)
SMALL = [whole((2, HEAD)), whole((ROWS, HEAD)), whole((ROWS, HEAD)), whole((ROWS, ROWS))]


def run_forward(own, other, weights, small):
    return pl.pallas_call(
        forward_kernel,
        grid=(2 * STEPS,),
        out_shape=jax.ShapeDtypeStruct((ROWS, WIDTH), jnp.bfloat16),
        in_specs=[
            pl.BlockSpec((ROWS // 2, CHUNK), lambda step: (0, first_phase(step))),
            pl.BlockSpec((ROWS // 2, CHUNK), lambda step: (0, first_phase(step))),
            pl.BlockSpec((CHUNK, QUERY), lambda step: (first_phase(step), 0)),
            pl.BlockSpec((BOTH, CHUNK), lambda step: (0, first_phase(step))),
            pl.BlockSpec((QUERY, CHUNK), lambda step: (0, second_phase(step))),
        ]
        + SMALL,
        out_specs=pl.BlockSpec((ROWS, CHUNK), lambda step: (0, second_phase(step))),
        scratch_shapes=[
            pltpu.VMEM((ROWS, QUERY + BOTH), jnp.float32),
            pltpu.VMEM((ROWS, QUERY), jnp.bfloat16),
        ],
        compiler_params=PARAMS,
        cost_estimate=pl.CostEstimate(flops=1500000000, bytes_accessed=14000000, transcendentals=50000),
    )(own, other, *weights, *small)


def run_project(rows, weights, turn):
    return pl.pallas_call(
        project_kernel,
        grid=(STEPS,),
        out_shape=jax.ShapeDtypeStruct((ROWS, QUERY + BOTH), jnp.bfloat16),
        in_specs=[
            pl.BlockSpec((ROWS, CHUNK), lambda step: (0, step)),
            pl.BlockSpec((CHUNK, QUERY), lambda step: (step, 0)),
            pl.BlockSpec((BOTH, CHUNK), lambda step: (0, step)),
            whole((ROWS, ROWS)),
        ],
        out_specs=whole((ROWS, QUERY + BOTH)),
        scratch_shapes=[pltpu.VMEM((ROWS, QUERY + BOTH), jnp.float32)],
        compiler_params=PARAMS,
        cost_estimate=pl.CostEstimate(flops=900000000, bytes_accessed=8000000, transcendentals=0),
    )(rows, weights[0], weights[1], turn)


def run_backward(own, other, projected, weights, small):
    return pl.pallas_call(
        backward_kernel,
        grid=(2 * STEPS,),
        out_shape=jax.ShapeDtypeStruct((ROWS, WIDTH), jnp.bfloat16),
        in_specs=[
            pl.BlockSpec((ROWS // 2, CHUNK), lambda step: (0, first_phase(step))),
            pl.BlockSpec((ROWS // 2, CHUNK), lambda step: (0, first_phase(step))),
            whole((ROWS, QUERY + BOTH)),
            pl.BlockSpec((CHUNK, QUERY), lambda step: (second_phase(step), 0)),
            pl.BlockSpec((BOTH, CHUNK), lambda step: (0, second_phase(step))),
            pl.BlockSpec((QUERY, CHUNK), lambda step: (0, first_phase(step))),
        ]
        + SMALL,
        out_specs=pl.BlockSpec((ROWS, CHUNK), lambda step: (0, second_phase(step))),
        scratch_shapes=[
            pltpu.VMEM((ROWS, QUERY), jnp.float32),
            pltpu.VMEM((ROWS, QUERY), jnp.bfloat16),
            pltpu.VMEM((ROWS, BOTH), jnp.bfloat16),
        ],
        compiler_params=PARAMS,
        cost_estimate=pl.CostEstimate(flops=1500000000, bytes_accessed=14000000, transcendentals=50000),
    )(own, other, projected, *weights, *small)


def mixed(weights, offset, stride, streams):
    return sum(weights[offset + i * stride] * streams[i] for i in range(4))


def norm_kernel(mix_in, streams, gain, copies, combined, scale):
    total = mixed(mix_in, 0, 1, streams[...].astype(jnp.float32))
    row_scale = norm_scale(total)
    normed = (total * row_scale * gain[...]).astype(copies.dtype)
    combined[...] = total
    scale[...] = jnp.broadcast_to(row_scale, scale.shape)
    if len(copies.shape) == 2:
        copies[...] = normed
    else:
        for chip in range(8):
            copies[chip] = normed


def grad_kernel(mix_out, grads, copies):
    out_grad = mixed(mix_out, 0, 1, grads[...].astype(jnp.float32)).astype(copies.dtype)
    for chip in range(8):
        copies[chip] = out_grad


def forward_end_kernel(mix_out, mix, landed, streams, out):
    rows = jnp.sum(landed[...].astype(jnp.float32), axis=0)
    streams_f = streams[...].astype(jnp.float32)
    for i in range(4):
        out[i] = (mixed(mix, 4 * i, 1, streams_f) + mix_out[i] * rows).astype(out.dtype)


def backward_end_kernel(mix_in, mix, landed, grads, gain, combined, scale, out):
    weighted = jnp.sum(landed[...].astype(jnp.float32), axis=0) * gain[...]
    row_scale = scale[:, :1]
    inner = jnp.mean(weighted * combined[...], axis=-1, keepdims=True)
    combined_grad = row_scale * weighted - combined[...] * (row_scale * row_scale * row_scale * inner)
    grads_f = grads[...].astype(jnp.float32)
    for j in range(4):
        out[j] = (mixed(mix, j, 4, grads_f) + mix_in[j] * combined_grad).astype(out.dtype)


def plain(kernel, scalars, arrays, outs):
    smem, vmem = pl.BlockSpec(memory_space=pltpu.SMEM), pl.BlockSpec(memory_space=pltpu.VMEM)
    return pl.pallas_call(
        kernel,
        out_shape=[jax.ShapeDtypeStruct(*out) for out in outs],
        in_specs=[smem] * len(scalars) + [vmem] * len(arrays),
        out_specs=[vmem] * len(outs),
        compiler_params=PARAMS,
        cost_estimate=pl.CostEstimate(flops=4000000, bytes_accessed=3000000, transcendentals=0),
    )(*scalars, *arrays)


def gathered(copies):
    own = lax.all_to_all(copies, "tensor", 0, 0, axis_index_groups=GROUPS, tiled=True)
    own = own.reshape(ROWS // 2, -1)
    return own, other_core(own)


def scattered(partial):
    received = other_core(partial[ROWS // 2 :])
    pair = partial[: ROWS // 2].astype(jnp.float32) + received.astype(jnp.float32)
    pair = pair.astype(jnp.bfloat16).reshape(8, LOCAL, -1)
    return lax.all_to_all(pair, "tensor", 0, 0, axis_index_groups=GROUPS, tiled=True)


def on_device(
    entering_streams,
    entering_grads,
    fresh_streams,
    loss_grads,
    stashed,
    slot_order,
    q_weight,
    kv_weight,
    out_weight,
    norm_gain,
    head_gains,
    stream_in,
    stream_out,
    stream_mix,
):
    section = lax.axis_index("section")
    parity = lax.axis_index("tensor") % 2
    partner = (section + 8) % 16
    queries_w, output_w = q_weight[0], out_weight[0]
    gain, gains = norm_gain[0], head_gains[0]
    mix_in, mix_out, mix = stream_in[0], stream_out[0], stream_mix[0]
    bf16, f32 = jnp.bfloat16, jnp.float32

    def chosen(build):
        return jnp.where(parity == 0, build(token_order(0)), build(token_order(1)))

    cosine = chosen(lambda order: jnp.concatenate([rope_of(order)[0]] * 2, axis=1))
    sine = chosen(lambda order: jnp.concatenate([-rope_of(order)[1], rope_of(order)[1]], axis=1))
    mask = chosen(lambda order: jnp.where(order[:, None] >= order[None, :], 0.0, -1e30).astype(f32))
    turn = chosen(lambda order: jnp.asarray(order[:, None] == np.arange(ROWS)[None, :], bf16))

    halves = jnp.swapaxes(kv_weight[0], 1, 2)
    others = other_core(halves)
    keys_values_w = jnp.where(
        parity == 0,
        jnp.concatenate([halves, others], axis=1),
        jnp.concatenate([others, halves], axis=1),
    ).reshape(2 * HEAD, -1)

    weights = (queries_w, keys_values_w, output_w)
    small = (gains, cosine, sine, mask)
    gain_row = gain[None]
    mix_flat = mix.reshape(16)
    row_shape, streams_shape = (LOCAL, WIDTH), (4, LOCAL, WIDTH)

    def normalise(streams, copied):
        first = ((8,) + row_shape if copied else row_shape, bf16)
        outs = [first, (row_shape, f32), ((LOCAL, HEAD), f32)]
        return plain(norm_kernel, [mix_in], [streams, gain_row], outs)

    def out_grad_of(grads):
        return plain(grad_kernel, [mix_out], [grads], [((8,) + row_shape, bf16)])[0]

    def forward_end(streams, landed):
        return plain(forward_end_kernel, [mix_out, mix_flat], [landed, streams], [(streams_shape, bf16)])[0]

    def backward_end(state, grads, landed):
        return plain(
            backward_end_kernel,
            [mix_in, mix_flat],
            [landed, grads, gain_row, *state],
            [(streams_shape, bf16)],
        )[0]

    stash = stashed[:, 0]
    first_slot = slot_order[partner, 0]
    forward_now, backward_now = entering_streams[0], entering_grads[0]
    saved = [
        to_partner(lax.dynamic_index_in_dim(stash, slot, 0, keepdims=False))
        for slot in (first_slot, 1 - first_slot)
    ]
    evicted_first = to_partner(forward_now)

    normed_own, normed_other = gathered(normalise(forward_now, True)[0])
    grad_own, grad_other = gathered(out_grad_of(backward_now))

    states, projected = [], []
    for streams in saved:
        normed, combined, scale = normalise(streams, False)
        states.append((combined, scale))
        rows = lax.all_gather(normed, "tensor", axis=0, tiled=True)
        projected.append(run_project(rows, weights, turn))

    landed = scattered(run_forward(normed_own, normed_other, weights, small))
    forward_out = forward_end(forward_now, landed)
    from_previous = shifted(forward_out, 1)

    landed = scattered(run_backward(grad_own, grad_other, projected[0], weights, small))
    backward_out = backward_end(states[0], backward_now, landed)
    from_following = shifted(backward_out, -1)

    forward_now = jnp.where(section == 0, fresh_streams[0], from_previous)
    evicted_second = to_partner(forward_now)
    normed_own, normed_other = gathered(normalise(forward_now, True)[0])
    landed_forward = scattered(run_forward(normed_own, normed_other, weights, small))

    backward_now = jnp.where(section == 15, loss_grads[0], from_following)
    grad_own, grad_other = gathered(out_grad_of(backward_now))
    landed_backward = scattered(run_backward(grad_own, grad_other, projected[1], weights, small))
    forward_out = forward_end(forward_now, landed_forward)
    backward_out = backward_end(states[1], backward_now, landed_backward)
    evicted = jnp.stack([evicted_first, evicted_second])
    return (forward_out[None], backward_out[None], evicted[:, None])


def solution(mesh):
    return jax.shard_map(
        on_device,
        mesh=mesh,
        in_specs=(
            P("section", None, "tensor", None),
            P("section", None, "tensor", None),
            P(None, None, "tensor", None),
            P(None, None, "tensor", None),
            P(None, "section", None, "tensor", None),
            P(),
            P("section", None, "tensor"),
            P("section", None, None, "tensor"),
            P("section", "tensor", None),
            P("section", None),
            P("section", None, None),
            P("section", None),
            P("section", None),
            P("section", None, None),
        ),
        out_specs=(
            P("section", None, "tensor", None),
            P("section", None, "tensor", None),
            P(None, "section", None, "tensor", None),
        ),
        check_vma=False,
    )
```

time: 595 us -> 253 us (0.43); the launches traced: 584 us -> 251 us
  waiting for transfers between devices: 446 us -> 66.5 us
  matrix products: 61.6 us -> 0 us
  starting transfers between devices: 17.1 us -> 68.4 us
  Pallas kernels: 0 us -> 50.2 us
  local copies, waits for them, and re-layouts: 14.9 us -> 33.2 us
  other arithmetic: 25.3 us -> 14.5 us
    reduce_scatter x4 -> x0, waiting for transfers between devices: 211 us -> none  [the longest x2 123 us: on_device(): lax.psum_scatter(run_input_terms(jnp.int32(0), lax.axis_size('tensor') *...]
    all_gather x6 -> x2, waiting for transfers between devices: 198 us -> 7.04 us  [on_device(): rows = lax.all_gather(normed, 'tensor', axis=0, tiled=True)]
    dot_general x30 -> x0, matrix products: 57.8 us -> none  [the longest x4 15.8 us: project_rows(): jnp.dot(lax.all_gather(normed, 'tensor', axis=0, tiled=True), joined_w, p...]
    pallas_call x0 -> x16, Pallas kernels: none -> 50.2 us  [the longest x2 15.8 us: run_backward(): pl.pallas_call(backward_kernel, grid=(2 * STEPS,), out_shape=jax.ShapeDty...]
    all_to_all x0 -> x8, starting transfers between devices: none -> 36.7 us  [the longest x4 21.1 us: gathered(): lax.all_to_all(copies, 'tensor', 0, 0, axis_index_groups=GROUPS, tiled=True)]
    all_to_all x0 -> x8, waiting for transfers between devices: none -> 31.6 us  [the longest x4 16.6 us: scattered(): lax.all_to_all(pair, 'tensor', 0, 0, axis_index_groups=GROUPS, tiled=True)]
    unnamed x108 -> x94, local copies, waits for them, and re-layouts: 7.29 us -> 29 us
    ppermute x12 -> x15, starting transfers between devices: 16.1 us -> 31.6 us  [the longest x9 14.6 us: other_core(): return lax.ppermute(value, 'tensor', [(i, i ^ 1) for i in range(16)])]
  transfers between devices with their start and end apart: 22 -> 25, of which waited for: 16 -> 12; matrix products, arithmetic and copies ran while one was open for 8% -> 7% of each run, Pallas kernels for 0% -> 19%
where the time goes in v1:
time: 253 us; the launch traced here: 251 us
  starting transfers between devices  68.4 us (27%)
  waiting for transfers between devices  66.5 us (26%)
  Pallas kernels  50.2 us (20%)
  local copies, waits for them, and re-layouts  33.2 us (13%)
  between operations  17.7 us (7%)
  other arithmetic  14.5 us (6%)
    unnamed x94, local copies, waits for them, and re-layouts  29 us
    all_to_all x4, starting transfers between devices, gathered(): lax.all_to_all(copies, 'tensor', 0, 0, axis_index_groups=GROUPS, tiled=True)  21.1 us
    ppermute x4, waiting for transfers between devices, to_partner(): return lax.ppermute(value, 'section', [(i, i ^ 8) for i in range(16)])  19.6 us
    all_to_all x4, waiting for transfers between devices, scattered(): lax.all_to_all(pair, 'tensor', 0, 0, axis_index_groups=GROUPS, tiled=True)  16.6 us
    pallas_call x2, Pallas kernels, run_backward(): pl.pallas_call(backward_kernel, grid=(2 * STEPS,), out_shape=jax.ShapeDty...  15.8 us
    all_to_all x4, starting transfers between devices, scattered(): lax.all_to_all(pair, 'tensor', 0, 0, axis_index_groups=GROUPS, tiled=True)  15.6 us
    pallas_call x10, Pallas kernels, plain(): pl.pallas_call(kernel, out_shape=[jax.ShapeDtypeStruct(*out) for out in o...  15.1 us
    all_to_all x4, waiting for transfers between devices, gathered(): lax.all_to_all(copies, 'tensor', 0, 0, axis_index_groups=GROUPS, tiled=True)  15 us
  transfers between devices with their start and end apart: 25, of which 12 were waited for; matrix products, arithmetic and copies ran while one was open for 7% of the time, Pallas kernels for 19%

profile of v1, /device:TPU:1, one launch (start us, length us, event | category | flops | bytes accessed | tf_op | source)
XLA Modules:
  0.0 250.6 jit_solution(3729377187010173984)
XLA Ops:
  11.2 6.3 %all-to-all-start = ((bf16[8,8,5120]{2,1,0:T(8,128)(2,1)}), bf16[8,8,5120]{2,1,0:T(8,128)(2,1)S(1)}, u32[]{:S(2)}, u32[]{:S(2)}) async-start(bf16[8,8,5120]{2,1,0:T(8,128)(2,1)} %get-tuple-element.11), calls=%async_computation | async-start | bytes 1310720 | tf_op jit(solution)/shard_map/all_to_all | solution.py:332
  22.2 2.9 %collective-permute-start.7 = (bf16[4,8,5120]{2,1,0:T(8,128)(2,1)S(1)}, bf16[4,8,5120]{2,1,0:T(8,128)(2,1)S(1)}, u32[]{:S(2)}, u32[]{:S(2)}) collective-permute-start(bf16[4,8,5120]{2,1,0:T(8,128)(2,1)S(1)} %get-tuple-element.23), channel_id=1, source_target_pairs={{0,128},{16,144},{32,160},{48,176},{64,192},{80,208},{96,224},{112... | collective-permute-start | bytes 983048 | tf_op jit(solution)/shard_map/ppermute | solution.py:29
  26.4 5.6 %collective-permute-done.7.streams = bf16[4,8,5120]{2,1,0:T(8,128)(2,1)S(1)} collective-permute-done((bf16[4,8,5120]{2,1,0:T(8,128)(2,1)S(1)}, bf16[4,8,5120]{2,1,0:T(8,128)(2,1)S(1)}, u32[]{:S(2)}, u32[]{:S(2)}) %collective-permute-start.7) | collective-permute-done | bytes 327712 | tf_op jit(solution)/shard_map/ppermute | solution.py:29
  34.9 4.8 %all-to-all-start.4 = ((bf16[8,8,5120]{2,1,0:T(8,128)(2,1)}), bf16[8,8,5120]{2,1,0:T(8,128)(2,1)}, u32[]{:S(2)}, u32[]{:S(2)}) async-start(bf16[8,8,5120]{2,1,0:T(8,128)(2,1)} %shard_map.253), calls=%async_computation.4 | async-start | bytes 1310720 | tf_op jit(solution)/shard_map/all_to_all | solution.py:332
  40.4 2.5 %collective-permute-start = (bf16[64,5120]{1,0:T(8,128)(2,1)S(1)}, bf16[64,5120]{1,0:T(8,128)(2,1)}, u32[]{:S(2)}, u32[]{:S(2)}) collective-permute-start(bf16[64,5120]{1,0:T(8,128)(2,1)S(1)} %bitcast.56), channel_id=1, source_target_pairs={{0,1},{1,0},{2,3},{3,2},{4,5},{5,4},{6,7},{7,6},{8,9},{9,8},{10,11... | collective-permute-start | bytes 1966088 | tf_op jit(solution)/shard_map/ppermute | solution.py:25
  43.0 4.5 %all-to-all-done.4 = bf16[8,8,5120]{2,1,0:T(8,128)(2,1)} async-done(((bf16[8,8,5120]{2,1,0:T(8,128)(2,1)}), bf16[8,8,5120]{2,1,0:T(8,128)(2,1)}, u32[]{:S(2)}, u32[]{:S(2)}) %all-to-all-start.4) | async-done | bytes 655392 | tf_op jit(solution)/shard_map/all_to_all | solution.py:332
  47.5 4.2 %collective-permute-start.6 = (bf16[64,5120]{1,0:T(8,128)(2,1)}, bf16[64,5120]{1,0:T(8,128)(2,1)}, u32[]{:S(2)}, u32[]{:S(2)}) collective-permute-start(bf16[64,5120]{1,0:T(8,128)(2,1)} %bitcast.18.own), channel_id=1, source_target_pairs={{0,1},{1,0},{2,3},{3,2},{4,5},{5,4},{6,7},{7,6},{8,9},{9,8},{10,11... | collective-permute-start | bytes 1966088 | tf_op jit(solution)/shard_map/ppermute | solution.py:25
  51.7 3.1 %maximum_select_fusion = bf16[2,128,5120]{2,1,0:T(8,128)(2,1)S(1)} fusion(bf16[2,64,5120]{2,1,0:T(8,128)(2,1)} %collective-permute-done.1, bf16[2,64,5120]{2,1,0:T(8,128)(2,1)} %bitcast.77, pred[]{:T(512)S(6)} %eq.17), kind=kLoop, calls=%fused_computation | loop fusion | flops 11796480 | bytes 5242881 | tf_op jit(solution)/shard_map/jit(_where)/select_n | solution.py:378
  57.6 6.9 %shard_map.248 = bf16[128,5120]{1,0:T(8,128)(2,1)S(1)} custom-call(bf16[64,5120]{1,0:T(8,128)(2,1)S(1)} %bitcast.57, bf16[64,5120]{1,0:T(8,128)(2,1)} %collective-permute-done.other, bf16[5120,384]{1,0:T(8,128)(2,1)S(1)} %bitcast.40, bf16[256,5120]{1,0:T(8,128)(2,1)S(1)} %bitcast.46, bf16[384,5120]{1,0:T(8,128)(2,1)S(1)} %bitcast.52, f32[2,128]{1,0:T(2,128)S(1)} %bitcast.69, ...), custom_call_target="tpu_custom_call" | custom-call | flops 1500000000 | bytes 14000000 | tf_op jit(solution)/shard_map/pallas_call | solution.py:214
  66.3 6.6 %all-gather.3.cloned.1.call-done.rows = bf16[128,5120]{1,0:T(8,128)(2,1)} async-done(((bf16[8,5120]{1,0:T(8,128)(2,1)}), bf16[128,5120]{1,0:T(8,128)(2,1)}) %all-gather.3.cloned.1.call-update) | async-done | bytes 1310736 | tf_op jit(solution)/shard_map/all_gather | solution.py:425
  76.3 2.7 %shard_map.255.projected = bf16[128,640]{1,0:T(8,128)(2,1)S(1)} custom-call(bf16[128,5120]{1,0:T(8,128)(2,1)S(1)} %copy-done.24, bf16[5120,384]{1,0:T(8,128)(2,1)S(1)} %bitcast.41, bf16[256,5120]{1,0:T(8,128)(2,1)S(1)} %bitcast.47, bf16[128,128]{1,0:T(8,128)(2,1)S(1)} %broadcast_select_fusion.turn), custom_call_target="tpu_custom_call" | custom-call | flops 900000000 | bytes 8000000 | tf_op jit(solution)/shard_map/pallas_call | solution.py:237
  79.0 7.9 %shard_map.256 = bf16[128,5120]{1,0:T(8,128)(2,1)S(1)} custom-call(bf16[64,5120]{1,0:T(8,128)(2,1)} %bitcast.18.own, bf16[64,5120]{1,0:T(8,128)(2,1)} %collective-permute-done.6.other, bf16[128,640]{1,0:T(8,128)(2,1)S(1)} %shard_map.255.projected, bf16[5120,384]{1,0:T(8,128)(2,1)S(1)} %bitcast.42, bf16[256,5120]{1,0:T(8,128)(2,1)S(1)} %bitcast.48, ...), custom_call_target="tpu_custom_call" | custom-call | flops 1500000000 | bytes 14000000 | tf_op jit(solution)/shard_map/pallas_call | solution.py:255
  91.6 3.6 %all-to-all-start.1 = ((bf16[8,8,5120]{2,1,0:T(8,128)(2,1)}), bf16[8,8,5120]{2,1,0:T(8,128)(2,1)S(1)}, u32[]{:S(2)}, u32[]{:S(2)}) async-start(bf16[8,8,5120]{2,1,0:T(8,128)(2,1)} %fusion), calls=%async_computation.1 | async-start | bytes 1310720 | tf_op jit(solution)/shard_map/all_to_all | solution.py:341
  97.6 7.9 %all-to-all-done.1.landed = bf16[8,8,5120]{2,1,0:T(8,128)(2,1)S(1)} async-done(((bf16[8,8,5120]{2,1,0:T(8,128)(2,1)}), bf16[8,8,5120]{2,1,0:T(8,128)(2,1)S(1)}, u32[]{:S(2)}, u32[]{:S(2)}) %all-to-all-start.1) | async-done | bytes 655392 | tf_op jit(solution)/shard_map/all_to_all | solution.py:341
  106.3 4.2 %all-to-all-start.5 = ((bf16[8,8,5120]{2,1,0:T(8,128)(2,1)}), bf16[8,8,5120]{2,1,0:T(8,128)(2,1)S(1)}, u32[]{:S(2)}, u32[]{:S(2)}) async-start(bf16[8,8,5120]{2,1,0:T(8,128)(2,1)} %fusion.2), calls=%async_computation.5 | async-start | bytes 1310720 | tf_op jit(solution)/shard_map/all_to_all | solution.py:341
  116.5 2.8 %collective-permute-start.11 = (bf16[4,8,5120]{2,1,0:T(8,128)(2,1)}, bf16[4,8,5120]{2,1,0:T(8,128)(2,1)}, u32[]{:S(2)}, u32[]{:S(2)}) collective-permute-start(bf16[4,8,5120]{2,1,0:T(8,128)(2,1)} %get-tuple-element.22), channel_id=1, source_target_pairs={{0,128},{16,144},{32,160},{48,176},{64,192},{80,208},{96,224},{112... | collective-permute-start | bytes 983048 | tf_op jit(solution)/shard_map/ppermute | solution.py:29
  123.8 6.1 %collective-permute-start.9 = (bf16[4,8,5120]{2,1,0:T(8,128)(2,1)}, bf16[4,8,5120]{2,1,0:T(8,128)(2,1)}, u32[]{:S(2)}, u32[]{:S(2)}) collective-permute-start(bf16[4,8,5120]{2,1,0:T(8,128)(2,1)} %shard_map.257), channel_id=1, source_target_pairs={{0,240},{16,0},{32,16},{48,32},{64,48},{80,64},{96,80},{112,96},{1... | collective-permute-start | bytes 983048 | tf_op jit(solution)/shard_map/ppermute | solution.py:33
  129.9 8.3 %collective-permute-done.3 = bf16[4,8,5120]{2,1,0:T(8,128)(2,1)} collective-permute-done((bf16[4,8,5120]{2,1,0:T(8,128)(2,1)}, bf16[4,8,5120]{2,1,0:T(8,128)(2,1)}, u32[]{:S(2)}, u32[]{:S(2)}) %collective-permute-start.3) | collective-permute-done | bytes 327712 | tf_op jit(solution)/shard_map/ppermute | solution.py:33
  140.4 4.2 %all-to-all-start.2 = ((bf16[8,8,5120]{2,1,0:T(8,128)(2,1)}), bf16[8,8,5120]{2,1,0:T(8,128)(2,1)}, u32[]{:S(2)}, u32[]{:S(2)}) async-start(bf16[8,8,5120]{2,1,0:T(8,128)(2,1)} %copy-done.28), calls=%async_computation.2 | async-start | bytes 1310720 | tf_op jit(solution)/shard_map/all_to_all | solution.py:332
  149.8 2.9 %all-to-all-done.2 = bf16[8,8,5120]{2,1,0:T(8,128)(2,1)} async-done(((bf16[8,8,5120]{2,1,0:T(8,128)(2,1)}), bf16[8,8,5120]{2,1,0:T(8,128)(2,1)}, u32[]{:S(2)}, u32[]{:S(2)}) %all-to-all-start.2) | async-done | bytes 655392 | tf_op jit(solution)/shard_map/all_to_all | solution.py:332
  152.7 5.8 %all-to-all-start.6 = ((bf16[8,8,5120]{2,1,0:T(8,128)(2,1)}), bf16[8,8,5120]{2,1,0:T(8,128)(2,1)}, u32[]{:S(2)}, u32[]{:S(2)}) async-start(bf16[8,8,5120]{2,1,0:T(8,128)(2,1)} %copy-done.18), calls=%async_computation.6 | async-start | bytes 1310720 | tf_op jit(solution)/shard_map/all_to_all | solution.py:332
  160.8 7.5 %all-to-all-done.6 = bf16[8,8,5120]{2,1,0:T(8,128)(2,1)} async-done(((bf16[8,8,5120]{2,1,0:T(8,128)(2,1)}), bf16[8,8,5120]{2,1,0:T(8,128)(2,1)}, u32[]{:S(2)}, u32[]{:S(2)}) %all-to-all-start.6) | async-done | bytes 655392 | tf_op jit(solution)/shard_map/all_to_all | solution.py:332
  168.2 3.7 %collective-permute-start.10 = (bf16[64,5120]{1,0:T(8,128)(2,1)}, bf16[64,5120]{1,0:T(8,128)(2,1)}, u32[]{:S(2)}, u32[]{:S(2)}) collective-permute-start(bf16[64,5120]{1,0:T(8,128)(2,1)} %bitcast.22.own), channel_id=1, source_target_pairs={{0,1},{1,0},{2,3},{3,2},{4,5},{5,4},{6,7},{7,6},{8,9},{9,8},{10,11... | collective-permute-start | bytes 1966088 | tf_op jit(solution)/shard_map/ppermute | solution.py:25
  176.3 7.1 %shard_map.251 = bf16[128,5120]{1,0:T(8,128)(2,1)S(1)} custom-call(bf16[64,5120]{1,0:T(8,128)(2,1)} %bitcast.13.own, bf16[64,5120]{1,0:T(8,128)(2,1)} %collective-permute-done.4.other, bf16[5120,384]{1,0:T(8,128)(2,1)S(1)} %bitcast.43, bf16[256,5120]{1,0:T(8,128)(2,1)S(1)} %bitcast.49, bf16[384,5120]{1,0:T(8,128)(2,1)S(1)} %bitcast.54, ...), custom_call_target="tpu_custom_call" | custom-call | flops 1500000000 | bytes 14000000 | tf_op jit(solution)/shard_map/pallas_call | solution.py:214
  189.2 2.7 %shard_map.260.projected = bf16[128,640]{1,0:T(8,128)(2,1)S(1)} custom-call(bf16[128,5120]{1,0:T(8,128)(2,1)S(1)} %copy-done.25, bf16[5120,384]{1,0:T(8,128)(2,1)S(1)} %bitcast.44, bf16[256,5120]{1,0:T(8,128)(2,1)S(1)} %bitcast.50, bf16[128,128]{1,0:T(8,128)(2,1)S(1)} %broadcast_select_fusion.turn), custom_call_target="tpu_custom_call" | custom-call | flops 900000000 | bytes 8000000 | tf_op jit(solution)/shard_map/pallas_call | solution.py:237
  191.9 7.9 %shard_map.261 = bf16[128,5120]{1,0:T(8,128)(2,1)S(1)} custom-call(bf16[64,5120]{1,0:T(8,128)(2,1)} %bitcast.22.own, bf16[64,5120]{1,0:T(8,128)(2,1)} %collective-permute-done.10.other, bf16[128,640]{1,0:T(8,128)(2,1)S(1)} %shard_map.260.projected, bf16[5120,384]{1,0:T(8,128)(2,1)S(1)} %bitcast.45, bf16[256,5120]{1,0:T(8,128)(2,1)S(1)} %bitcast.51, ...), custom_call_target="tpu_custom_call" | custom-call | flops 1500000000 | bytes 14000000 | tf_op jit(solution)/shard_map/pallas_call | solution.py:255
  204.5 3.5 %all-to-all-start.3 = ((bf16[8,8,5120]{2,1,0:T(8,128)(2,1)}), bf16[8,8,5120]{2,1,0:T(8,128)(2,1)S(1)}, u32[]{:S(2)}, u32[]{:S(2)}) async-start(bf16[8,8,5120]{2,1,0:T(8,128)(2,1)} %fusion.1), calls=%async_computation.3 | async-start | bytes 1310720 | tf_op jit(solution)/shard_map/all_to_all | solution.py:341
  210.3 7.9 %all-to-all-done.3.landed = bf16[8,8,5120]{2,1,0:T(8,128)(2,1)S(1)} async-done(((bf16[8,8,5120]{2,1,0:T(8,128)(2,1)}), bf16[8,8,5120]{2,1,0:T(8,128)(2,1)S(1)}, u32[]{:S(2)}, u32[]{:S(2)}) %all-to-all-start.3) | async-done | bytes 655392 | tf_op jit(solution)/shard_map/all_to_all | solution.py:341
  218.2 4.2 %all-to-all-start.7 = ((bf16[8,8,5120]{2,1,0:T(8,128)(2,1)}), bf16[8,8,5120]{2,1,0:T(8,128)(2,1)S(1)}, u32[]{:S(2)}, u32[]{:S(2)}) async-start(bf16[8,8,5120]{2,1,0:T(8,128)(2,1)} %fusion.3), calls=%async_computation.7 | async-start | bytes 1310720 | tf_op jit(solution)/shard_map/all_to_all | solution.py:341
  222.4 2.6 %collective-permute-start.13 = (bf16[4,8,5120]{2,1,0:T(8,128)(2,1)S(1)}, bf16[4,8,5120]{2,1,0:T(8,128)(2,1)S(1)}, u32[]{:S(2)}, u32[]{:S(2)}) collective-permute-start(bf16[4,8,5120]{2,1,0:T(8,128)(2,1)S(1)} %bitcast.62), channel_id=1, source_target_pairs={{0,128},{16,144},{32,160},{48,176},{64,192},{80,208},{96,224},{112... | collective-permute-start | bytes 983048 | tf_op jit(solution)/shard_map/ppermute | solution.py:29
  225.4 7.0 %collective-permute-done.13 = bf16[4,8,5120]{2,1,0:T(8,128)(2,1)S(1)} collective-permute-done((bf16[4,8,5120]{2,1,0:T(8,128)(2,1)S(1)}, bf16[4,8,5120]{2,1,0:T(8,128)(2,1)S(1)}, u32[]{:S(2)}, u32[]{:S(2)}) %collective-permute-start.13) | collective-permute-done | bytes 327712 | tf_op jit(solution)/shard_map/ppermute | solution.py:29
  232.4 7.0 %collective-permute-done.14 = bf16[4,8,5120]{2,1,0:T(8,128)(2,1)S(1)} collective-permute-done((bf16[4,8,5120]{2,1,0:T(8,128)(2,1)S(1)}, bf16[4,8,5120]{2,1,0:T(8,128)(2,1)S(1)}, u32[]{:S(2)}, u32[]{:S(2)}) %collective-permute-start.14) | collective-permute-done | bytes 327712 | tf_op jit(solution)/shard_map/ppermute | solution.py:29
  (150 shorter events, 68.1 us)
Async XLA Ops:
  11.2 20.8 %copy-start.27 = (f32[1,5120]{1,0:T(1,128)S(1)}, f32[1,5120]{1,0:T(1,128)}, u32[]{:S(2)}) copy-start(f32[1,5120]{1,0:T(1,128)} %gain.11) | copy-start | bytes 61444
  11.2 20.8 %copy-start.34 = (f32[1,4]{1,0:T(1,128)S(1)}, f32[1,4]{1,0:T(1,128)}, u32[]{:S(2)}) copy-start(f32[1,4]{1,0:T(1,128)} %param.35) | copy-start | bytes 52
  11.2 22.3 %copy-start.19 = (bf16[1,4,8,5120]{3,2,1,0:T(8,128)(2,1)S(1)}, bf16[1,4,8,5120]{3,2,1,0:T(8,128)(2,1)}, u32[]{:S(2)}) copy-start(bf16[1,4,8,5120]{3,2,1,0:T(8,128)(2,1)} %param.25) | copy-start | bytes 983044
  11.2 22.3 %copy-start.36 = (f32[1,4]{1,0:T(1,128)S(1)}, f32[1,4]{1,0:T(1,128)}, u32[]{:S(2)}) copy-start(f32[1,4]{1,0:T(1,128)} %param.36) | copy-start | bytes 52
  11.2 23.7 %all-to-all-start = ((bf16[8,8,5120]{2,1,0:T(8,128)(2,1)}), bf16[8,8,5120]{2,1,0:T(8,128)(2,1)S(1)}, u32[]{:S(2)}, u32[]{:S(2)}) async-start(bf16[8,8,5120]{2,1,0:T(8,128)(2,1)} %get-tuple-element.11), calls=%async_computation | async-start | bytes 1310720 | tf_op jit(solution)/shard_map/all_to_all | solution.py:332
  17.6 55.3 %all-gather.3.cloned.1.call-start = ((), (), s32[]{:S(2)}) async-start(), calls=%async_computation.8 | async-start | bytes 1392640 | tf_op jit(solution)/shard_map/all_gather | solution.py:425
  22.2 9.8 %collective-permute-start.7 = (bf16[4,8,5120]{2,1,0:T(8,128)(2,1)S(1)}, bf16[4,8,5120]{2,1,0:T(8,128)(2,1)S(1)}, u32[]{:S(2)}, u32[]{:S(2)}) collective-permute-start(bf16[4,8,5120]{2,1,0:T(8,128)(2,1)S(1)} %get-tuple-element.23), channel_id=1, source_target_pairs={{0,128},{16,144},{32,160},{48,176},{64,192},{80,208},{96,224},{112... | collective-permute-start | bytes 983048 | tf_op jit(solution)/shard_map/ppermute | solution.py:29
  25.2 14.6 %copy-start.41 = (f32[128,128]{1,0:T(8,128)S(1)}, f32[128,128]{1,0:T(8,128)}, u32[]{:S(2)}) copy-start(f32[128,128]{1,0:T(8,128)} %constant.86) | copy-start | bytes 196612
  25.2 26.5 %collective-permute-start.1 = (bf16[2,64,5120]{2,1,0:T(8,128)(2,1)S(1)}, bf16[2,64,5120]{2,1,0:T(8,128)(2,1)}, u32[]{:S(2)}, u32[]{:S(2)}) collective-permute-start(bf16[2,64,5120]{2,1,0:T(8,128)(2,1)S(1)} %bitcast.78), channel_id=1, source_target_pairs={{0,1},{1,0},{2,3},{3,2},{4,5},{5,4},{6,7},{7,6},{8,9},{9,8},{10,11... | collective-permute-start | bytes 3932168 | tf_op jit(solution)/shard_map/ppermute | solution.py:25
  34.9 12.6 %all-to-all-start.4 = ((bf16[8,8,5120]{2,1,0:T(8,128)(2,1)}), bf16[8,8,5120]{2,1,0:T(8,128)(2,1)}, u32[]{:S(2)}, u32[]{:S(2)}) async-start(bf16[8,8,5120]{2,1,0:T(8,128)(2,1)} %shard_map.253), calls=%async_computation.4 | async-start | bytes 1310720 | tf_op jit(solution)/shard_map/all_to_all | solution.py:332
  40.4 14.4 %collective-permute-start = (bf16[64,5120]{1,0:T(8,128)(2,1)S(1)}, bf16[64,5120]{1,0:T(8,128)(2,1)}, u32[]{:S(2)}, u32[]{:S(2)}) collective-permute-start(bf16[64,5120]{1,0:T(8,128)(2,1)S(1)} %bitcast.56), channel_id=1, source_target_pairs={{0,1},{1,0},{2,3},{3,2},{4,5},{5,4},{6,7},{7,6},{8,9},{9,8},{10,11... | collective-permute-start | bytes 1966088 | tf_op jit(solution)/shard_map/ppermute | solution.py:25
  47.5 31.4 %collective-permute-start.6 = (bf16[64,5120]{1,0:T(8,128)(2,1)}, bf16[64,5120]{1,0:T(8,128)(2,1)}, u32[]{:S(2)}, u32[]{:S(2)}) collective-permute-start(bf16[64,5120]{1,0:T(8,128)(2,1)} %bitcast.18.own), channel_id=1, source_target_pairs={{0,1},{1,0},{2,3},{3,2},{4,5},{5,4},{6,7},{7,6},{8,9},{9,8},{10,11... | collective-permute-start | bytes 1966088 | tf_op jit(solution)/shard_map/ppermute | solution.py:25
  65.6 23.6 %collective-permute-start.2 = (bf16[64,5120]{1,0:T(8,128)(2,1)S(1)}, bf16[64,5120]{1,0:T(8,128)(2,1)}, u32[]{:S(2)}, u32[]{:S(2)}) collective-permute-start(bf16[64,5120]{1,0:T(8,128)(2,1)S(1)} %slice.33), channel_id=1, source_target_pairs={{0,1},{1,0},{2,3},{3,2},{4,5},{5,4},{6,7},{7,6},{8,9},{9,8},{10,11... | collective-permute-start | bytes 1966088 | tf_op jit(solution)/shard_map/ppermute | solution.py:25
  88.9 6.4 %collective-permute-start.8 = (bf16[64,5120]{1,0:T(8,128)(2,1)}, bf16[64,5120]{1,0:T(8,128)(2,1)}, u32[]{:S(2)}, u32[]{:S(2)}) collective-permute-start(bf16[64,5120]{1,0:T(8,128)(2,1)} %slice.37), channel_id=1, source_target_pairs={{0,1},{1,0},{2,3},{3,2},{4,5},{5,4},{6,7},{7,6},{8,9},{9,8},{10,11... | collective-permute-start | bytes 1966088 | tf_op jit(solution)/shard_map/ppermute | solution.py:25
  91.6 13.8 %all-to-all-start.1 = ((bf16[8,8,5120]{2,1,0:T(8,128)(2,1)}), bf16[8,8,5120]{2,1,0:T(8,128)(2,1)S(1)}, u32[]{:S(2)}, u32[]{:S(2)}) async-start(bf16[8,8,5120]{2,1,0:T(8,128)(2,1)} %fusion), calls=%async_computation.1 | async-start | bytes 1310720 | tf_op jit(solution)/shard_map/all_to_all | solution.py:341
  95.3 15.2 %copy-start.44 = (f32[1,4,4]{2,1,0:T(4,128)S(1)}, f32[1,4,4]{2,1,0:T(4,128)}, u32[]{:S(2)}) copy-start(f32[1,4,4]{2,1,0:T(4,128)} %param.37) | copy-start | bytes 196
  106.3 13.8 %all-to-all-start.5 = ((bf16[8,8,5120]{2,1,0:T(8,128)(2,1)}), bf16[8,8,5120]{2,1,0:T(8,128)(2,1)S(1)}, u32[]{:S(2)}, u32[]{:S(2)}) async-start(bf16[8,8,5120]{2,1,0:T(8,128)(2,1)} %fusion.2), calls=%async_computation.5 | async-start | bytes 1310720 | tf_op jit(solution)/shard_map/all_to_all | solution.py:341
  114.3 23.9 %collective-permute-start.3 = (bf16[4,8,5120]{2,1,0:T(8,128)(2,1)}, bf16[4,8,5120]{2,1,0:T(8,128)(2,1)}, u32[]{:S(2)}, u32[]{:S(2)}) collective-permute-start(bf16[4,8,5120]{2,1,0:T(8,128)(2,1)} %shard_map.249), channel_id=1, source_target_pairs={{0,16},{16,32},{32,48},{48,64},{64,80},{80,96},{96,112},{112,128},... | collective-permute-start | bytes 983048 | tf_op jit(solution)/shard_map/ppermute | solution.py:33
  116.5 28.1 %collective-permute-start.11 = (bf16[4,8,5120]{2,1,0:T(8,128)(2,1)}, bf16[4,8,5120]{2,1,0:T(8,128)(2,1)}, u32[]{:S(2)}, u32[]{:S(2)}) collective-permute-start(bf16[4,8,5120]{2,1,0:T(8,128)(2,1)} %get-tuple-element.22), channel_id=1, source_target_pairs={{0,128},{16,144},{32,160},{48,176},{64,192},{80,208},{96,224},{112... | collective-permute-start | bytes 983048 | tf_op jit(solution)/shard_map/ppermute | solution.py:29
  122.0 16.2 %copy-start.39 = (bf16[1,4,8,5120]{3,2,1,0:T(8,128)(2,1)S(1)}, bf16[1,4,8,5120]{3,2,1,0:T(8,128)(2,1)}, u32[]{:S(2)}) copy-start(bf16[1,4,8,5120]{3,2,1,0:T(8,128)(2,1)} %param.26) | copy-start | bytes 983044
  123.8 23.4 %collective-permute-start.9 = (bf16[4,8,5120]{2,1,0:T(8,128)(2,1)}, bf16[4,8,5120]{2,1,0:T(8,128)(2,1)}, u32[]{:S(2)}, u32[]{:S(2)}) collective-permute-start(bf16[4,8,5120]{2,1,0:T(8,128)(2,1)} %shard_map.257), channel_id=1, source_target_pairs={{0,240},{16,0},{32,16},{48,32},{64,48},{80,64},{96,80},{112,96},{1... | collective-permute-start | bytes 983048 | tf_op jit(solution)/shard_map/ppermute | solution.py:33
  140.4 12.3 %all-to-all-start.2 = ((bf16[8,8,5120]{2,1,0:T(8,128)(2,1)}), bf16[8,8,5120]{2,1,0:T(8,128)(2,1)}, u32[]{:S(2)}, u32[]{:S(2)}) async-start(bf16[8,8,5120]{2,1,0:T(8,128)(2,1)} %copy-done.28), calls=%async_computation.2 | async-start | bytes 1310720 | tf_op jit(solution)/shard_map/all_to_all | solution.py:332
  144.6 41.2 %all-gather.5.cloned.1.call-start = ((), (), s32[]{:S(2)}) async-start(), calls=%async_computation.9 | async-start | bytes 1392640 | tf_op jit(solution)/shard_map/all_gather | solution.py:425
  152.7 15.5 %all-to-all-start.6 = ((bf16[8,8,5120]{2,1,0:T(8,128)(2,1)}), bf16[8,8,5120]{2,1,0:T(8,128)(2,1)}, u32[]{:S(2)}, u32[]{:S(2)}) async-start(bf16[8,8,5120]{2,1,0:T(8,128)(2,1)} %copy-done.18), calls=%async_computation.6 | async-start | bytes 1310720 | tf_op jit(solution)/shard_map/all_to_all | solution.py:332
  158.5 13.4 %collective-permute-start.4 = (bf16[64,5120]{1,0:T(8,128)(2,1)}, bf16[64,5120]{1,0:T(8,128)(2,1)}, u32[]{:S(2)}, u32[]{:S(2)}) collective-permute-start(bf16[64,5120]{1,0:T(8,128)(2,1)} %bitcast.13.own), channel_id=1, source_target_pairs={{0,1},{1,0},{2,3},{3,2},{4,5},{5,4},{6,7},{7,6},{8,9},{9,8},{10,11... | collective-permute-start | bytes 1966088 | tf_op jit(solution)/shard_map/ppermute | solution.py:25
  168.2 23.6 %collective-permute-start.10 = (bf16[64,5120]{1,0:T(8,128)(2,1)}, bf16[64,5120]{1,0:T(8,128)(2,1)}, u32[]{:S(2)}, u32[]{:S(2)}) collective-permute-start(bf16[64,5120]{1,0:T(8,128)(2,1)} %bitcast.22.own), channel_id=1, source_target_pairs={{0,1},{1,0},{2,3},{3,2},{4,5},{5,4},{6,7},{7,6},{8,9},{9,8},{10,11... | collective-permute-start | bytes 1966088 | tf_op jit(solution)/shard_map/ppermute | solution.py:25
  185.3 16.8 %collective-permute-start.5 = (bf16[64,5120]{1,0:T(8,128)(2,1)}, bf16[64,5120]{1,0:T(8,128)(2,1)}, u32[]{:S(2)}, u32[]{:S(2)}) collective-permute-start(bf16[64,5120]{1,0:T(8,128)(2,1)} %slice.35), channel_id=1, source_target_pairs={{0,1},{1,0},{2,3},{3,2},{4,5},{5,4},{6,7},{7,6},{8,9},{9,8},{10,11... | collective-permute-start | bytes 1966088 | tf_op jit(solution)/shard_map/ppermute | solution.py:25
  201.8 6.3 %collective-permute-start.12 = (bf16[64,5120]{1,0:T(8,128)(2,1)}, bf16[64,5120]{1,0:T(8,128)(2,1)}, u32[]{:S(2)}, u32[]{:S(2)}) collective-permute-start(bf16[64,5120]{1,0:T(8,128)(2,1)} %slice.39), channel_id=1, source_target_pairs={{0,1},{1,0},{2,3},{3,2},{4,5},{5,4},{6,7},{7,6},{8,9},{9,8},{10,11... | collective-permute-start | bytes 1966088 | tf_op jit(solution)/shard_map/ppermute | solution.py:25
  204.5 13.7 %all-to-all-start.3 = ((bf16[8,8,5120]{2,1,0:T(8,128)(2,1)}), bf16[8,8,5120]{2,1,0:T(8,128)(2,1)S(1)}, u32[]{:S(2)}, u32[]{:S(2)}) async-start(bf16[8,8,5120]{2,1,0:T(8,128)(2,1)} %fusion.1), calls=%async_computation.3 | async-start | bytes 1310720 | tf_op jit(solution)/shard_map/all_to_all | solution.py:341
  218.2 23.7 %all-to-all-start.7 = ((bf16[8,8,5120]{2,1,0:T(8,128)(2,1)}), bf16[8,8,5120]{2,1,0:T(8,128)(2,1)S(1)}, u32[]{:S(2)}, u32[]{:S(2)}) async-start(bf16[8,8,5120]{2,1,0:T(8,128)(2,1)} %fusion.3), calls=%async_computation.7 | async-start | bytes 1310720 | tf_op jit(solution)/shard_map/all_to_all | solution.py:341
  222.4 10.0 %collective-permute-start.13 = (bf16[4,8,5120]{2,1,0:T(8,128)(2,1)S(1)}, bf16[4,8,5120]{2,1,0:T(8,128)(2,1)S(1)}, u32[]{:S(2)}, u32[]{:S(2)}) collective-permute-start(bf16[4,8,5120]{2,1,0:T(8,128)(2,1)S(1)} %bitcast.62), channel_id=1, source_target_pairs={{0,128},{16,144},{32,160},{48,176},{64,192},{80,208},{96,224},{112... | collective-permute-start | bytes 983048 | tf_op jit(solution)/shard_map/ppermute | solution.py:29
  225.0 14.5 %collective-permute-start.14 = (bf16[4,8,5120]{2,1,0:T(8,128)(2,1)S(1)}, bf16[4,8,5120]{2,1,0:T(8,128)(2,1)S(1)}, u32[]{:S(2)}, u32[]{:S(2)}) collective-permute-start(bf16[4,8,5120]{2,1,0:T(8,128)(2,1)S(1)} %bitcast_select_fusion.1.streams), channel_id=1, source_target_pairs={{0,128},{16,144},{32,160},{48,176},{64,192},{80,208},{96,224},{112... | collective-permute-start | bytes 983048 | tf_op jit(solution)/shard_map/ppermute | solution.py:29
  (40 other events, 141.2 us)
Sparse Core Ops, SparseCore 0:
  33.6 39.2 all-gather.2
  147.9 37.8 all-gather.4

commit v2 on v1

v2 whole, which is shorter than its diff:
```python
import functools
import math

import jax
import jax.numpy as jnp
import numpy as np
from jax import lax
from jax.experimental import pallas as pl
from jax.experimental.pallas import tpu as pltpu
from jax.sharding import PartitionSpec as P

EPSILON = 1e-06
ROPE_BASE = 1000000.0
ROWS = 128
LOCAL = 8
HEAD = 128
WIDTH = 5120
CHUNK = 2560
STEPS = WIDTH // CHUNK
QUERY = 384
BOTH = 256
GROUPS = [[core + 2 * chip for chip in range(8)] for core in range(2)]


def other_core(value):
    return lax.ppermute(value, "tensor", [(i, i ^ 1) for i in range(16)])


def to_partner(value):
    return lax.ppermute(value, "section", [(i, i ^ 8) for i in range(16)])


def shifted(value, by):
    return lax.ppermute(value, "section", [(i, (i + by) % 16) for i in range(16)])


def token_order(parity):
    own = [2 * chip + parity for chip in range(8)]
    other = [2 * chip + 1 - parity for chip in range(8)]
    return np.concatenate([np.arange(LOCAL) + LOCAL * block for block in own + other])


def tables_of(order):
    half = HEAD // 2
    frequency = np.float32(ROPE_BASE) ** (-np.arange(half, dtype=np.float32) / np.float32(half))
    angles = order.astype(np.float32)[:, None] * frequency[None, :]
    cosine, sine = np.cos(angles), np.sin(angles)
    mask = np.where(order[:, None] >= order[None, :], 0.0, -1e30)
    turn = order[:, None] == np.arange(ROWS)[None, :]
    planes = [np.concatenate([cosine, cosine], 1), np.concatenate([-sine, sine], 1), mask, turn]
    return np.stack(planes).astype(np.float32)


TABLES = np.stack([tables_of(token_order(0)), tables_of(token_order(1))])


def dot(left, right):
    return jnp.dot(left, right, preferred_element_type=jnp.float32)


def dot_nt(left, right):
    return lax.dot_general(left, right, (((1,), (1,)), ((), ())), preferred_element_type=jnp.float32)


def dot_tn(left, right):
    return lax.dot_general(left, right, (((0,), (0,)), ((), ())), preferred_element_type=jnp.float32)


def rope(values, cosine, sine):
    return values * cosine + pltpu.roll(values, HEAD // 2, 1) * sine


def rope_back(grads, cosine, sine):
    return grads * cosine - pltpu.roll(grads, HEAD // 2, 1) * sine


def norm_scale(values):
    return lax.rsqrt(jnp.mean(values * values, axis=-1, keepdims=True) + EPSILON)


def head_back(grads, values, scale, gain):
    weighted = grads * gain
    inner = jnp.mean(values * weighted, axis=-1, keepdims=True)
    return scale * weighted - values * (scale * scale * scale * inner)


def softmax_of(query_head, key_head, mask):
    scores = dot_nt(query_head, key_head) * (1.0 / math.sqrt(HEAD)) + mask
    scores = scores - jnp.max(scores, axis=-1, keepdims=True)
    weights = jnp.exp(scores)
    return weights / jnp.sum(weights, axis=-1, keepdims=True)


def joined(own, other, parity):
    first = jnp.where(parity == 0, own, other)
    second = jnp.where(parity == 0, other, own)
    return jnp.concatenate([first, second], axis=1)


def ordered(total, parity):
    own, other = total[:, QUERY : QUERY + HEAD], total[:, QUERY + HEAD :]
    half = HEAD // 2
    keys = joined(own[:, :half], other[:, :half], parity)
    values = joined(own[:, half:], other[:, half:], parity)
    return jnp.concatenate([total[:, :QUERY], keys, values], axis=1).astype(jnp.bfloat16)


def attend(projected, gains, cosine, sine, mask):
    bf16, f32 = jnp.bfloat16, jnp.float32
    keys = projected[:, QUERY : QUERY + HEAD].astype(f32)
    key_head = rope(keys * norm_scale(keys) * gains[1:2], cosine, sine).astype(bf16)
    values = projected[:, QUERY + HEAD :]
    context = []
    for head in range(QUERY // HEAD):
        queries = projected[:, head * HEAD : (head + 1) * HEAD].astype(f32)
        query_head = rope(queries * norm_scale(queries) * gains[0:1], cosine, sine).astype(bf16)
        weights = softmax_of(query_head, key_head, mask)
        context.append(dot(weights.astype(bf16), values).astype(bf16))
    return jnp.concatenate(context, axis=1)


def attend_back(projected, context_grad, gains, cosine, sine, mask, parity):
    bf16, f32 = jnp.bfloat16, jnp.float32
    root = 1.0 / math.sqrt(HEAD)
    keys = projected[:, QUERY : QUERY + HEAD].astype(f32)
    key_scale = norm_scale(keys)
    key_head = rope(keys * key_scale * gains[1:2], cosine, sine).astype(bf16)
    values = projected[:, QUERY + HEAD :]
    query_grads = []
    key_total = jnp.zeros((ROWS, HEAD), f32)
    value_total = jnp.zeros((ROWS, HEAD), f32)
    for head in range(QUERY // HEAD):
        queries = projected[:, head * HEAD : (head + 1) * HEAD].astype(f32)
        query_scale = norm_scale(queries)
        query_head = rope(queries * query_scale * gains[0:1], cosine, sine).astype(bf16)
        weights = softmax_of(query_head, key_head, mask)
        upstream = context_grad[:, head * HEAD : (head + 1) * HEAD].astype(bf16)
        value_total = value_total + dot_tn(weights.astype(bf16), upstream)
        weights_grad = dot_nt(upstream, values).astype(bf16).astype(f32)
        inner = jnp.sum(weights * weights_grad, axis=-1, keepdims=True)
        scores_grad = (weights * (weights_grad - inner) * root).astype(bf16)
        key_total = key_total + dot_tn(scores_grad, query_head)
        turned = rope_back(dot(scores_grad, key_head), cosine, sine)
        query_grads.append(head_back(turned, queries, query_scale, gains[0:1]).astype(bf16))
    key_grad = head_back(rope_back(key_total, cosine, sine), keys, key_scale, gains[1:2])
    half = HEAD // 2
    own = joined(key_grad[:, :half], value_total[:, :half], 0)
    other = joined(key_grad[:, half:], value_total[:, half:], 0)
    first = jnp.where(parity == 0, own, other)
    second = jnp.where(parity == 0, other, own)
    return jnp.concatenate(query_grads, axis=1), first.astype(bf16), second.astype(bf16)


PARAMS = pltpu.CompilerParams(vmem_limit_bytes=62 * 2**20)
SCALAR = pl.BlockSpec(memory_space=pltpu.SMEM)
FAR = pl.BlockSpec(memory_space=pl.ANY)
HALF = ROWS // 2
HALF_ROWS = jax.ShapeDtypeStruct((HALF, WIDTH), jnp.bfloat16)
BF = jnp.bfloat16


def started(copies):
    for copy in copies:
        copy.start()
    return copies


def waited(copies):
    for copy in copies:
        copy.wait()


def columns(chunk):
    return pl.ds(chunk * CHUNK, CHUNK)


def query_loads(queries_w, own_w, other_w, near, sems):
    near_q, near_own, near_other = near
    return [
        [
            pltpu.make_async_copy(
                queries_w.at[columns(c), :], near_q.at[columns(c), :], sems.at[c, 0]
            ),
            pltpu.make_async_copy(own_w.at[:, columns(c)], near_own.at[:, columns(c)], sems.at[c, 1]),
            pltpu.make_async_copy(
                other_w.at[:, columns(c)], near_other.at[:, columns(c)], sems.at[c, 2]
            ),
        ]
        for c in range(STEPS)
    ]


def output_loads(output_w, near, sems):
    return [
        [pltpu.make_async_copy(output_w.at[:, columns(c)], near.at[:, columns(c)], sems.at[c])]
        for c in range(STEPS)
    ]


def row_loads(own, other, rows, sems, part=0):
    if other is None:
        return [pltpu.make_async_copy(own, rows, sems.at[0])]
    source = pl.ds(part * WIDTH, WIDTH)
    return [
        pltpu.make_async_copy(own.at[:, source], rows.at[pl.ds(0, HALF), :], sems.at[0]),
        pltpu.make_async_copy(other.at[:, source], rows.at[pl.ds(HALF, HALF), :], sems.at[1]),
    ]


def stores(near, mine, theirs, c, sems):
    return [
        pltpu.make_async_copy(
            near.at[pl.ds(HALF, HALF), columns(c)], theirs.at[:, columns(c)], sems.at[c, 0]
        ),
        pltpu.make_async_copy(
            near.at[pl.ds(0, HALF), columns(c)], mine.at[:, columns(c)], sems.at[c, 1]
        ),
    ]


def project_chunks(rows, near, loads):
    near_q, near_own, near_other = near
    queries = own = other = 0.0
    for c in range(STEPS):
        waited(loads[c])
        part = rows[:, c * CHUNK : (c + 1) * CHUNK]
        queries += dot(part, near_q[c * CHUNK : (c + 1) * CHUNK, :])
        own += dot_nt(part, near_own[:, c * CHUNK : (c + 1) * CHUNK])
        other += dot_nt(part, near_other[:, c * CHUNK : (c + 1) * CHUNK])
    return jnp.concatenate([queries, own, other], axis=1)


WEIGHT_SCRATCH = [
    pltpu.VMEM((WIDTH, QUERY), BF),
    pltpu.VMEM((HEAD, WIDTH), BF),
    pltpu.VMEM((HEAD, WIDTH), BF),
    pltpu.SemaphoreType.DMA((STEPS, 3)),
]
ROW_SCRATCH = [pltpu.VMEM((ROWS, WIDTH), BF), pltpu.SemaphoreType.DMA((2,))]
SMALL_SCRATCH = [
    pltpu.VMEM((2, HEAD), jnp.float32),
    pltpu.VMEM((4, ROWS, HEAD), jnp.float32),
    pltpu.SemaphoreType.DMA((2,)),
]
OUT_SCRATCH = [pltpu.VMEM((ROWS, WIDTH), BF), pltpu.SemaphoreType.DMA((STEPS, 2))]


def small_loads(gains, tables, near_gains, near_tables, sems):
    return [
        pltpu.make_async_copy(gains, near_gains, sems.at[0]),
        pltpu.make_async_copy(tables, near_tables, sems.at[1]),
    ]


def forward_kernel(
    turned, parity, *refs
):
    own, other = refs[0], None if turned else refs[1]
    queries_w, own_w, other_w, output_w, gains, tables, _, *rest = refs[1 if turned else 2 :]
    mine, theirs, near_q, near_own, near_other, weight_sems, rows, row_sems = rest[:8]
    near_gains, near_tables, small_sems, near_out, out_sems, near_output_w, output_sems = rest[8:15]
    near = (near_q, near_own, near_other)
    row_copies = started(row_loads(own, other, rows, row_sems))
    loads = [started(part) for part in query_loads(queries_w, own_w, other_w, near, weight_sems)]
    small_copies = started(small_loads(gains, tables, near_gains, near_tables, small_sems))
    output_copies = [started(part) for part in output_loads(output_w, near_output_w, output_sems)]
    waited(row_copies)
    projected = ordered(project_chunks(rows, near, loads), parity[0])
    waited(small_copies)
    if turned:
        projected = dot(near_tables[3].astype(BF), projected).astype(BF)
    context = attend(projected, near_gains[...], near_tables[0], near_tables[1], near_tables[2])
    sent = []
    for c in range(STEPS):
        waited(output_copies[c])
        part = dot(context, near_output_w[:, c * CHUNK : (c + 1) * CHUNK])
        near_out[:, c * CHUNK : (c + 1) * CHUNK] = part.astype(BF)
        sent += started(stores(near_out, mine, theirs, c, out_sems))
    waited(sent)


def project_kernel(
    parity, own, queries_w, own_w, other_w, tables, after, out,
    near_q, near_own, near_other, weight_sems, rows, row_sems, near_turn, near_out, sems,
):
    del after
    near = (near_q, near_own, near_other)
    row_copies = started(row_loads(own, None, rows, row_sems))
    loads = [started(part) for part in query_loads(queries_w, own_w, other_w, near, weight_sems)]
    table_copy = started([pltpu.make_async_copy(tables.at[3], near_turn, sems.at[0])])
    waited(row_copies)
    projected = ordered(project_chunks(rows, near, loads), parity[0])
    waited(table_copy)
    near_out[...] = dot(near_turn[...].astype(BF), projected).astype(BF)
    waited(started([pltpu.make_async_copy(near_out, out, sems.at[1])]))


def context_kernel(
    part, own, other, output_w, after, out, rows, row_sems, near_output_w, output_sems, near_out, sems
):
    del after
    row_copies = started(row_loads(own, other, rows, row_sems, part))
    output_copies = [started(chunk) for chunk in output_loads(output_w, near_output_w, output_sems)]
    waited(row_copies)
    near_out[...] = context_chunks(rows, near_output_w, output_copies)
    waited(started([pltpu.make_async_copy(near_out, out, sems.at[0])]))


def context_chunks(rows, near_output_w, output_copies):
    context_grad = 0.0
    for c in range(STEPS):
        waited(output_copies[c])
        part = slice(c * CHUNK, (c + 1) * CHUNK)
        context_grad += dot_nt(rows[:, part], near_output_w[:, part])
    return context_grad


def grads_out(grads, near, loads, near_out, mine, theirs, out_sems):
    query_grad, own_grad, other_grad = grads
    near_q, near_own, near_other = near
    sent = []
    for c in range(STEPS):
        waited(loads[c])
        part = slice(c * CHUNK, (c + 1) * CHUNK)
        total = dot_nt(query_grad, near_q[part, :])
        total = total + dot(own_grad, near_own[:, part]) + dot(other_grad, near_other[:, part])
        near_out[:, part] = total.astype(BF)
        sent += started(stores(near_out, mine, theirs, c, out_sems))
    waited(sent)


def first_backward_kernel(
    parity, own, other, context_grad, queries_w, own_w, other_w, gains, tables, after, mine, theirs,
    near_q, near_own, near_other, weight_sems, rows, row_sems, near_gains, near_tables, small_sems,
    near_out, out_sems, near_context, context_sem,
):
    del after
    near = (near_q, near_own, near_other)
    row_copies = started(row_loads(own, other, rows, row_sems))
    loads = [started(part) for part in query_loads(queries_w, own_w, other_w, near, weight_sems)]
    small_copies = started(small_loads(gains, tables, near_gains, near_tables, small_sems))
    small_copies += started([pltpu.make_async_copy(context_grad, near_context, context_sem.at[0])])
    waited(row_copies)
    projected = ordered(project_chunks(rows, near, loads), parity[0])
    waited(small_copies)
    grads = attend_back(
        projected, near_context[...], near_gains[...], near_tables[0], near_tables[1], near_tables[2], parity[0]
    )
    grads_out(grads, near, [[]] * STEPS, near_out, mine, theirs, out_sems)


def second_backward_kernel(
    parity, own, other, projected, queries_w, own_w, other_w, output_w, gains, tables, after, mine, theirs,
    near_q, near_own, near_other, weight_sems, rows, row_sems, near_gains, near_tables, small_sems,
    near_out, out_sems, near_output_w, output_sems, near_projected, projected_sem,
):
    del after
    near = (near_q, near_own, near_other)
    row_copies = started(row_loads(own, other, rows, row_sems))
    output_copies = [started(part) for part in output_loads(output_w, near_output_w, output_sems)]
    small_copies = started(small_loads(gains, tables, near_gains, near_tables, small_sems))
    small_copies += started([pltpu.make_async_copy(projected, near_projected, projected_sem.at[0])])
    loads = [started(part) for part in query_loads(queries_w, own_w, other_w, near, weight_sems)]
    waited(row_copies)
    context_grad = context_chunks(rows, near_output_w, output_copies)
    waited(small_copies)
    grads = attend_back(
        near_projected[...], context_grad, near_gains[...], near_tables[0], near_tables[1], near_tables[2], parity[0]
    )
    grads_out(grads, near, loads, near_out, mine, theirs, out_sems)


def far_call(kernel, scalars, arrays, out_shape, scratch, time):
    return pl.pallas_call(
        kernel,
        out_shape=out_shape,
        in_specs=[SCALAR] * len(scalars) + [FAR] * len(arrays),
        out_specs=[FAR] * len(out_shape),
        scratch_shapes=scratch,
        compiler_params=PARAMS,
        cost_estimate=pl.CostEstimate(
            flops=time * 1000000000, bytes_accessed=1000, transcendentals=0
        ),
    )(*scalars, *arrays)


OUTPUT_SCRATCH = [pltpu.VMEM((QUERY, WIDTH), BF), pltpu.SemaphoreType.DMA((STEPS,))]
MAIN_SCRATCH = WEIGHT_SCRATCH + ROW_SCRATCH + SMALL_SCRATCH + OUT_SCRATCH
PROJECTED = jax.ShapeDtypeStruct((ROWS, QUERY + BOTH), BF)
CONTEXT = jax.ShapeDtypeStruct((ROWS, QUERY), jnp.float32)


def run_forward(gathered_rows, weights, small, after):
    arrays = [*gathered_rows, *weights, *small[1:], after]
    scratch = MAIN_SCRATCH + OUTPUT_SCRATCH
    kernel = functools.partial(forward_kernel, len(gathered_rows) == 1)
    return far_call(kernel, small[:1], arrays, [HALF_ROWS] * 2, scratch, 8)


def run_project(rows, weights, small, after):
    scratch = [
        pltpu.VMEM((ROWS, HEAD), jnp.float32),
        pltpu.VMEM(PROJECTED.shape, BF),
        pltpu.SemaphoreType.DMA((2,)),
    ]
    arrays = [rows, *weights[:3], small[2], after]
    return far_call(project_kernel, small[:1], arrays, [PROJECTED], WEIGHT_SCRATCH + ROW_SCRATCH + scratch, 5)[0]


def run_context(own, other, part, output_w, after):
    scratch = [pltpu.VMEM(CONTEXT.shape, CONTEXT.dtype), pltpu.SemaphoreType.DMA((1,))]
    kernel = functools.partial(context_kernel, part)
    arrays = [own, other, output_w, after]
    return far_call(kernel, [], arrays, [CONTEXT], ROW_SCRATCH + OUTPUT_SCRATCH + scratch, 4)[0]


def run_first_backward(own, other, context_grad, weights, small, after):
    scratch = [pltpu.VMEM(CONTEXT.shape, CONTEXT.dtype), pltpu.SemaphoreType.DMA((1,))]
    arrays = [own, other, context_grad, *weights[:3], *small[1:], after]
    outs = [HALF_ROWS] * 2
    return far_call(first_backward_kernel, small[:1], arrays, outs, MAIN_SCRATCH + scratch, 12)


def run_second_backward(own, other, projected, weights, small, after):
    scratch = [pltpu.VMEM(PROJECTED.shape, BF), pltpu.SemaphoreType.DMA((1,))]
    arrays = [own, other, projected, *weights, *small[1:], after]
    scratch = MAIN_SCRATCH + OUTPUT_SCRATCH + scratch
    return far_call(second_backward_kernel, small[:1], arrays, [HALF_ROWS] * 2, scratch, 12)


def mixed(weights, offset, stride, streams):
    return sum(weights[offset + i * stride] * streams[i] for i in range(4))


def normed_rows(scalars, streams, gain):
    total = mixed(scalars, 0, 1, streams.astype(jnp.float32))
    scale = norm_scale(total)
    return (total * scale * gain).astype(BF), total, scale


def out_grad_rows(scalars, grads):
    return mixed(scalars, 4, 1, grads.astype(jnp.float32)).astype(BF)


def front_kernel(scalars, slot, saved, grads, gain, both, combined, scale):
    both[:, :WIDTH], combined[...], row_scale = normed_rows(scalars, saved[slot[0]], gain[...])
    both[:, WIDTH:] = out_grad_rows(scalars, grads[...])
    scale[...] = jnp.broadcast_to(row_scale, scale.shape)


def norm_kernel(scalars, streams, gain, normed):
    normed[...] = normed_rows(scalars, streams[...], gain[...])[0]


def next_norm_kernel(scalars, local, arrived, fresh, gain, normed):
    rows = normed_rows(scalars, fresh[...], gain[...])[0]
    normed[...] = jnp.where(local[0] == 1, rows, arrived[...])


def next_grad_kernel(scalars, local, arrived, loss, out_grad):
    out_grad[...] = jnp.where(local[0] == 1, out_grad_rows(scalars, loss[...]), arrived[...])


def saved_kernel(scalars, slot, saved, gain, normed, combined, scale):
    normed[...], combined[...], row_scale = normed_rows(scalars, saved[1 - slot[0]], gain[...])
    scale[...] = jnp.broadcast_to(row_scale, scale.shape)


def pair_kernel(mine, received, out):
    pair = mine[...].astype(jnp.float32) + received[...].astype(jnp.float32)
    out[...] = pair.astype(out.dtype)


def forward_end_kernel(scalars, landed, streams, out):
    rows = jnp.sum(landed[...].astype(jnp.float32), axis=0)
    streams_f = streams[...].astype(jnp.float32)
    for i in range(4):
        out[i] = (mixed(scalars, 8 + 4 * i, 1, streams_f) + scalars[4 + i] * rows).astype(out.dtype)


def forward_next_kernel(scalars, following, landed, streams, next_gain, out, normed):
    forward_end_kernel(scalars, landed, streams, out)
    normed[...] = normed_rows(following, out[...], next_gain[...])[0]


def backward_next_kernel(scalars, preceding, landed, grads, gain, combined, scale, out, out_grad):
    backward_end_kernel(scalars, landed, grads, gain, combined, scale, out)
    out_grad[...] = out_grad_rows(preceding, out[...])


def backward_end_kernel(scalars, landed, grads, gain, combined, scale, out):
    weighted = jnp.sum(landed[...].astype(jnp.float32), axis=0) * gain[...]
    row_scale = scale[:, :1]
    inner = jnp.mean(weighted * combined[...], axis=-1, keepdims=True)
    combined_grad = row_scale * weighted - combined[...] * (row_scale * row_scale * row_scale * inner)
    grads_f = grads[...].astype(jnp.float32)
    for j in range(4):
        out[j] = (mixed(scalars, 8 + j, 4, grads_f) + scalars[j] * combined_grad).astype(out.dtype)


def plain(kernel, scalars, arrays, outs, after=None):
    n, m, k = len(scalars), len(arrays), len(outs)
    extra = [] if after is None else [after]
    e = len(extra)

    def body(*refs):
        far_in, far_out = refs[n : n + m], refs[n + m + e : n + m + e + k]
        rest = refs[n + m + e + k :]
        near_in, near_out, sems, out_sems = rest[:m], rest[m : m + k], rest[m + k], rest[m + k + 1]
        waited(
            started([pltpu.make_async_copy(far_in[i], near_in[i], sems.at[i]) for i in range(m)])
        )
        kernel(*refs[:n], *near_in, *near_out)
        sent = []
        for i in range(k):
            if outs[i][2]:
                for chip in range(8):
                    sent.append(
                        pltpu.make_async_copy(near_out[i], far_out[i].at[chip], out_sems.at[i, chip])
                    )
            else:
                sent.append(pltpu.make_async_copy(near_out[i], far_out[i], out_sems.at[i, 0]))
        waited(started(sent))

    shapes = [((8,) if out[2] else ()) + out[0] for out in outs]
    return pl.pallas_call(
        body,
        out_shape=[jax.ShapeDtypeStruct(shape, out[1]) for shape, out in zip(shapes, outs)],
        in_specs=[SCALAR] * n + [FAR] * (m + e),
        out_specs=[FAR] * k,
        scratch_shapes=[pltpu.VMEM(array.shape, array.dtype) for array in arrays]
        + [pltpu.VMEM(out[0], out[1]) for out in outs]
        + [pltpu.SemaphoreType.DMA((m,)), pltpu.SemaphoreType.DMA((k, 8))],
        compiler_params=PARAMS,
        cost_estimate=pl.CostEstimate(flops=2500000000, bytes_accessed=1000, transcendentals=0),
    )(*scalars, *arrays, *extra)


def after(value, *events):
    return lax.optimization_barrier((value, *events))[0]


def landed_rows(copies):
    own = lax.all_to_all(copies, "tensor", 0, 0, axis_index_groups=GROUPS, tiled=True)
    return own.reshape(HALF, -1)


def paired(mine, received, event):
    return plain(pair_kernel, [], [mine, received], [(mine.shape, mine.dtype, False)], event)[0]


def scattered(pair):
    return lax.all_to_all(
        pair.reshape(8, LOCAL, -1), "tensor", 0, 0, axis_index_groups=GROUPS, tiled=True
    )


def on_device(
    entering_streams,
    entering_grads,
    fresh_streams,
    loss_grads,
    stashed,
    slot_order,
    q_weight,
    kv_weight,
    out_weight,
    norm_gain,
    head_gains,
    stream_in,
    stream_out,
    stream_mix,
):
    section = lax.axis_index("section")
    parity = lax.axis_index("tensor") % 2
    partner = (section + 8) % 16
    queries_w, output_w = q_weight[0], out_weight[0]
    gain, gains = norm_gain[0], head_gains[0]
    mix_in, mix_out, mix = stream_in[0], stream_out[0], stream_mix[0]
    bf16, f32 = jnp.bfloat16, jnp.float32

    tables = jnp.where(parity == 0, jnp.asarray(TABLES[0]), jnp.asarray(TABLES[1]))

    own_w = jnp.swapaxes(kv_weight[0], 1, 2).reshape(HEAD, -1)
    other_w = other_core(own_w)
    weights = (queries_w, own_w, other_w, output_w)
    small = (parity[None].astype(jnp.int32), gains, tables)
    gain_row, mix_flat = gain[None], mix.reshape(16)
    row_shape, streams_shape = (LOCAL, WIDTH), (4, LOCAL, WIDTH)
    row, copied = (row_shape, bf16, False), (row_shape, bf16, True)
    streams_out = (streams_shape, bf16, False)
    state_outs = [(row_shape, f32, False), ((LOCAL, HEAD), f32, False)]

    scalars = jnp.concatenate([mix_in, mix_out, mix_flat])
    saved = to_partner(stashed[:, 0])
    forward_now, backward_now = entering_streams[0], entering_grads[0]
    params = jnp.concatenate([gain, scalars, jnp.zeros((104,), f32)])[None]
    params = shifted(params, -1)
    preceding = shifted(scalars, 1)
    at_start = (section == 0).astype(jnp.int32)[None]
    at_end = (section == 15).astype(jnp.int32)[None]
    slot = slot_order[section, 0][None]
    normed = plain(norm_kernel, [scalars], [forward_now, gain_row], [copied])[0]
    normed, saved, params, preceding = lax.optimization_barrier((normed, saved, params, preceding))
    next_gain, following = params[:, :WIDTH], params[0, WIDTH : WIDTH + 24]
    own = landed_rows(normed)
    other = other_core(own)

    both_out = ((LOCAL, 2 * WIDTH), bf16, True)
    both, *first_state = plain(
        front_kernel, [scalars, slot], [saved, backward_now, gain_row], [both_out] + state_outs, normed
    )
    both_own = landed_rows(both)

    forward_partial = run_forward([own, other], weights, small, both)
    forward_received = other_core(forward_partial[1])
    both_own = after(both_own, forward_partial[0])
    both_other = other_core(both_own)
    saved_normed, *second_state = plain(
        saved_kernel, [scalars, slot], [saved, gain_row], [row] + state_outs, forward_partial[0]
    )
    saved_rows = lax.all_gather(saved_normed, "tensor", axis=0, tiled=True)
    forward_pair = paired(forward_partial[0], forward_received, saved_normed)
    landed = scattered(forward_pair)

    evicted_first = to_partner(forward_now)
    both_other = after(both_other, forward_pair)
    context_grad = run_context(both_own, both_other, 1, output_w, evicted_first)
    backward_partial = run_first_backward(both_own, both_other, context_grad, weights, small, context_grad)
    backward_received = other_core(backward_partial[1])
    forward_out, next_normed = plain(
        forward_next_kernel,
        [scalars, following],
        [landed, forward_now, next_gain],
        [streams_out, row],
        backward_partial[0],
    )
    arrived = shifted(next_normed, 1)

    backward_pair = paired(backward_partial[0], backward_received, forward_out)
    landed = scattered(after(backward_pair, arrived))
    arrived = after(arrived, backward_pair)
    normed_copies = plain(
        next_norm_kernel, [scalars, at_start], [arrived, fresh_streams[0], gain_row], [copied]
    )[0]
    projected = run_project(saved_rows, weights, small, normed_copies)
    own = landed_rows(after(normed_copies, projected))
    backward_out, next_grad = plain(
        backward_next_kernel,
        [scalars, preceding],
        [landed, backward_now, gain_row, *first_state],
        [streams_out, row],
        projected,
    )
    arrived = shifted(next_grad, -1)

    grad_copies = plain(
        next_grad_kernel, [scalars, at_end], [arrived, loss_grads[0]], [copied]
    )[0]
    grad_own = landed_rows(grad_copies)
    own = after(own, arrived)
    other = other_core(own)
    forward_sent = after(forward_out, own)
    from_previous = shifted(forward_sent, 1)
    forward_partial = run_forward([own, other], weights, small, grad_copies)
    forward_received = other_core(forward_partial[1])
    own = after(grad_own, forward_partial[0])
    other = other_core(own)
    from_following = shifted(after(backward_out, own), -1)
    forward_pair = paired(forward_partial[0], forward_received, grad_copies)
    landed_forward = scattered(after(forward_pair, own))
    backward_partial = run_second_backward(own, other, projected, weights, small, forward_pair)
    backward_pair = paired(backward_partial[0], other_core(backward_partial[1]), from_following)
    landed_backward = scattered(backward_pair)
    from_previous = after(from_previous, backward_partial[0])
    forward_now = jnp.where(section == 0, fresh_streams[0], from_previous)
    evicted_second = to_partner(forward_now)
    backward_now = jnp.where(section == 15, loss_grads[0], from_following)
    forward_out = plain(
        forward_end_kernel, [scalars], [landed_forward, forward_now], [streams_out], backward_pair
    )[0]
    backward_out = plain(
        backward_end_kernel,
        [scalars],
        [landed_backward, backward_now, gain_row, *second_state],
        [streams_out],
        forward_out,
    )[0]
    evicted = jnp.stack([evicted_first, evicted_second])
    return (forward_out[None], backward_out[None], evicted[:, None])


def solution(mesh):
    return jax.shard_map(
        on_device,
        mesh=mesh,
        in_specs=(
            P("section", None, "tensor", None),
            P("section", None, "tensor", None),
            P(None, None, "tensor", None),
            P(None, None, "tensor", None),
            P(None, "section", None, "tensor", None),
            P(),
            P("section", None, "tensor"),
            P("section", None, None, "tensor"),
            P("section", "tensor", None),
            P("section", None),
            P("section", None, None),
            P("section", None),
            P("section", None),
            P("section", None, None),
        ),
        out_specs=(
            P("section", None, "tensor", None),
            P("section", None, "tensor", None),
            P(None, "section", None, "tensor", None),
        ),
        check_vma=False,
    )
```

time: 253 us -> 221 us (0.87)
  waiting for transfers between devices: 66.5 us -> 24.3 us
  Pallas kernels: 50.2 us -> 88.5 us
  local copies, waits for them, and re-layouts: 33.2 us -> 11.2 us
  other arithmetic: 14.5 us -> 4.89 us
  starting transfers between devices: 68.4 us -> 76.5 us
  between operations: 17.7 us -> 14.4 us
    pallas_call x16 -> x19, Pallas kernels: 50.2 us -> 88.5 us  [the longest x6 50.2 us: far_call(): pl.pallas_call(kernel, out_shape=out_shape, in_specs=[SCALAR] * len(scala...]
    unnamed x94 -> x52, local copies, waits for them, and re-layouts: 29 us -> 7.94 us
    ppermute x4 -> x3, waiting for transfers between devices: 19.6 us -> 0.01 us  [to_partner(): return lax.ppermute(value, 'section', [(i, i ^ 8) for i in range(16)])]
    all_to_all x8, waiting for transfers between devices: 31.6 us -> 14.4 us  [the longest x4 8.99 us: landed_rows(): lax.all_to_all(copies, 'tensor', 0, 0, axis_index_groups=GROUPS, tiled=True)]
    ppermute x2 -> x6, starting transfers between devices: 8.34 us -> 18 us  [shifted(): lax.ppermute(value, 'section', [(i, (i + by) % 16) for i in range(16)])]
    reshape x4 -> x0, other arithmetic: 8.66 us -> none  [scattered(): pair = pair.astype(jnp.bfloat16).reshape(8, LOCAL, -1)]
    all_gather x2 -> x1, waiting for transfers between devices: 7.04 us -> 0.02 us  [on_device(): saved_rows = lax.all_gather(saved_normed, 'tensor', axis=0, tiled=True)]
    ppermute x9, starting transfers between devices: 14.6 us -> 11.1 us  [other_core(): return lax.ppermute(value, 'tensor', [(i, i ^ 1) for i in range(16)])]
  transfers between devices with their start and end apart: 25 -> 27, of which waited for: 12 -> 9; matrix products, arithmetic and copies ran while one was open for 7% -> 4% of each run, Pallas kernels for 19% -> 39%
where the time goes in v2:
time: 221 us; the launch traced here: 220 us
  Pallas kernels  88.5 us (40%)
  starting transfers between devices  76.5 us (35%)
  waiting for transfers between devices  24.3 us (11%)
  between operations  14.4 us (7%)
  local copies, waits for them, and re-layouts  11.2 us (5%)
  other arithmetic  4.89 us (2%)
    pallas_call x6, Pallas kernels, far_call(): pl.pallas_call(kernel, out_shape=out_shape, in_specs=[SCALAR] * len(scala...  50.2 us
    pallas_call x13, Pallas kernels, plain(): pl.pallas_call(body, out_shape=[jax.ShapeDtypeStruct(shape, out[1]) for s...  38.3 us
    all_to_all x4, starting transfers between devices, scattered(): lax.all_to_all(pair.reshape(8, LOCAL, -1), 'tensor', 0, 0, axis_index_gro...  20.6 us
    all_to_all x4, starting transfers between devices, landed_rows(): lax.all_to_all(copies, 'tensor', 0, 0, axis_index_groups=GROUPS, tiled=True)  18.7 us
    ppermute x6, starting transfers between devices, shifted(): lax.ppermute(value, 'section', [(i, (i + by) % 16) for i in range(16)])  18 us
    ppermute x9, starting transfers between devices, other_core(): return lax.ppermute(value, 'tensor', [(i, i ^ 1) for i in range(16)])  11.1 us
    all_to_all x4, waiting for transfers between devices, landed_rows(): lax.all_to_all(copies, 'tensor', 0, 0, axis_index_groups=GROUPS, tiled=True)  8.99 us
    ppermute x3, starting transfers between devices, to_partner(): return lax.ppermute(value, 'section', [(i, i ^ 8) for i in range(16)])  8.09 us
  transfers between devices with their start and end apart: 27, of which 9 were waited for; matrix products, arithmetic and copies ran while one was open for 4% of the time, Pallas kernels for 39%

profile of v2, /device:TPU:1, one launch (start us, length us, event | category | flops | bytes accessed | tf_op | source)
XLA Modules:
  0.0 219.9 jit_solution(6786308654479152951)
XLA Ops:
  7.2 3.8 %collective-permute-start = (bf16[2,4,8,5120]{3,2,1,0:T(8,128)(2,1)}, bf16[2,4,8,5120]{3,2,1,0:T(8,128)(2,1)S(1)}, u32[]{:S(2)}, u32[]{:S(2)}) collective-permute-start(bf16[2,4,8,5120]{3,2,1,0:T(8,128)(2,1)} %bitcast.76), channel_id=1, source_target_pairs={{0,128},{16,144},{32,160},{48,176},{64,192},{80,208},{96,224},{112... | collective-permute-start | bytes 1966088 | tf_op jit(solution)/shard_map/ppermute | solution.py:30
  12.6 6.6 %collective-permute-start.1 = (f32[1,5248]{1,0:T(1,128)S(1)}, f32[1,5248]{1,0:T(1,128)S(1)}, u32[]{:S(2)}, u32[]{:S(2)}) collective-permute-start(f32[1,5248]{1,0:T(1,128)S(1)} %broadcast_in_dim.32), channel_id=1, source_target_pairs={{0,240},{16,0},{32,16},{48,32},{64,48},{80,64},{96,80},{112,96},{1... | collective-permute-start | bytes 62984 | tf_op jit(solution)/shard_map/ppermute | solution.py:34
  23.2 3.4 %collective-permute-done.2.refs_1_ = f32[24]{0:T(128)S(1)} collective-permute-done((f32[24]{0:T(128)S(1)}, f32[24]{0:T(128)S(1)}, u32[]{:S(2)}, u32[]{:S(2)}) %collective-permute-start.2) | collective-permute-done | bytes 128 | tf_op jit(solution)/shard_map/ppermute | solution.py:34
  26.6 4.5 %all-to-all-start = ((bf16[8,8,5120]{2,1,0:T(8,128)(2,1)}), bf16[8,8,5120]{2,1,0:T(8,128)(2,1)S(1)}, u32[]{:S(2)}, u32[]{:S(2)}) async-start(bf16[8,8,5120]{2,1,0:T(8,128)(2,1)} %shard_map.175.refs_5_), calls=%async_computation | async-start | bytes 1310720 | tf_op jit(solution)/shard_map/all_to_all | solution.py:544
  31.7 4.1 %shard_map.176 = (bf16[8,8,10240]{2,1,0:T(8,128)(2,1)}, f32[8,5120]{1,0:T(8,128)}, f32[8,128]{1,0:T(8,128)}) custom-call(f32[24]{0:T(128)} %copy-done.15, s32[1]{0:T(128)} %bitcast.17.refs_1_, bf16[2,4,8,5120]{3,2,1,0:T(8,128)(2,1)} %copy-done.16, bf16[4,8,5120]{2,1,0:T(8,128)(2,1)} %bitcast.80, f32[1,5120]{1,0:T(1,128)} %refs_3_.3, ...), custom_call_target="tpu_custom_call" | custom-call | flops 2500000000 | bytes 1000 | tf_op jit(solution)/shard_map/pallas_call | solution.py:526
  35.8 3.0 %all-to-all-done = bf16[8,8,5120]{2,1,0:T(8,128)(2,1)S(1)} async-done(((bf16[8,8,5120]{2,1,0:T(8,128)(2,1)}), bf16[8,8,5120]{2,1,0:T(8,128)(2,1)S(1)}, u32[]{:S(2)}, u32[]{:S(2)}) %all-to-all-start) | async-done | bytes 655392 | tf_op jit(solution)/shard_map/all_to_all | solution.py:544
  38.8 5.8 %all-to-all-start.2 = ((bf16[8,8,10240]{2,1,0:T(8,128)(2,1)}), bf16[8,8,10240]{2,1,0:T(8,128)(2,1)S(1)}, u32[]{:S(2)}, u32[]{:S(2)}) async-start(bf16[8,8,10240]{2,1,0:T(8,128)(2,1)} %get-tuple-element.39.refs_8_), calls=%async_computation.2 | async-start | bytes 2621440 | tf_op jit(solution)/shard_map/all_to_all | solution.py:544
  47.6 2.9 %collective-permute-done.4.refs_4_.other_w = bf16[128,5120]{1,0:T(8,128)(2,1)} collective-permute-done((bf16[128,5120]{1,0:T(8,128)(2,1)}, bf16[128,5120]{1,0:T(8,128)(2,1)}, u32[]{:S(2)}, u32[]{:S(2)}) %collective-permute-start.4) | collective-permute-done | bytes 1310752 | tf_op jit(solution)/shard_map/ppermute | solution.py:26
  51.4 8.6 %shard_map.177 = (bf16[64,5120]{1,0:T(8,128)(2,1)}, bf16[64,5120]{1,0:T(8,128)(2,1)}) custom-call(s32[1]{0:T(128)} %bitcast.2.parity, bf16[64,5120]{1,0:T(8,128)(2,1)} %bitcast.44, bf16[64,5120]{1,0:T(8,128)(2,1)} %copy-done.17, bf16[5120,384]{1,0:T(8,128)(2,1)} %bitcast.61, bf16[128,5120]{1,0:T(8,128)(2,1)} %bitcast.71, ...), custom_call_target="tpu_custom_call" | custom-call | flops 8000000000 | bytes 1000 | tf_op jit(solution)/shard_map/pallas_call | solution.py:374
  63.1 3.2 %collective-permute-start.7 = (bf16[4,8,5120]{2,1,0:T(8,128)(2,1)}, bf16[4,8,5120]{2,1,0:T(8,128)(2,1)}, u32[]{:S(2)}, u32[]{:S(2)}) collective-permute-start(bf16[4,8,5120]{2,1,0:T(8,128)(2,1)} %bitcast.78), channel_id=1, source_target_pairs={{0,128},{16,144},{32,160},{48,176},{64,192},{80,208},{96,224},{112... | collective-permute-start | bytes 983048 | tf_op jit(solution)/shard_map/ppermute | solution.py:30
  66.3 3.5 %shard_map.178 = (bf16[8,5120]{1,0:T(8,128)(2,1)}, f32[8,5120]{1,0:T(8,128)}, f32[8,128]{1,0:T(8,128)}) custom-call(f32[24]{0:T(128)} %copy-done.15, s32[1]{0:T(128)} %bitcast.17.refs_1_, bf16[2,4,8,5120]{3,2,1,0:T(8,128)(2,1)} %copy-done.16, f32[1,5120]{1,0:T(1,128)} %refs_3_.3, bf16[64,5120]{1,0:T(8,128)(2,1)} %get-tuple-element.40.refs_4_.refs_0_), custom_call_target="tpu_custom_call" | custom-call | flops 2500000000 | bytes 1000 | tf_op jit(solution)/shard_map/pallas_call | solution.py:526
  73.1 3.7 %all-to-all-start.1 = ((bf16[8,8,5120]{2,1,0:T(8,128)(2,1)}), bf16[8,8,5120]{2,1,0:T(8,128)(2,1)S(1)}, u32[]{:S(2)}, u32[]{:S(2)}) async-start(bf16[8,8,5120]{2,1,0:T(8,128)(2,1)} %bitcast.50), calls=%async_computation.1 | async-start | bytes 1310720 | tf_op jit(solution)/shard_map/all_to_all | solution.py:553
  76.9 4.5 %shard_map.180.context_grad.after = f32[128,384]{1,0:T(8,128)} custom-call(bf16[64,10240]{1,0:T(8,128)(2,1)} %bitcast.41, bf16[64,10240]{1,0:T(8,128)(2,1)} %collective-permute-done.6.other, bf16[384,5120]{1,0:T(8,128)(2,1)} %bitcast.67, bf16[4,8,5120]{2,1,0:T(8,128)(2,1)} %collective-permute-done.7.after), custom_call_target="tpu_custom_call" | custom-call | flops 4000000000 | bytes 1000 | tf_op jit(solution)/shard_map/pallas_call | solution.py:374
  81.4 9.6 %shard_map.181 = (bf16[64,5120]{1,0:T(8,128)(2,1)}, bf16[64,5120]{1,0:T(8,128)(2,1)}) custom-call(s32[1]{0:T(128)} %bitcast.2.parity, bf16[64,10240]{1,0:T(8,128)(2,1)} %bitcast.42, bf16[64,10240]{1,0:T(8,128)(2,1)} %collective-permute-done.6.other, f32[128,384]{1,0:T(8,128)} %shard_map.180.context_grad.after, bf16[5120,384]{1,0:T(8,128)(2,1)} %bitcast.62, ...), custom_call_target="tpu_custom_call" | custom-call | flops 12000000000 | bytes 1000 | tf_op jit(solution)/shard_map/pallas_call | solution.py:374
  93.9 3.3 %shard_map.182 = (bf16[4,8,5120]{2,1,0:T(8,128)(2,1)}, bf16[8,5120]{1,0:T(8,128)(2,1)}) custom-call(f32[24]{0:T(128)} %copy-done.15, f32[24]{0:T(128)} %slice_bitcast_fusion.refs_1_, bf16[8,8,5120]{2,1,0:T(8,128)(2,1)} %copy-done.6, bf16[4,8,5120]{2,1,0:T(8,128)(2,1)} %bitcast.79, f32[1,5120]{1,0:T(1,128)} %slice.7.refs_4_, ...), custom_call_target="tpu_custom_call" | custom-call | flops 2500000000 | bytes 1000 | tf_op jit(solution)/shard_map/pallas_call | solution.py:526
  97.2 3.1 %collective-permute-start.8 = (bf16[8,5120]{1,0:T(8,128)(2,1)}, bf16[8,5120]{1,0:T(8,128)(2,1)S(1)}, u32[]{:S(2)}, u32[]{:S(2)}) collective-permute-start(bf16[8,5120]{1,0:T(8,128)(2,1)} %get-tuple-element.46), channel_id=1, source_target_pairs={{0,16},{16,32},{32,48},{48,64},{64,80},{80,96},{96,112},{112,128},... | collective-permute-start | bytes 245768 | tf_op jit(solution)/shard_map/ppermute | solution.py:34
  103.5 3.4 %collective-permute-done.8.refs_2_ = bf16[8,5120]{1,0:T(8,128)(2,1)S(1)} collective-permute-done((bf16[8,5120]{1,0:T(8,128)(2,1)}, bf16[8,5120]{1,0:T(8,128)(2,1)S(1)}, u32[]{:S(2)}, u32[]{:S(2)}) %collective-permute-start.8) | collective-permute-done | bytes 81952 | tf_op jit(solution)/shard_map/ppermute | solution.py:34
  106.9 6.8 %all-to-all-start.4 = ((bf16[8,8,5120]{2,1,0:T(8,128)(2,1)}), bf16[8,8,5120]{2,1,0:T(8,128)(2,1)S(1)}, u32[]{:S(2)}, u32[]{:S(2)}) async-start(bf16[8,8,5120]{2,1,0:T(8,128)(2,1)} %bitcast.52), calls=%async_computation.4 | async-start | bytes 1310720 | tf_op jit(solution)/shard_map/all_to_all | solution.py:553
  116.6 5.9 %shard_map.185.refs_7_.projected = bf16[128,640]{1,0:T(8,128)(2,1)} custom-call(s32[1]{0:T(128)} %bitcast.2.parity, bf16[128,5120]{1,0:T(8,128)(2,1)} %all-gather.2.cloned.1.call-done.own, bf16[5120,384]{1,0:T(8,128)(2,1)} %bitcast.63, bf16[128,5120]{1,0:T(8,128)(2,1)} %bitcast.73, bf16[128,5120]{1,0:T(8,128)(2,1)} %collective-permute-done.4.refs_4_.other_w, ...), custom_call_target="tpu_custom_call" | custom-call | flops 5000000000 | bytes 1000 | tf_op jit(solution)/shard_map/pallas_call | solution.py:374
  123.4 4.7 %all-to-all-start.3 = ((bf16[8,8,5120]{2,1,0:T(8,128)(2,1)}), bf16[8,8,5120]{2,1,0:T(8,128)(2,1)S(1)}, u32[]{:S(2)}, u32[]{:S(2)}) async-start(bf16[8,8,5120]{2,1,0:T(8,128)(2,1)} %shard_map.184.after), calls=%async_computation.3 | async-start | bytes 1310720 | tf_op jit(solution)/shard_map/all_to_all | solution.py:544
  128.1 3.4 %shard_map.186 = (bf16[4,8,5120]{2,1,0:T(8,128)(2,1)}, bf16[8,5120]{1,0:T(8,128)(2,1)}) custom-call(f32[24]{0:T(128)} %copy-done.15, f32[24]{0:T(128)} %copy-done.25, bf16[8,8,5120]{2,1,0:T(8,128)(2,1)} %copy-done.7, bf16[4,8,5120]{2,1,0:T(8,128)(2,1)} %bitcast.81, f32[1,5120]{1,0:T(1,128)} %refs_3_.3, f32[8,5120]{1,0:T(8,128)} %get-tuple-element.53.refs_5_, ...), custom_call_target="tpu_custom_call" | custom-call | flops 2500000000 | bytes 1000 | tf_op jit(solution)/shard_map/pallas_call | solution.py:526
  133.9 4.6 %all-to-all-done.3 = bf16[8,8,5120]{2,1,0:T(8,128)(2,1)S(1)} async-done(((bf16[8,8,5120]{2,1,0:T(8,128)(2,1)}), bf16[8,8,5120]{2,1,0:T(8,128)(2,1)S(1)}, u32[]{:S(2)}, u32[]{:S(2)}) %all-to-all-start.3) | async-done | bytes 655392 | tf_op jit(solution)/shard_map/all_to_all | solution.py:544
  138.5 3.4 %collective-permute-start.11 = (bf16[64,5120]{1,0:T(8,128)(2,1)S(1)}, bf16[64,5120]{1,0:T(8,128)(2,1)S(1)}, u32[]{:S(2)}, u32[]{:S(2)}) collective-permute-start(bf16[64,5120]{1,0:T(8,128)(2,1)S(1)} %bitcast.47), channel_id=1, source_target_pairs={{0,1},{1,0},{2,3},{3,2},{4,5},{5,4},{6,7},{7,6},{8,9},{9,8},{10,11... | collective-permute-start | bytes 1966088 | tf_op jit(solution)/shard_map/ppermute | solution.py:26
  144.7 3.8 %all-to-all-start.5 = ((bf16[8,8,5120]{2,1,0:T(8,128)(2,1)}), bf16[8,8,5120]{2,1,0:T(8,128)(2,1)S(1)}, u32[]{:S(2)}, u32[]{:S(2)}) async-start(bf16[8,8,5120]{2,1,0:T(8,128)(2,1)} %shard_map.187.refs_8_.refs_2_), calls=%async_computation.5 | async-start | bytes 1310720 | tf_op jit(solution)/shard_map/all_to_all | solution.py:544
  149.3 8.6 %shard_map.188 = (bf16[64,5120]{1,0:T(8,128)(2,1)}, bf16[64,5120]{1,0:T(8,128)(2,1)}) custom-call(s32[1]{0:T(128)} %bitcast.2.parity, bf16[64,5120]{1,0:T(8,128)(2,1)} %bitcast.48, bf16[64,5120]{1,0:T(8,128)(2,1)} %copy-done.21, bf16[5120,384]{1,0:T(8,128)(2,1)} %bitcast.64, bf16[128,5120]{1,0:T(8,128)(2,1)} %bitcast.74, ...), custom_call_target="tpu_custom_call" | custom-call | flops 8000000000 | bytes 1000 | tf_op jit(solution)/shard_map/pallas_call | solution.py:374
  162.2 3.4 %collective-permute-start.16 = (bf16[4,8,5120]{2,1,0:T(8,128)(2,1)}, bf16[4,8,5120]{2,1,0:T(8,128)(2,1)S(1)}, u32[]{:S(2)}, u32[]{:S(2)}) collective-permute-start(bf16[4,8,5120]{2,1,0:T(8,128)(2,1)} %get-tuple-element.66), channel_id=1, source_target_pairs={{0,240},{16,0},{32,16},{48,32},{64,48},{80,64},{96,80},{112,96},{1... | collective-permute-start | bytes 983048 | tf_op jit(solution)/shard_map/ppermute | solution.py:34
  168.9 4.4 %all-to-all-start.6 = ((bf16[8,8,5120]{2,1,0:T(8,128)(2,1)}), bf16[8,8,5120]{2,1,0:T(8,128)(2,1)S(1)}, u32[]{:S(2)}, u32[]{:S(2)}) async-start(bf16[8,8,5120]{2,1,0:T(8,128)(2,1)} %bitcast.49), calls=%async_computation.6 | async-start | bytes 1310720 | tf_op jit(solution)/shard_map/all_to_all | solution.py:553
  173.4 12.8 %shard_map.190 = (bf16[64,5120]{1,0:T(8,128)(2,1)}, bf16[64,5120]{1,0:T(8,128)(2,1)}) custom-call(s32[1]{0:T(128)} %bitcast.2.parity, bf16[64,5120]{1,0:T(8,128)(2,1)} %bitcast.46, bf16[64,5120]{1,0:T(8,128)(2,1)} %collective-permute-done.14.other, bf16[128,640]{1,0:T(8,128)(2,1)} %shard_map.185.refs_7_.projected, bf16[5120,384]{1,0:T(8,128)(2,1)} %bitcast.65, ...), custom_call_target="tpu_custom_call" | custom-call | flops 12000000000 | bytes 1000 | tf_op jit(solution)/shard_map/pallas_call | solution.py:374
  193.1 5.6 %all-to-all-start.7 = ((bf16[8,8,5120]{2,1,0:T(8,128)(2,1)}), bf16[8,8,5120]{2,1,0:T(8,128)(2,1)S(1)}, u32[]{:S(2)}, u32[]{:S(2)}) async-start(bf16[8,8,5120]{2,1,0:T(8,128)(2,1)} %bitcast.51), calls=%async_computation.7 | async-start | bytes 1310720 | tf_op jit(solution)/shard_map/all_to_all | solution.py:553
  201.3 3.0 %shard_map.192.refs_6_ = bf16[4,8,5120]{2,1,0:T(8,128)(2,1)} custom-call(f32[24]{0:T(128)} %copy-done.15, bf16[8,8,5120]{2,1,0:T(8,128)(2,1)} %copy-done.3, bf16[4,8,5120]{2,1,0:T(8,128)(2,1)} %broadcast_select_fusion.1.refs_2_, bf16[64,5120]{1,0:T(8,128)(2,1)} %shard_map.191.refs_3_), custom_call_target="tpu_custom_call" | custom-call | flops 2500000000 | bytes 1000 | tf_op jit(solution)/shard_map/pallas_call | solution.py:526
  204.3 4.5 %all-to-all-done.7.refs_1_ = bf16[8,8,5120]{2,1,0:T(8,128)(2,1)S(1)} async-done(((bf16[8,8,5120]{2,1,0:T(8,128)(2,1)}), bf16[8,8,5120]{2,1,0:T(8,128)(2,1)S(1)}, u32[]{:S(2)}, u32[]{:S(2)}) %all-to-all-start.7) | async-done | bytes 655392 | tf_op jit(solution)/shard_map/all_to_all | solution.py:553
  209.7 3.3 %shard_map.193 = bf16[4,8,5120]{2,1,0:T(8,128)(2,1)} custom-call(f32[24]{0:T(128)} %copy-done.15, bf16[8,8,5120]{2,1,0:T(8,128)(2,1)} %copy-done.8, bf16[4,8,5120]{2,1,0:T(8,128)(2,1)} %broadcast_select_fusion.refs_2_, f32[1,5120]{1,0:T(1,128)} %refs_3_.3, f32[8,5120]{1,0:T(8,128)} %get-tuple-element.67.refs_4_, f32[8,128]{1,0:T(8,128)} %get-tuple-element.68.refs_5_, ...), custom_call_target="tpu_custom_call" | custom-call | flops 2500000000 | bytes 1000 | tf_op jit(solution)/shard_map/pallas_call | solution.py:526
  (106 shorter events, 50.1 us)
Async XLA Ops:
  7.2 23.9 %copy-start = (s32[16,2]{0,1:T(2,128)S(1)}, s32[16,2]{0,1:T(2,128)}, u32[]{:S(2)}) copy-start(s32[16,2]{0,1:T(2,128)} %param.21) | copy-start | bytes 388
  7.2 19.4 %collective-permute-start = (bf16[2,4,8,5120]{3,2,1,0:T(8,128)(2,1)}, bf16[2,4,8,5120]{3,2,1,0:T(8,128)(2,1)S(1)}, u32[]{:S(2)}, u32[]{:S(2)}) collective-permute-start(bf16[2,4,8,5120]{3,2,1,0:T(8,128)(2,1)} %bitcast.76), channel_id=1, source_target_pairs={{0,128},{16,144},{32,160},{48,176},{64,192},{80,208},{96,224},{112... | collective-permute-start | bytes 1966088 | tf_op jit(solution)/shard_map/ppermute | solution.py:30
  12.6 14.0 %collective-permute-start.1 = (f32[1,5248]{1,0:T(1,128)S(1)}, f32[1,5248]{1,0:T(1,128)S(1)}, u32[]{:S(2)}, u32[]{:S(2)}) collective-permute-start(f32[1,5248]{1,0:T(1,128)S(1)} %broadcast_in_dim.32), channel_id=1, source_target_pairs={{0,240},{16,0},{32,16},{48,32},{64,48},{80,64},{96,80},{112,96},{1... | collective-permute-start | bytes 62984 | tf_op jit(solution)/shard_map/ppermute | solution.py:34
  19.9 6.6 %collective-permute-start.2 = (f32[24]{0:T(128)S(1)}, f32[24]{0:T(128)S(1)}, u32[]{:S(2)}, u32[]{:S(2)}) collective-permute-start(f32[24]{0:T(128)S(1)} %pad_maximum_fusion.refs_0_), channel_id=1, source_target_pairs={{0,16},{16,32},{32,48},{48,64},{64,80},{80,96},{96,112},{112,128},... | collective-permute-start | bytes 296 | tf_op jit(solution)/shard_map/ppermute | solution.py:34
  26.6 9.2 %copy-start.25 = (f32[24]{0:T(128)}, f32[24]{0:T(128)S(1)}, u32[]{:S(2)}) copy-start(f32[24]{0:T(128)S(1)} %collective-permute-done.2.refs_1_) | copy-start | bytes 292
  26.6 12.2 %all-to-all-start = ((bf16[8,8,5120]{2,1,0:T(8,128)(2,1)}), bf16[8,8,5120]{2,1,0:T(8,128)(2,1)S(1)}, u32[]{:S(2)}, u32[]{:S(2)}) async-start(bf16[8,8,5120]{2,1,0:T(8,128)(2,1)} %shard_map.175.refs_5_), calls=%async_computation | async-start | bytes 1310720 | tf_op jit(solution)/shard_map/all_to_all | solution.py:544
  38.8 22.6 %all-to-all-start.2 = ((bf16[8,8,10240]{2,1,0:T(8,128)(2,1)}), bf16[8,8,10240]{2,1,0:T(8,128)(2,1)S(1)}, u32[]{:S(2)}, u32[]{:S(2)}) async-start(bf16[8,8,10240]{2,1,0:T(8,128)(2,1)} %get-tuple-element.39.refs_8_), calls=%async_computation.2 | async-start | bytes 2621440 | tf_op jit(solution)/shard_map/all_to_all | solution.py:544
  44.6 72.0 %all-gather.2.cloned.1.call-start = ((), (), s32[]{:S(2)}) async-start(), calls=%async_computation.8 | async-start | bytes 1392640 | tf_op jit(solution)/shard_map/all_gather | solution.py:622
  44.6 5.9 %collective-permute-start.4 = (bf16[128,5120]{1,0:T(8,128)(2,1)}, bf16[128,5120]{1,0:T(8,128)(2,1)}, u32[]{:S(2)}, u32[]{:S(2)}) collective-permute-start(bf16[128,5120]{1,0:T(8,128)(2,1)} %bitcast.70), channel_id=1, source_target_pairs={{0,1},{1,0},{2,3},{3,2},{4,5},{5,4},{6,7},{7,6},{8,9},{9,8},{10,11... | collective-permute-start | bytes 3932168 | tf_op jit(solution)/shard_map/ppermute | solution.py:26
  46.8 3.7 %collective-permute-start.3 = (bf16[64,5120]{1,0:T(8,128)(2,1)S(1)}, bf16[64,5120]{1,0:T(8,128)(2,1)S(1)}, u32[]{:S(2)}, u32[]{:S(2)}) collective-permute-start(bf16[64,5120]{1,0:T(8,128)(2,1)S(1)} %bitcast.43), channel_id=1, source_target_pairs={{0,1},{1,0},{2,3},{3,2},{4,5},{5,4},{6,7},{7,6},{8,9},{9,8},{10,11... | collective-permute-start | bytes 1966088 | tf_op jit(solution)/shard_map/ppermute | solution.py:26
  61.4 8.4 %copy-start.1 = (bf16[8,8,10240]{2,1,0:T(8,128)(2,1)}, bf16[8,8,10240]{2,1,0:T(8,128)(2,1)S(1)}, u32[]{:S(2)}) copy-start(bf16[8,8,10240]{2,1,0:T(8,128)(2,1)S(1)} %all-to-all-done.2) | copy-start | bytes 3932164
  61.4 15.4 %collective-permute-start.6 = (bf16[64,10240]{1,0:T(8,128)(2,1)S(1)}, bf16[64,10240]{1,0:T(8,128)(2,1)}, u32[]{:S(2)}, u32[]{:S(2)}) collective-permute-start(bf16[64,10240]{1,0:T(8,128)(2,1)S(1)} %bitcast.40), channel_id=1, source_target_pairs={{0,1},{1,0},{2,3},{3,2},{4,5},{5,4},{6,7},{7,6},{8,9},{9,8},{10,11... | collective-permute-start | bytes 3932168 | tf_op jit(solution)/shard_map/ppermute | solution.py:26
  63.1 6.8 %collective-permute-start.5 = (bf16[64,5120]{1,0:T(8,128)(2,1)}, bf16[64,5120]{1,0:T(8,128)(2,1)S(1)}, u32[]{:S(2)}, u32[]{:S(2)}) collective-permute-start(bf16[64,5120]{1,0:T(8,128)(2,1)} %get-tuple-element.41), channel_id=1, source_target_pairs={{0,1},{1,0},{2,3},{3,2},{4,5},{5,4},{6,7},{7,6},{8,9},{9,8},{10,11... | collective-permute-start | bytes 1966088 | tf_op jit(solution)/shard_map/ppermute | solution.py:26
  63.1 13.8 %collective-permute-start.7 = (bf16[4,8,5120]{2,1,0:T(8,128)(2,1)}, bf16[4,8,5120]{2,1,0:T(8,128)(2,1)}, u32[]{:S(2)}, u32[]{:S(2)}) collective-permute-start(bf16[4,8,5120]{2,1,0:T(8,128)(2,1)} %bitcast.78), channel_id=1, source_target_pairs={{0,128},{16,144},{32,160},{48,176},{64,192},{80,208},{96,224},{112... | collective-permute-start | bytes 983048 | tf_op jit(solution)/shard_map/ppermute | solution.py:30
  73.1 19.9 %all-to-all-start.1 = ((bf16[8,8,5120]{2,1,0:T(8,128)(2,1)}), bf16[8,8,5120]{2,1,0:T(8,128)(2,1)S(1)}, u32[]{:S(2)}, u32[]{:S(2)}) async-start(bf16[8,8,5120]{2,1,0:T(8,128)(2,1)} %bitcast.50), calls=%async_computation.1 | async-start | bytes 1310720 | tf_op jit(solution)/shard_map/all_to_all | solution.py:553
  91.1 9.2 %collective-permute-start.9 = (bf16[64,5120]{1,0:T(8,128)(2,1)}, bf16[64,5120]{1,0:T(8,128)(2,1)S(1)}, u32[]{:S(2)}, u32[]{:S(2)}) collective-permute-start(bf16[64,5120]{1,0:T(8,128)(2,1)} %get-tuple-element.47), channel_id=1, source_target_pairs={{0,1},{1,0},{2,3},{3,2},{4,5},{5,4},{6,7},{7,6},{8,9},{9,8},{10,11... | collective-permute-start | bytes 1966088 | tf_op jit(solution)/shard_map/ppermute | solution.py:26
  97.2 9.7 %collective-permute-start.8 = (bf16[8,5120]{1,0:T(8,128)(2,1)}, bf16[8,5120]{1,0:T(8,128)(2,1)S(1)}, u32[]{:S(2)}, u32[]{:S(2)}) collective-permute-start(bf16[8,5120]{1,0:T(8,128)(2,1)} %get-tuple-element.46), channel_id=1, source_target_pairs={{0,16},{16,32},{32,48},{48,64},{64,80},{80,96},{96,112},{112,128},... | collective-permute-start | bytes 245768 | tf_op jit(solution)/shard_map/ppermute | solution.py:34
  106.9 16.5 %all-to-all-start.4 = ((bf16[8,8,5120]{2,1,0:T(8,128)(2,1)}), bf16[8,8,5120]{2,1,0:T(8,128)(2,1)S(1)}, u32[]{:S(2)}, u32[]{:S(2)}) async-start(bf16[8,8,5120]{2,1,0:T(8,128)(2,1)} %bitcast.52), calls=%async_computation.4 | async-start | bytes 1310720 | tf_op jit(solution)/shard_map/all_to_all | solution.py:553
  123.4 15.1 %all-to-all-start.3 = ((bf16[8,8,5120]{2,1,0:T(8,128)(2,1)}), bf16[8,8,5120]{2,1,0:T(8,128)(2,1)S(1)}, u32[]{:S(2)}, u32[]{:S(2)}) async-start(bf16[8,8,5120]{2,1,0:T(8,128)(2,1)} %shard_map.184.after), calls=%async_computation.3 | async-start | bytes 1310720 | tf_op jit(solution)/shard_map/all_to_all | solution.py:544
  131.5 7.0 %collective-permute-start.10 = (bf16[8,5120]{1,0:T(8,128)(2,1)}, bf16[8,5120]{1,0:T(8,128)(2,1)S(1)}, u32[]{:S(2)}, u32[]{:S(2)}) collective-permute-start(bf16[8,5120]{1,0:T(8,128)(2,1)} %get-tuple-element.55), channel_id=1, source_target_pairs={{0,240},{16,0},{32,16},{48,32},{64,48},{80,64},{96,80},{112,96},{1... | collective-permute-start | bytes 245768 | tf_op jit(solution)/shard_map/ppermute | solution.py:34
  138.5 9.9 %collective-permute-start.11 = (bf16[64,5120]{1,0:T(8,128)(2,1)S(1)}, bf16[64,5120]{1,0:T(8,128)(2,1)S(1)}, u32[]{:S(2)}, u32[]{:S(2)}) collective-permute-start(bf16[64,5120]{1,0:T(8,128)(2,1)S(1)} %bitcast.47), channel_id=1, source_target_pairs={{0,1},{1,0},{2,3},{3,2},{4,5},{5,4},{6,7},{7,6},{8,9},{9,8},{10,11... | collective-permute-start | bytes 1966088 | tf_op jit(solution)/shard_map/ppermute | solution.py:26
  144.7 13.9 %all-to-all-start.5 = ((bf16[8,8,5120]{2,1,0:T(8,128)(2,1)}), bf16[8,8,5120]{2,1,0:T(8,128)(2,1)S(1)}, u32[]{:S(2)}, u32[]{:S(2)}) async-start(bf16[8,8,5120]{2,1,0:T(8,128)(2,1)} %shard_map.187.refs_8_.refs_2_), calls=%async_computation.5 | async-start | bytes 1310720 | tf_op jit(solution)/shard_map/all_to_all | solution.py:544
  157.9 7.8 %collective-permute-start.12 = (bf16[64,5120]{1,0:T(8,128)(2,1)}, bf16[64,5120]{1,0:T(8,128)(2,1)S(1)}, u32[]{:S(2)}, u32[]{:S(2)}) collective-permute-start(bf16[64,5120]{1,0:T(8,128)(2,1)} %get-tuple-element.58), channel_id=1, source_target_pairs={{0,1},{1,0},{2,3},{3,2},{4,5},{5,4},{6,7},{7,6},{8,9},{9,8},{10,11... | collective-permute-start | bytes 1966088 | tf_op jit(solution)/shard_map/ppermute | solution.py:26
  158.6 10.3 %copy-start.4 = (bf16[8,8,5120]{2,1,0:T(8,128)(2,1)}, bf16[8,8,5120]{2,1,0:T(8,128)(2,1)S(1)}, u32[]{:S(2)}) copy-start(bf16[8,8,5120]{2,1,0:T(8,128)(2,1)S(1)} %all-to-all-done.5) | copy-start | bytes 1966084
  158.6 14.8 %collective-permute-start.14 = (bf16[64,5120]{1,0:T(8,128)(2,1)S(1)}, bf16[64,5120]{1,0:T(8,128)(2,1)}, u32[]{:S(2)}, u32[]{:S(2)}) collective-permute-start(bf16[64,5120]{1,0:T(8,128)(2,1)S(1)} %bitcast.45), channel_id=1, source_target_pairs={{0,1},{1,0},{2,3},{3,2},{4,5},{5,4},{6,7},{7,6},{8,9},{9,8},{10,11... | collective-permute-start | bytes 1966088 | tf_op jit(solution)/shard_map/ppermute | solution.py:26
  159.8 26.4 %collective-permute-start.13 = (bf16[4,8,5120]{2,1,0:T(8,128)(2,1)}, bf16[4,8,5120]{2,1,0:T(8,128)(2,1)}, u32[]{:S(2)}, u32[]{:S(2)}) collective-permute-start(bf16[4,8,5120]{2,1,0:T(8,128)(2,1)} %get-tuple-element.61.refs_2_), channel_id=1, source_target_pairs={{0,16},{16,32},{32,48},{48,64},{64,80},{80,96},{96,112},{112,128},... | collective-permute-start | bytes 983048 | tf_op jit(solution)/shard_map/ppermute | solution.py:34
  162.2 26.8 %collective-permute-start.16 = (bf16[4,8,5120]{2,1,0:T(8,128)(2,1)}, bf16[4,8,5120]{2,1,0:T(8,128)(2,1)S(1)}, u32[]{:S(2)}, u32[]{:S(2)}) collective-permute-start(bf16[4,8,5120]{2,1,0:T(8,128)(2,1)} %get-tuple-element.66), channel_id=1, source_target_pairs={{0,240},{16,0},{32,16},{48,32},{64,48},{80,64},{96,80},{112,96},{1... | collective-permute-start | bytes 983048 | tf_op jit(solution)/shard_map/ppermute | solution.py:34
  168.9 24.2 %all-to-all-start.6 = ((bf16[8,8,5120]{2,1,0:T(8,128)(2,1)}), bf16[8,8,5120]{2,1,0:T(8,128)(2,1)S(1)}, u32[]{:S(2)}, u32[]{:S(2)}) async-start(bf16[8,8,5120]{2,1,0:T(8,128)(2,1)} %bitcast.49), calls=%async_computation.6 | async-start | bytes 1310720 | tf_op jit(solution)/shard_map/all_to_all | solution.py:553
  173.4 13.8 %copy-start.9 = (bf16[1,4,8,5120]{3,2,1,0:T(8,128)(2,1)S(1)}, bf16[1,4,8,5120]{3,2,1,0:T(8,128)(2,1)}, u32[]{:S(2)}) copy-start(bf16[1,4,8,5120]{3,2,1,0:T(8,128)(2,1)} %param.18) | copy-start | bytes 983044
  186.2 2.9 %collective-permute-start.15 = (bf16[64,5120]{1,0:T(8,128)(2,1)}, bf16[64,5120]{1,0:T(8,128)(2,1)S(1)}, u32[]{:S(2)}, u32[]{:S(2)}) collective-permute-start(bf16[64,5120]{1,0:T(8,128)(2,1)} %get-tuple-element.64), channel_id=1, source_target_pairs={{0,1},{1,0},{2,3},{3,2},{4,5},{5,4},{6,7},{7,6},{8,9},{9,8},{10,11... | collective-permute-start | bytes 1966088 | tf_op jit(solution)/shard_map/ppermute | solution.py:26
  188.0 11.5 %collective-permute-start.17 = (bf16[4,8,5120]{2,1,0:T(8,128)(2,1)}, bf16[4,8,5120]{2,1,0:T(8,128)(2,1)S(1)}, u32[]{:S(2)}, u32[]{:S(2)}) collective-permute-start(bf16[4,8,5120]{2,1,0:T(8,128)(2,1)} %broadcast_select_fusion.1.refs_2_), channel_id=1, source_target_pairs={{0,128},{16,144},{32,160},{48,176},{64,192},{80,208},{96,224},{112... | collective-permute-start | bytes 983048 | tf_op jit(solution)/shard_map/ppermute | solution.py:30
  193.1 15.7 %all-to-all-start.7 = ((bf16[8,8,5120]{2,1,0:T(8,128)(2,1)}), bf16[8,8,5120]{2,1,0:T(8,128)(2,1)S(1)}, u32[]{:S(2)}, u32[]{:S(2)}) async-start(bf16[8,8,5120]{2,1,0:T(8,128)(2,1)} %bitcast.51), calls=%async_computation.7 | async-start | bytes 1310720 | tf_op jit(solution)/shard_map/all_to_all | solution.py:553
  (21 other events, 77.9 us)
Sparse Core Ops, SparseCore 0:
  70.0 37.0 all-gather.1

commit v3 on v2

--- a/solution.py
+++ b/solution.py
@@ -280,19 +280,17 @@
 
 
 def project_kernel(
-    parity, own, queries_w, own_w, other_w, tables, after, out,
-    near_q, near_own, near_other, weight_sems, rows, row_sems, near_turn, near_out, sems,
+    parity, own, other, queries_w, own_w, other_w, after, out,
+    near_q, near_own, near_other, weight_sems, rows, row_sems, near_out, sems,
 ):
     del after
     near = (near_q, near_own, near_other)
-    row_copies = started(row_loads(own, None, rows, row_sems))
+    row_copies = started(row_loads(own, other, rows, row_sems, 2))
     loads = [started(part) for part in query_loads(queries_w, own_w, other_w, near, weight_sems)]
-    table_copy = started([pltpu.make_async_copy(tables.at[3], near_turn, sems.at[0])])
     waited(row_copies)
     projected = ordered(project_chunks(rows, near, loads), parity[0])
-    waited(table_copy)
-    near_out[...] = dot(near_turn[...].astype(BF), projected).astype(BF)
-    waited(started([pltpu.make_async_copy(near_out, out, sems.at[1])]))
+    near_out[...] = projected
+    waited(started([pltpu.make_async_copy(near_out, out, sems.at[0])]))
 
 
 def context_kernel(
@@ -397,14 +395,11 @@
     return far_call(kernel, small[:1], arrays, [HALF_ROWS] * 2, scratch, 8)
 
 
-def run_project(rows, weights, small, after):
-    scratch = [
-        pltpu.VMEM((ROWS, HEAD), jnp.float32),
-        pltpu.VMEM(PROJECTED.shape, BF),
-        pltpu.SemaphoreType.DMA((2,)),
-    ]
-    arrays = [rows, *weights[:3], small[2], after]
-    return far_call(project_kernel, small[:1], arrays, [PROJECTED], WEIGHT_SCRATCH + ROW_SCRATCH + scratch, 5)[0]
+def run_project(own, other, weights, small, after):
+    scratch = [pltpu.VMEM(PROJECTED.shape, BF), pltpu.SemaphoreType.DMA((1,))]
+    arrays = [own, other, *weights[:3], after]
+    scratch = WEIGHT_SCRATCH + ROW_SCRATCH + scratch
+    return far_call(project_kernel, small[:1], arrays, [PROJECTED], scratch, 5)[0]
 
 
 def run_context(own, other, part, output_w, after):
@@ -442,10 +437,14 @@
     return mixed(scalars, 4, 1, grads.astype(jnp.float32)).astype(BF)
 
 
-def front_kernel(scalars, slot, saved, grads, gain, both, combined, scale):
-    both[:, :WIDTH], combined[...], row_scale = normed_rows(scalars, saved[slot[0]], gain[...])
-    both[:, WIDTH:] = out_grad_rows(scalars, grads[...])
-    scale[...] = jnp.broadcast_to(row_scale, scale.shape)
+def front_kernel(scalars, slot, saved, grads, gain, every, *states):
+    for tick in range(2):
+        combined, scale = states[2 * tick : 2 * tick + 2]
+        chosen = slot[0] if tick == 0 else 1 - slot[0]
+        normed, combined[...], row_scale = normed_rows(scalars, saved[chosen], gain[...])
+        every[:, 2 * tick * WIDTH : (2 * tick + 1) * WIDTH] = normed
+        scale[...] = jnp.broadcast_to(row_scale, scale.shape)
+    every[:, WIDTH : 2 * WIDTH] = out_grad_rows(scalars, grads[...])
 
 
 def norm_kernel(scalars, streams, gain, normed):
@@ -459,11 +458,6 @@
 
 def next_grad_kernel(scalars, local, arrived, loss, out_grad):
     out_grad[...] = jnp.where(local[0] == 1, out_grad_rows(scalars, loss[...]), arrived[...])
-
-
-def saved_kernel(scalars, slot, saved, gain, normed, combined, scale):
-    normed[...], combined[...], row_scale = normed_rows(scalars, saved[1 - slot[0]], gain[...])
-    scale[...] = jnp.broadcast_to(row_scale, scale.shape)
 
 
 def pair_kernel(mine, received, out):
@@ -606,25 +600,21 @@
     own = landed_rows(normed)
     other = other_core(own)
 
-    both_out = ((LOCAL, 2 * WIDTH), bf16, True)
-    both, *first_state = plain(
-        front_kernel, [scalars, slot], [saved, backward_now, gain_row], [both_out] + state_outs, normed
+    both_out = ((LOCAL, 3 * WIDTH), bf16, True)
+    both, *states = plain(
+        front_kernel, [scalars, slot], [saved, backward_now, gain_row], [both_out] + state_outs * 2, normed
     )
+    first_state, second_state = states[:2], states[2:]
     both_own = landed_rows(both)
 
     forward_partial = run_forward([own, other], weights, small, both)
     forward_received = other_core(forward_partial[1])
-    both_own = after(both_own, forward_partial[0])
+    forward_pair = paired(forward_partial[0], forward_received, forward_partial[0])
+    evicted_first = to_partner(forward_now)
+    both_own = after(both_own, forward_pair, evicted_first)
     both_other = other_core(both_own)
-    saved_normed, *second_state = plain(
-        saved_kernel, [scalars, slot], [saved, gain_row], [row] + state_outs, forward_partial[0]
-    )
-    saved_rows = lax.all_gather(saved_normed, "tensor", axis=0, tiled=True)
-    forward_pair = paired(forward_partial[0], forward_received, saved_normed)
     landed = scattered(forward_pair)
 
-    evicted_first = to_partner(forward_now)
-    both_other = after(both_other, forward_pair)
     context_grad = run_context(both_own, both_other, 1, output_w, evicted_first)
     backward_partial = run_first_backward(both_own, both_other, context_grad, weights, small, context_grad)
     backward_received = other_core(backward_partial[1])
@@ -643,7 +633,7 @@
     normed_copies = plain(
         next_norm_kernel, [scalars, at_start], [arrived, fresh_streams[0], gain_row], [copied]
     )[0]
-    projected = run_project(saved_rows, weights, small, normed_copies)
+    projected = run_project(both_own, both_other, weights, small, normed_copies)
     own = landed_rows(after(normed_copies, projected))
     backward_out, next_grad = plain(
         backward_next_kernel,

time: 221 us -> 208 us (0.941)
  between operations: 14.4 us -> 1.11 us
  waiting for transfers between devices: 24.3 us -> 29.4 us
  Pallas kernels: 88.5 us -> 85.1 us
  local copies, waits for them, and re-layouts: 11.2 us -> 8.92 us
    ppermute x3, waiting for transfers between devices: 0.01 us -> 5.99 us  [to_partner(): return lax.ppermute(value, 'section', [(i, i ^ 8) for i in range(16)])]
    pallas_call x13 -> x12, Pallas kernels: 38.3 us -> 35.2 us  [plain(): pl.pallas_call(body, out_shape=[jax.ShapeDtypeStruct(shape, out[1]) for s...]
    unnamed x52 -> x44, local copies, waits for them, and re-layouts: 7.94 us -> 5.56 us
    all_to_all x4, waiting for transfers between devices: 8.99 us -> 6.78 us  [landed_rows(): lax.all_to_all(copies, 'tensor', 0, 0, axis_index_groups=GROUPS, tiled=True)]
  transfers between devices with their start and end apart: 27 -> 26, of which waited for: 9 -> 10; matrix products, arithmetic and copies ran while one was open for 4% -> 5% of each run, Pallas kernels for 39% -> 40%
where the time goes in v3:
time: 208 us; the launch traced here: 207 us
  Pallas kernels  85.1 us (41%)
  starting transfers between devices  76.3 us (37%)
  waiting for transfers between devices  29.4 us (14%)
  local copies, waits for them, and re-layouts  8.92 us (4%)
  other arithmetic  6.01 us (3%)
    pallas_call x6, Pallas kernels, far_call(): pl.pallas_call(kernel, out_shape=out_shape, in_specs=[SCALAR] * len(scala...  49.9 us
    pallas_call x12, Pallas kernels, plain(): pl.pallas_call(body, out_shape=[jax.ShapeDtypeStruct(shape, out[1]) for s...  35.2 us
    all_to_all x4, starting transfers between devices, scattered(): lax.all_to_all(pair.reshape(8, LOCAL, -1), 'tensor', 0, 0, axis_index_gro...  22.6 us
    all_to_all x4, starting transfers between devices, landed_rows(): lax.all_to_all(copies, 'tensor', 0, 0, axis_index_groups=GROUPS, tiled=True)  18.6 us
    ppermute x6, starting transfers between devices, shifted(): lax.ppermute(value, 'section', [(i, (i + by) % 16) for i in range(16)])  18 us
    ppermute x9, starting transfers between devices, other_core(): return lax.ppermute(value, 'tensor', [(i, i ^ 1) for i in range(16)])  10.3 us
    ppermute x6, waiting for transfers between devices, shifted(): lax.ppermute(value, 'section', [(i, (i + by) % 16) for i in range(16)])  8.12 us
    all_to_all x4, waiting for transfers between devices, landed_rows(): lax.all_to_all(copies, 'tensor', 0, 0, axis_index_groups=GROUPS, tiled=True)  6.78 us
  transfers between devices with their start and end apart: 26, of which 10 were waited for; matrix products, arithmetic and copies ran while one was open for 5% of the time, Pallas kernels for 40%

profile of v3, /device:TPU:1, one launch (start us, length us, event | category | flops | bytes accessed | tf_op | source)
XLA Modules:
  0.0 206.8 jit_solution(4434477241444498928)
XLA Ops:
  0.6 3.8 %collective-permute-start = (bf16[2,4,8,5120]{3,2,1,0:T(8,128)(2,1)}, bf16[2,4,8,5120]{3,2,1,0:T(8,128)(2,1)S(1)}, u32[]{:S(2)}, u32[]{:S(2)}) collective-permute-start(bf16[2,4,8,5120]{3,2,1,0:T(8,128)(2,1)} %bitcast.76), channel_id=1, source_target_pairs={{0,128},{16,144},{32,160},{48,176},{64,192},{80,208},{96,224},{112... | collective-permute-start | bytes 1966088 | tf_op jit(solution)/shard_map/ppermute | solution.py:30
  6.1 6.6 %collective-permute-start.1 = (f32[1,5248]{1,0:T(1,128)S(1)}, f32[1,5248]{1,0:T(1,128)S(1)}, u32[]{:S(2)}, u32[]{:S(2)}) collective-permute-start(f32[1,5248]{1,0:T(1,128)S(1)} %broadcast_in_dim.32), channel_id=1, source_target_pairs={{0,240},{16,0},{32,16},{48,32},{64,48},{80,64},{96,80},{112,96},{1... | collective-permute-start | bytes 62984 | tf_op jit(solution)/shard_map/ppermute | solution.py:34
  13.9 2.7 %shard_map.175.refs_5_ = bf16[8,8,5120]{2,1,0:T(8,128)(2,1)} custom-call(f32[24]{0:T(128)} %copy-done.13, bf16[4,8,5120]{2,1,0:T(8,128)(2,1)} %bitcast.77, f32[1,5120]{1,0:T(1,128)} %refs_3_.1), custom_call_target="tpu_custom_call" | custom-call | flops 2500000000 | bytes 1000 | tf_op jit(solution)/shard_map/pallas_call | solution.py:520
  16.7 3.4 %collective-permute-done.2.refs_1_ = f32[24]{0:T(128)S(1)} collective-permute-done((f32[24]{0:T(128)S(1)}, f32[24]{0:T(128)S(1)}, u32[]{:S(2)}, u32[]{:S(2)}) %collective-permute-start.2) | collective-permute-done | bytes 128 | tf_op jit(solution)/shard_map/ppermute | solution.py:34
  20.1 4.5 %all-to-all-start = ((bf16[8,8,5120]{2,1,0:T(8,128)(2,1)}), bf16[8,8,5120]{2,1,0:T(8,128)(2,1)S(1)}, u32[]{:S(2)}, u32[]{:S(2)}) async-start(bf16[8,8,5120]{2,1,0:T(8,128)(2,1)} %shard_map.175.refs_5_), calls=%async_computation | async-start | bytes 1310720 | tf_op jit(solution)/shard_map/all_to_all | solution.py:538
  25.1 4.6 %shard_map.176 = (bf16[8,8,15360]{2,1,0:T(8,128)(2,1)}, f32[8,5120]{1,0:T(8,128)}, f32[8,128]{1,0:T(8,128)}, f32[8,5120]{1,0:T(8,128)}, f32[8,128]{1,0:T(8,128)}) custom-call(f32[24]{0:T(128)} %copy-done.13, s32[1]{0:T(128)} %bitcast.17.refs_1_, bf16[2,4,8,5120]{3,2,1,0:T(8,128)(2,1)} %copy-done.14, bf16[4,8,5120]{2,1,0:T(8,128)(2,1)} %bitcast.80, ...), custom_call_target="tpu_custom_call" | custom-call | flops 2500000000 | bytes 1000 | tf_op jit(solution)/shard_map/pallas_call | solution.py:520
  33.1 5.6 %all-to-all-start.2 = ((bf16[8,8,15360]{2,1,0:T(8,128)(2,1)}), bf16[8,8,15360]{2,1,0:T(8,128)(2,1)S(1)}, u32[]{:S(2)}, u32[]{:S(2)}) async-start(bf16[8,8,15360]{2,1,0:T(8,128)(2,1)} %get-tuple-element.37.refs_8_), calls=%async_computation.2 | async-start | bytes 3932160 | tf_op jit(solution)/shard_map/all_to_all | solution.py:538
  44.9 8.7 %shard_map.177 = (bf16[64,5120]{1,0:T(8,128)(2,1)}, bf16[64,5120]{1,0:T(8,128)(2,1)}) custom-call(s32[1]{0:T(128)} %bitcast.2.parity, bf16[64,5120]{1,0:T(8,128)(2,1)} %bitcast.45, bf16[64,5120]{1,0:T(8,128)(2,1)} %collective-permute-done.3.refs_1_, bf16[5120,384]{1,0:T(8,128)(2,1)} %bitcast.61, bf16[128,5120]{1,0:T(8,128)(2,1)} %bitcast.71, ...), custom_call_target="tpu_custom_call" | custom-call | flops 8000000000 | bytes 1000 | tf_op jit(solution)/shard_map/pallas_call | solution.py:372
  59.0 6.0 %collective-permute-done.6.after = bf16[4,8,5120]{2,1,0:T(8,128)(2,1)} collective-permute-done((bf16[4,8,5120]{2,1,0:T(8,128)(2,1)}, bf16[4,8,5120]{2,1,0:T(8,128)(2,1)}, u32[]{:S(2)}, u32[]{:S(2)}) %collective-permute-start.6) | collective-permute-done | bytes 327712 | tf_op jit(solution)/shard_map/ppermute | solution.py:30
  65.9 5.3 %all-to-all-start.1 = ((bf16[8,8,5120]{2,1,0:T(8,128)(2,1)}), bf16[8,8,5120]{2,1,0:T(8,128)(2,1)}, u32[]{:S(2)}, u32[]{:S(2)}) async-start(bf16[8,8,5120]{2,1,0:T(8,128)(2,1)} %bitcast.51), calls=%async_computation.1 | async-start | bytes 1310720 | tf_op jit(solution)/shard_map/all_to_all | solution.py:547
  71.2 4.5 %shard_map.179.context_grad.after = f32[128,384]{1,0:T(8,128)} custom-call(bf16[64,15360]{1,0:T(8,128)(2,1)} %bitcast.41, bf16[64,15360]{1,0:T(8,128)(2,1)} %collective-permute-done.7.other, bf16[384,5120]{1,0:T(8,128)(2,1)} %bitcast.67, bf16[4,8,5120]{2,1,0:T(8,128)(2,1)} %collective-permute-done.6.after), custom_call_target="tpu_custom_call" | custom-call | flops 4000000000 | bytes 1000 | tf_op jit(solution)/shard_map/pallas_call | solution.py:372
  75.8 9.6 %shard_map.180 = (bf16[64,5120]{1,0:T(8,128)(2,1)}, bf16[64,5120]{1,0:T(8,128)(2,1)}) custom-call(s32[1]{0:T(128)} %bitcast.2.parity, bf16[64,15360]{1,0:T(8,128)(2,1)} %bitcast.42, bf16[64,15360]{1,0:T(8,128)(2,1)} %collective-permute-done.7.other, f32[128,384]{1,0:T(8,128)} %shard_map.179.context_grad.after, bf16[5120,384]{1,0:T(8,128)(2,1)} %bitcast.62, ...), custom_call_target="tpu_custom_call" | custom-call | flops 12000000000 | bytes 1000 | tf_op jit(solution)/shard_map/pallas_call | solution.py:372
  86.9 3.3 %shard_map.181 = (bf16[4,8,5120]{2,1,0:T(8,128)(2,1)}, bf16[8,5120]{1,0:T(8,128)(2,1)}) custom-call(f32[24]{0:T(128)} %copy-done.13, f32[24]{0:T(128)} %slice_bitcast_fusion.refs_1_, bf16[8,8,5120]{2,1,0:T(8,128)(2,1)} %all-to-all-done.1.refs_2_, bf16[4,8,5120]{2,1,0:T(8,128)(2,1)} %bitcast.79, f32[1,5120]{1,0:T(1,128)} %slice.7.refs_4_, ...), custom_call_target="tpu_custom_call" | custom-call | flops 2500000000 | bytes 1000 | tf_op jit(solution)/shard_map/pallas_call | solution.py:520
  90.2 2.8 %collective-permute-start.8 = (bf16[8,5120]{1,0:T(8,128)(2,1)}, bf16[8,5120]{1,0:T(8,128)(2,1)S(1)}, u32[]{:S(2)}, u32[]{:S(2)}) collective-permute-start(bf16[8,5120]{1,0:T(8,128)(2,1)} %get-tuple-element.42), channel_id=1, source_target_pairs={{0,16},{16,32},{32,48},{48,64},{64,80},{80,96},{96,112},{112,128},... | collective-permute-start | bytes 245768 | tf_op jit(solution)/shard_map/ppermute | solution.py:34
  96.2 4.7 %collective-permute-done.8.refs_2_ = bf16[8,5120]{1,0:T(8,128)(2,1)S(1)} collective-permute-done((bf16[8,5120]{1,0:T(8,128)(2,1)}, bf16[8,5120]{1,0:T(8,128)(2,1)S(1)}, u32[]{:S(2)}, u32[]{:S(2)}) %collective-permute-start.8) | collective-permute-done | bytes 81952 | tf_op jit(solution)/shard_map/ppermute | solution.py:34
  100.9 7.5 %all-to-all-start.4 = ((bf16[8,8,5120]{2,1,0:T(8,128)(2,1)}), bf16[8,8,5120]{2,1,0:T(8,128)(2,1)S(1)}, u32[]{:S(2)}, u32[]{:S(2)}) async-start(bf16[8,8,5120]{2,1,0:T(8,128)(2,1)} %bitcast.53), calls=%async_computation.4 | async-start | bytes 1310720 | tf_op jit(solution)/shard_map/all_to_all | solution.py:547
  108.4 2.8 %shard_map.183.after = bf16[8,8,5120]{2,1,0:T(8,128)(2,1)} custom-call(f32[24]{0:T(128)} %copy-done.13, s32[1]{0:T(128)} %bitcast.3.refs_1_, bf16[8,5120]{1,0:T(8,128)(2,1)} %copy-done.19, bf16[4,8,5120]{2,1,0:T(8,128)(2,1)} %bitcast.54, f32[1,5120]{1,0:T(1,128)} %refs_3_.1), custom_call_target="tpu_custom_call" | custom-call | flops 2500000000 | bytes 1000 | tf_op jit(solution)/shard_map/pallas_call | solution.py:520
  111.2 5.7 %shard_map.184.refs_7_.projected = bf16[128,640]{1,0:T(8,128)(2,1)} custom-call(s32[1]{0:T(128)} %bitcast.2.parity, bf16[64,15360]{1,0:T(8,128)(2,1)} %bitcast.43, bf16[64,15360]{1,0:T(8,128)(2,1)} %collective-permute-done.7.other, bf16[5120,384]{1,0:T(8,128)(2,1)} %bitcast.63, bf16[128,5120]{1,0:T(8,128)(2,1)} %bitcast.73, ...), custom_call_target="tpu_custom_call" | custom-call | flops 5000000000 | bytes 1000 | tf_op jit(solution)/shard_map/pallas_call | solution.py:372
  118.1 4.7 %all-to-all-start.3 = ((bf16[8,8,5120]{2,1,0:T(8,128)(2,1)}), bf16[8,8,5120]{2,1,0:T(8,128)(2,1)S(1)}, u32[]{:S(2)}, u32[]{:S(2)}) async-start(bf16[8,8,5120]{2,1,0:T(8,128)(2,1)} %shard_map.183.after), calls=%async_computation.3 | async-start | bytes 1310720 | tf_op jit(solution)/shard_map/all_to_all | solution.py:538
  122.8 3.4 %shard_map.185 = (bf16[4,8,5120]{2,1,0:T(8,128)(2,1)}, bf16[8,5120]{1,0:T(8,128)(2,1)}) custom-call(f32[24]{0:T(128)} %copy-done.13, f32[24]{0:T(128)} %copy-done.21, bf16[8,8,5120]{2,1,0:T(8,128)(2,1)} %copy-done.6, bf16[4,8,5120]{2,1,0:T(8,128)(2,1)} %bitcast.81, f32[1,5120]{1,0:T(1,128)} %refs_3_.1, f32[8,5120]{1,0:T(8,128)} %get-tuple-element.49.refs_5_, ...), custom_call_target="tpu_custom_call" | custom-call | flops 2500000000 | bytes 1000 | tf_op jit(solution)/shard_map/pallas_call | solution.py:520
  128.6 4.3 %all-to-all-done.3 = bf16[8,8,5120]{2,1,0:T(8,128)(2,1)S(1)} async-done(((bf16[8,8,5120]{2,1,0:T(8,128)(2,1)}), bf16[8,8,5120]{2,1,0:T(8,128)(2,1)S(1)}, u32[]{:S(2)}, u32[]{:S(2)}) %all-to-all-start.3) | async-done | bytes 655392 | tf_op jit(solution)/shard_map/all_to_all | solution.py:538
  132.9 3.1 %collective-permute-start.11 = (bf16[64,5120]{1,0:T(8,128)(2,1)S(1)}, bf16[64,5120]{1,0:T(8,128)(2,1)S(1)}, u32[]{:S(2)}, u32[]{:S(2)}) collective-permute-start(bf16[64,5120]{1,0:T(8,128)(2,1)S(1)} %bitcast.49), channel_id=1, source_target_pairs={{0,1},{1,0},{2,3},{3,2},{4,5},{5,4},{6,7},{7,6},{8,9},{9,8},{10,11... | collective-permute-start | bytes 1966088 | tf_op jit(solution)/shard_map/ppermute | solution.py:26
  136.0 2.7 %shard_map.186.refs_8_.refs_2_ = bf16[8,8,5120]{2,1,0:T(8,128)(2,1)} custom-call(f32[24]{0:T(128)} %copy-done.13, s32[1]{0:T(128)} %bitcast.24.refs_1_, bf16[8,5120]{1,0:T(8,128)(2,1)} %copy-done.20, bf16[4,8,5120]{2,1,0:T(8,128)(2,1)} %bitcast.55), custom_call_target="tpu_custom_call" | custom-call | flops 2500000000 | bytes 1000 | tf_op jit(solution)/shard_map/pallas_call | solution.py:520
  138.7 3.8 %all-to-all-start.5 = ((bf16[8,8,5120]{2,1,0:T(8,128)(2,1)}), bf16[8,8,5120]{2,1,0:T(8,128)(2,1)S(1)}, u32[]{:S(2)}, u32[]{:S(2)}) async-start(bf16[8,8,5120]{2,1,0:T(8,128)(2,1)} %shard_map.186.refs_8_.refs_2_), calls=%async_computation.5 | async-start | bytes 1310720 | tf_op jit(solution)/shard_map/all_to_all | solution.py:538
  143.4 8.6 %shard_map.187 = (bf16[64,5120]{1,0:T(8,128)(2,1)}, bf16[64,5120]{1,0:T(8,128)(2,1)}) custom-call(s32[1]{0:T(128)} %bitcast.2.parity, bf16[64,5120]{1,0:T(8,128)(2,1)} %bitcast.50, bf16[64,5120]{1,0:T(8,128)(2,1)} %copy-done.17, bf16[5120,384]{1,0:T(8,128)(2,1)} %bitcast.64, bf16[128,5120]{1,0:T(8,128)(2,1)} %bitcast.74, ...), custom_call_target="tpu_custom_call" | custom-call | flops 8000000000 | bytes 1000 | tf_op jit(solution)/shard_map/pallas_call | solution.py:372
  155.5 4.9 %collective-permute-start.16 = (bf16[4,8,5120]{2,1,0:T(8,128)(2,1)}, bf16[4,8,5120]{2,1,0:T(8,128)(2,1)S(1)}, u32[]{:S(2)}, u32[]{:S(2)}) collective-permute-start(bf16[4,8,5120]{2,1,0:T(8,128)(2,1)} %get-tuple-element.62), channel_id=1, source_target_pairs={{0,240},{16,0},{32,16},{48,32},{64,48},{80,64},{96,80},{112,96},{1... | collective-permute-start | bytes 983048 | tf_op jit(solution)/shard_map/ppermute | solution.py:34
  163.6 4.5 %all-to-all-start.6 = ((bf16[8,8,5120]{2,1,0:T(8,128)(2,1)}), bf16[8,8,5120]{2,1,0:T(8,128)(2,1)S(1)}, u32[]{:S(2)}, u32[]{:S(2)}) async-start(bf16[8,8,5120]{2,1,0:T(8,128)(2,1)} %bitcast.48), calls=%async_computation.6 | async-start | bytes 1310720 | tf_op jit(solution)/shard_map/all_to_all | solution.py:547
  168.1 12.8 %shard_map.189 = (bf16[64,5120]{1,0:T(8,128)(2,1)}, bf16[64,5120]{1,0:T(8,128)(2,1)}) custom-call(s32[1]{0:T(128)} %bitcast.2.parity, bf16[64,5120]{1,0:T(8,128)(2,1)} %bitcast.47, bf16[64,5120]{1,0:T(8,128)(2,1)} %collective-permute-done.14.other, bf16[128,640]{1,0:T(8,128)(2,1)} %shard_map.184.refs_7_.projected, bf16[5120,384]{1,0:T(8,128)(2,1)} %bitcast.65, ...), custom_call_target="tpu_custom_call" | custom-call | flops 12000000000 | bytes 1000 | tf_op jit(solution)/shard_map/pallas_call | solution.py:372
  187.0 5.4 %all-to-all-start.7 = ((bf16[8,8,5120]{2,1,0:T(8,128)(2,1)}), bf16[8,8,5120]{2,1,0:T(8,128)(2,1)S(1)}, u32[]{:S(2)}, u32[]{:S(2)}) async-start(bf16[8,8,5120]{2,1,0:T(8,128)(2,1)} %bitcast.52), calls=%async_computation.7 | async-start | bytes 1310720 | tf_op jit(solution)/shard_map/all_to_all | solution.py:547
  196.2 3.0 %shard_map.191.refs_6_ = bf16[4,8,5120]{2,1,0:T(8,128)(2,1)} custom-call(f32[24]{0:T(128)} %copy-done.13, bf16[8,8,5120]{2,1,0:T(8,128)(2,1)} %copy-done.3, bf16[4,8,5120]{2,1,0:T(8,128)(2,1)} %broadcast_select_fusion.1.refs_2_, bf16[64,5120]{1,0:T(8,128)(2,1)} %shard_map.190.refs_3_), custom_call_target="tpu_custom_call" | custom-call | flops 2500000000 | bytes 1000 | tf_op jit(solution)/shard_map/pallas_call | solution.py:520
  199.2 3.4 %all-to-all-done.7.refs_1_ = bf16[8,8,5120]{2,1,0:T(8,128)(2,1)S(1)} async-done(((bf16[8,8,5120]{2,1,0:T(8,128)(2,1)}), bf16[8,8,5120]{2,1,0:T(8,128)(2,1)S(1)}, u32[]{:S(2)}, u32[]{:S(2)}) %all-to-all-start.7) | async-done | bytes 655392 | tf_op jit(solution)/shard_map/all_to_all | solution.py:547
  203.4 3.3 %shard_map.192 = bf16[4,8,5120]{2,1,0:T(8,128)(2,1)} custom-call(f32[24]{0:T(128)} %copy-done.13, bf16[8,8,5120]{2,1,0:T(8,128)(2,1)} %copy-done.7, bf16[4,8,5120]{2,1,0:T(8,128)(2,1)} %broadcast_select_fusion.refs_2_, f32[1,5120]{1,0:T(1,128)} %refs_3_.1, f32[8,5120]{1,0:T(8,128)} %get-tuple-element.63.refs_4_, f32[8,128]{1,0:T(8,128)} %get-tuple-element.64.refs_5_, ...), custom_call_target="tpu_custom_call" | custom-call | flops 2500000000 | bytes 1000 | tf_op jit(solution)/shard_map/pallas_call | solution.py:520
  (94 shorter events, 45.9 us)
Async XLA Ops:
  0.6 23.9 %copy-start = (s32[16,2]{0,1:T(2,128)S(1)}, s32[16,2]{0,1:T(2,128)}, u32[]{:S(2)}) copy-start(s32[16,2]{0,1:T(2,128)} %param.21) | copy-start | bytes 388
  0.6 19.4 %collective-permute-start = (bf16[2,4,8,5120]{3,2,1,0:T(8,128)(2,1)}, bf16[2,4,8,5120]{3,2,1,0:T(8,128)(2,1)S(1)}, u32[]{:S(2)}, u32[]{:S(2)}) collective-permute-start(bf16[2,4,8,5120]{3,2,1,0:T(8,128)(2,1)} %bitcast.76), channel_id=1, source_target_pairs={{0,128},{16,144},{32,160},{48,176},{64,192},{80,208},{96,224},{112... | collective-permute-start | bytes 1966088 | tf_op jit(solution)/shard_map/ppermute | solution.py:30
  6.1 14.0 %collective-permute-start.1 = (f32[1,5248]{1,0:T(1,128)S(1)}, f32[1,5248]{1,0:T(1,128)S(1)}, u32[]{:S(2)}, u32[]{:S(2)}) collective-permute-start(f32[1,5248]{1,0:T(1,128)S(1)} %broadcast_in_dim.32), channel_id=1, source_target_pairs={{0,240},{16,0},{32,16},{48,32},{64,48},{80,64},{96,80},{112,96},{1... | collective-permute-start | bytes 62984 | tf_op jit(solution)/shard_map/ppermute | solution.py:34
  13.4 6.6 %collective-permute-start.2 = (f32[24]{0:T(128)S(1)}, f32[24]{0:T(128)S(1)}, u32[]{:S(2)}, u32[]{:S(2)}) collective-permute-start(f32[24]{0:T(128)S(1)} %pad_maximum_fusion.refs_0_), channel_id=1, source_target_pairs={{0,16},{16,32},{32,48},{48,64},{64,80},{80,96},{96,112},{112,128},... | collective-permute-start | bytes 296 | tf_op jit(solution)/shard_map/ppermute | solution.py:34
  20.0 9.7 %copy-start.21 = (f32[24]{0:T(128)}, f32[24]{0:T(128)S(1)}, u32[]{:S(2)}) copy-start(f32[24]{0:T(128)S(1)} %collective-permute-done.2.refs_1_) | copy-start | bytes 292
  20.1 12.2 %all-to-all-start = ((bf16[8,8,5120]{2,1,0:T(8,128)(2,1)}), bf16[8,8,5120]{2,1,0:T(8,128)(2,1)S(1)}, u32[]{:S(2)}, u32[]{:S(2)}) async-start(bf16[8,8,5120]{2,1,0:T(8,128)(2,1)} %shard_map.175.refs_5_), calls=%async_computation | async-start | bytes 1310720 | tf_op jit(solution)/shard_map/all_to_all | solution.py:538
  33.1 31.9 %all-to-all-start.2 = ((bf16[8,8,15360]{2,1,0:T(8,128)(2,1)}), bf16[8,8,15360]{2,1,0:T(8,128)(2,1)S(1)}, u32[]{:S(2)}, u32[]{:S(2)}) async-start(bf16[8,8,15360]{2,1,0:T(8,128)(2,1)} %get-tuple-element.37.refs_8_), calls=%async_computation.2 | async-start | bytes 3932160 | tf_op jit(solution)/shard_map/all_to_all | solution.py:538
  38.7 5.2 %collective-permute-start.4 = (bf16[128,5120]{1,0:T(8,128)(2,1)}, bf16[128,5120]{1,0:T(8,128)(2,1)}, u32[]{:S(2)}, u32[]{:S(2)}) collective-permute-start(bf16[128,5120]{1,0:T(8,128)(2,1)} %bitcast.70), channel_id=1, source_target_pairs={{0,1},{1,0},{2,3},{3,2},{4,5},{5,4},{6,7},{7,6},{8,9},{9,8},{10,11... | collective-permute-start | bytes 3932168 | tf_op jit(solution)/shard_map/ppermute | solution.py:26
  40.9 3.9 %collective-permute-start.3 = (bf16[64,5120]{1,0:T(8,128)(2,1)}, bf16[64,5120]{1,0:T(8,128)(2,1)}, u32[]{:S(2)}, u32[]{:S(2)}) collective-permute-start(bf16[64,5120]{1,0:T(8,128)(2,1)} %bitcast.44), channel_id=1, source_target_pairs={{0,1},{1,0},{2,3},{3,2},{4,5},{5,4},{6,7},{7,6},{8,9},{9,8},{10,11... | collective-permute-start | bytes 1966088 | tf_op jit(solution)/shard_map/ppermute | solution.py:26
  53.5 3.1 %collective-permute-start.5 = (bf16[64,5120]{1,0:T(8,128)(2,1)}, bf16[64,5120]{1,0:T(8,128)(2,1)}, u32[]{:S(2)}, u32[]{:S(2)}) collective-permute-start(bf16[64,5120]{1,0:T(8,128)(2,1)} %get-tuple-element.39), channel_id=1, source_target_pairs={{0,1},{1,0},{2,3},{3,2},{4,5},{5,4},{6,7},{7,6},{8,9},{9,8},{10,11... | collective-permute-start | bytes 1966088 | tf_op jit(solution)/shard_map/ppermute | solution.py:26
  54.0 11.0 %collective-permute-start.6 = (bf16[4,8,5120]{2,1,0:T(8,128)(2,1)}, bf16[4,8,5120]{2,1,0:T(8,128)(2,1)}, u32[]{:S(2)}, u32[]{:S(2)}) collective-permute-start(bf16[4,8,5120]{2,1,0:T(8,128)(2,1)} %bitcast.78), channel_id=1, source_target_pairs={{0,128},{16,144},{32,160},{48,176},{64,192},{80,208},{96,224},{112... | collective-permute-start | bytes 983048 | tf_op jit(solution)/shard_map/ppermute | solution.py:30
  65.0 6.2 %collective-permute-start.7 = (bf16[64,15360]{1,0:T(8,128)(2,1)S(1)}, bf16[64,15360]{1,0:T(8,128)(2,1)}, u32[]{:S(2)}, u32[]{:S(2)}) collective-permute-start(bf16[64,15360]{1,0:T(8,128)(2,1)S(1)} %bitcast.40), channel_id=1, source_target_pairs={{0,1},{1,0},{2,3},{3,2},{4,5},{5,4},{6,7},{7,6},{8,9},{9,8},{10,11... | collective-permute-start | bytes 5898248 | tf_op jit(solution)/shard_map/ppermute | solution.py:26
  65.9 21.0 %all-to-all-start.1 = ((bf16[8,8,5120]{2,1,0:T(8,128)(2,1)}), bf16[8,8,5120]{2,1,0:T(8,128)(2,1)}, u32[]{:S(2)}, u32[]{:S(2)}) async-start(bf16[8,8,5120]{2,1,0:T(8,128)(2,1)} %bitcast.51), calls=%async_computation.1 | async-start | bytes 1310720 | tf_op jit(solution)/shard_map/all_to_all | solution.py:547
  85.4 7.6 %collective-permute-start.9 = (bf16[64,5120]{1,0:T(8,128)(2,1)}, bf16[64,5120]{1,0:T(8,128)(2,1)S(1)}, u32[]{:S(2)}, u32[]{:S(2)}) collective-permute-start(bf16[64,5120]{1,0:T(8,128)(2,1)} %get-tuple-element.43), channel_id=1, source_target_pairs={{0,1},{1,0},{2,3},{3,2},{4,5},{5,4},{6,7},{7,6},{8,9},{9,8},{10,11... | collective-permute-start | bytes 1966088 | tf_op jit(solution)/shard_map/ppermute | solution.py:26
  90.2 10.7 %collective-permute-start.8 = (bf16[8,5120]{1,0:T(8,128)(2,1)}, bf16[8,5120]{1,0:T(8,128)(2,1)S(1)}, u32[]{:S(2)}, u32[]{:S(2)}) collective-permute-start(bf16[8,5120]{1,0:T(8,128)(2,1)} %get-tuple-element.42), channel_id=1, source_target_pairs={{0,16},{16,32},{32,48},{48,64},{64,80},{80,96},{96,112},{112,128},... | collective-permute-start | bytes 245768 | tf_op jit(solution)/shard_map/ppermute | solution.py:34
  100.9 17.2 %all-to-all-start.4 = ((bf16[8,8,5120]{2,1,0:T(8,128)(2,1)}), bf16[8,8,5120]{2,1,0:T(8,128)(2,1)S(1)}, u32[]{:S(2)}, u32[]{:S(2)}) async-start(bf16[8,8,5120]{2,1,0:T(8,128)(2,1)} %bitcast.53), calls=%async_computation.4 | async-start | bytes 1310720 | tf_op jit(solution)/shard_map/all_to_all | solution.py:547
  118.1 14.8 %all-to-all-start.3 = ((bf16[8,8,5120]{2,1,0:T(8,128)(2,1)}), bf16[8,8,5120]{2,1,0:T(8,128)(2,1)S(1)}, u32[]{:S(2)}, u32[]{:S(2)}) async-start(bf16[8,8,5120]{2,1,0:T(8,128)(2,1)} %shard_map.183.after), calls=%async_computation.3 | async-start | bytes 1310720 | tf_op jit(solution)/shard_map/all_to_all | solution.py:538
  126.2 6.7 %collective-permute-start.10 = (bf16[8,5120]{1,0:T(8,128)(2,1)}, bf16[8,5120]{1,0:T(8,128)(2,1)S(1)}, u32[]{:S(2)}, u32[]{:S(2)}) collective-permute-start(bf16[8,5120]{1,0:T(8,128)(2,1)} %get-tuple-element.51), channel_id=1, source_target_pairs={{0,240},{16,0},{32,16},{48,32},{64,48},{80,64},{96,80},{112,96},{1... | collective-permute-start | bytes 245768 | tf_op jit(solution)/shard_map/ppermute | solution.py:34
  132.9 9.6 %collective-permute-start.11 = (bf16[64,5120]{1,0:T(8,128)(2,1)S(1)}, bf16[64,5120]{1,0:T(8,128)(2,1)S(1)}, u32[]{:S(2)}, u32[]{:S(2)}) collective-permute-start(bf16[64,5120]{1,0:T(8,128)(2,1)S(1)} %bitcast.49), channel_id=1, source_target_pairs={{0,1},{1,0},{2,3},{3,2},{4,5},{5,4},{6,7},{7,6},{8,9},{9,8},{10,11... | collective-permute-start | bytes 1966088 | tf_op jit(solution)/shard_map/ppermute | solution.py:26
  138.7 14.2 %all-to-all-start.5 = ((bf16[8,8,5120]{2,1,0:T(8,128)(2,1)}), bf16[8,8,5120]{2,1,0:T(8,128)(2,1)S(1)}, u32[]{:S(2)}, u32[]{:S(2)}) async-start(bf16[8,8,5120]{2,1,0:T(8,128)(2,1)} %shard_map.186.refs_8_.refs_2_), calls=%async_computation.5 | async-start | bytes 1310720 | tf_op jit(solution)/shard_map/all_to_all | solution.py:538
  152.0 8.3 %collective-permute-start.12 = (bf16[64,5120]{1,0:T(8,128)(2,1)}, bf16[64,5120]{1,0:T(8,128)(2,1)S(1)}, u32[]{:S(2)}, u32[]{:S(2)}) collective-permute-start(bf16[64,5120]{1,0:T(8,128)(2,1)} %get-tuple-element.54), channel_id=1, source_target_pairs={{0,1},{1,0},{2,3},{3,2},{4,5},{5,4},{6,7},{7,6},{8,9},{9,8},{10,11... | collective-permute-start | bytes 1966088 | tf_op jit(solution)/shard_map/ppermute | solution.py:26
  153.0 10.6 %copy-start.4 = (bf16[8,8,5120]{2,1,0:T(8,128)(2,1)}, bf16[8,8,5120]{2,1,0:T(8,128)(2,1)S(1)}, u32[]{:S(2)}) copy-start(bf16[8,8,5120]{2,1,0:T(8,128)(2,1)S(1)} %all-to-all-done.5) | copy-start | bytes 1966084
  153.0 15.1 %collective-permute-start.14 = (bf16[64,5120]{1,0:T(8,128)(2,1)S(1)}, bf16[64,5120]{1,0:T(8,128)(2,1)}, u32[]{:S(2)}, u32[]{:S(2)}) collective-permute-start(bf16[64,5120]{1,0:T(8,128)(2,1)S(1)} %bitcast.46), channel_id=1, source_target_pairs={{0,1},{1,0},{2,3},{3,2},{4,5},{5,4},{6,7},{7,6},{8,9},{9,8},{10,11... | collective-permute-start | bytes 1966088 | tf_op jit(solution)/shard_map/ppermute | solution.py:26
  154.2 26.7 %collective-permute-start.13 = (bf16[4,8,5120]{2,1,0:T(8,128)(2,1)}, bf16[4,8,5120]{2,1,0:T(8,128)(2,1)}, u32[]{:S(2)}, u32[]{:S(2)}) collective-permute-start(bf16[4,8,5120]{2,1,0:T(8,128)(2,1)} %get-tuple-element.57.refs_2_), channel_id=1, source_target_pairs={{0,16},{16,32},{32,48},{48,64},{64,80},{80,96},{96,112},{112,128},... | collective-permute-start | bytes 983048 | tf_op jit(solution)/shard_map/ppermute | solution.py:34
  155.5 27.5 %collective-permute-start.16 = (bf16[4,8,5120]{2,1,0:T(8,128)(2,1)}, bf16[4,8,5120]{2,1,0:T(8,128)(2,1)S(1)}, u32[]{:S(2)}, u32[]{:S(2)}) collective-permute-start(bf16[4,8,5120]{2,1,0:T(8,128)(2,1)} %get-tuple-element.62), channel_id=1, source_target_pairs={{0,240},{16,0},{32,16},{48,32},{64,48},{80,64},{96,80},{112,96},{1... | collective-permute-start | bytes 983048 | tf_op jit(solution)/shard_map/ppermute | solution.py:34
  163.6 23.4 %all-to-all-start.6 = ((bf16[8,8,5120]{2,1,0:T(8,128)(2,1)}), bf16[8,8,5120]{2,1,0:T(8,128)(2,1)S(1)}, u32[]{:S(2)}, u32[]{:S(2)}) async-start(bf16[8,8,5120]{2,1,0:T(8,128)(2,1)} %bitcast.48), calls=%async_computation.6 | async-start | bytes 1310720 | tf_op jit(solution)/shard_map/all_to_all | solution.py:547
  168.0 13.8 %copy-start.8 = (bf16[1,4,8,5120]{3,2,1,0:T(8,128)(2,1)S(1)}, bf16[1,4,8,5120]{3,2,1,0:T(8,128)(2,1)}, u32[]{:S(2)}) copy-start(bf16[1,4,8,5120]{3,2,1,0:T(8,128)(2,1)} %param.18) | copy-start | bytes 983044
  180.9 2.9 %collective-permute-start.15 = (bf16[64,5120]{1,0:T(8,128)(2,1)}, bf16[64,5120]{1,0:T(8,128)(2,1)S(1)}, u32[]{:S(2)}, u32[]{:S(2)}) collective-permute-start(bf16[64,5120]{1,0:T(8,128)(2,1)} %get-tuple-element.60), channel_id=1, source_target_pairs={{0,1},{1,0},{2,3},{3,2},{4,5},{5,4},{6,7},{7,6},{8,9},{9,8},{10,11... | collective-permute-start | bytes 1966088 | tf_op jit(solution)/shard_map/ppermute | solution.py:26
  182.7 9.8 %copy-start.9 = (bf16[1,4,8,5120]{3,2,1,0:T(8,128)(2,1)S(1)}, bf16[1,4,8,5120]{3,2,1,0:T(8,128)(2,1)}, u32[]{:S(2)}) copy-start(bf16[1,4,8,5120]{3,2,1,0:T(8,128)(2,1)} %param.19) | copy-start | bytes 983044
  182.7 11.6 %collective-permute-start.17 = (bf16[4,8,5120]{2,1,0:T(8,128)(2,1)}, bf16[4,8,5120]{2,1,0:T(8,128)(2,1)}, u32[]{:S(2)}, u32[]{:S(2)}) collective-permute-start(bf16[4,8,5120]{2,1,0:T(8,128)(2,1)} %broadcast_select_fusion.1.refs_2_), channel_id=1, source_target_pairs={{0,128},{16,144},{32,160},{48,176},{64,192},{80,208},{96,224},{112... | collective-permute-start | bytes 983048 | tf_op jit(solution)/shard_map/ppermute | solution.py:30
  187.0 9.2 %copy-start.3 = (bf16[8,8,5120]{2,1,0:T(8,128)(2,1)}, bf16[8,8,5120]{2,1,0:T(8,128)(2,1)S(1)}, u32[]{:S(2)}) copy-start(bf16[8,8,5120]{2,1,0:T(8,128)(2,1)S(1)} %all-to-all-done.6.refs_1_) | copy-start | bytes 1966084
  187.0 15.5 %all-to-all-start.7 = ((bf16[8,8,5120]{2,1,0:T(8,128)(2,1)}), bf16[8,8,5120]{2,1,0:T(8,128)(2,1)S(1)}, u32[]{:S(2)}, u32[]{:S(2)}) async-start(bf16[8,8,5120]{2,1,0:T(8,128)(2,1)} %bitcast.52), calls=%async_computation.7 | async-start | bytes 1310720 | tf_op jit(solution)/shard_map/all_to_all | solution.py:547
  (16 other events, 56.4 us)

commit v4 on v3

--- a/solution.py
+++ b/solution.py
@@ -540,7 +540,8 @@
 
 
 def paired(mine, received, event):
-    return plain(pair_kernel, [], [mine, received], [(mine.shape, mine.dtype, False)], event)[0]
+    pair = after(mine, event).astype(jnp.float32) + received.astype(jnp.float32)
+    return pair.astype(jnp.bfloat16)
 
 
 def scattered(pair):

time: 208 us -> 203 us (0.976)
  Pallas kernels: 85.1 us -> 75.9 us
  other arithmetic: 6.01 us -> 10.4 us
  local copies, waits for them, and re-layouts: 8.92 us -> 6.41 us
  starting transfers between devices: 76.3 us -> 78.4 us
    pallas_call x12 -> x8, Pallas kernels: 35.2 us -> 25.9 us  [plain(): pl.pallas_call(body, out_shape=[jax.ShapeDtypeStruct(shape, out[1]) for s...]
    convert_element_type x0 -> x4, other arithmetic: none -> 6.22 us  [paired(): return pair.astype(jnp.bfloat16)]
    unnamed x44 -> x42, local copies, waits for them, and re-layouts: 5.56 us -> 3.12 us
    ppermute x6, waiting for transfers between devices: 8.12 us -> 10.2 us  [shifted(): lax.ppermute(value, 'section', [(i, (i + by) % 16) for i in range(16)])]
    ppermute x3, waiting for transfers between devices: 5.99 us -> 8.08 us  [to_partner(): return lax.ppermute(value, 'section', [(i, i ^ 8) for i in range(16)])]
  transfers between devices with their start and end apart: 26 -> 26, of which waited for: 10 -> 10; matrix products, arithmetic and copies ran while one was open for 5% -> 7% of each run, Pallas kernels for 40% -> 36%
where the time goes in v4:
time: 203 us; the launch traced here: 202 us
  starting transfers between devices  78.4 us (39%)
  Pallas kernels  75.9 us (37%)
  waiting for transfers between devices  29.7 us (15%)
  other arithmetic  10.4 us (5%)
  local copies, waits for them, and re-layouts  6.41 us (3%)
    pallas_call x6, Pallas kernels, far_call(): pl.pallas_call(kernel, out_shape=out_shape, in_specs=[SCALAR] * len(scala...  50 us
    pallas_call x8, Pallas kernels, plain(): pl.pallas_call(body, out_shape=[jax.ShapeDtypeStruct(shape, out[1]) for s...  25.9 us
    all_to_all x4, starting transfers between devices, scattered(): lax.all_to_all(pair.reshape(8, LOCAL, -1), 'tensor', 0, 0, axis_index_gro...  22.4 us
    ppermute x6, starting transfers between devices, shifted(): lax.ppermute(value, 'section', [(i, (i + by) % 16) for i in range(16)])  18.8 us
    all_to_all x4, starting transfers between devices, landed_rows(): lax.all_to_all(copies, 'tensor', 0, 0, axis_index_groups=GROUPS, tiled=True)  18.4 us
    ppermute x9, starting transfers between devices, other_core(): return lax.ppermute(value, 'tensor', [(i, i ^ 1) for i in range(16)])  11.9 us
    ppermute x6, waiting for transfers between devices, shifted(): lax.ppermute(value, 'section', [(i, (i + by) % 16) for i in range(16)])  10.2 us
    ppermute x3, waiting for transfers between devices, to_partner(): return lax.ppermute(value, 'section', [(i, i ^ 8) for i in range(16)])  8.08 us
  transfers between devices with their start and end apart: 26, of which 10 were waited for; matrix products, arithmetic and copies ran while one was open for 7% of the time, Pallas kernels for 36%

profile of v4, /device:TPU:1, one launch (start us, length us, event | category | flops | bytes accessed | tf_op | source)
XLA Modules:
  0.0 201.9 jit_solution(4514873881164410293)
XLA Ops:
  0.6 3.8 %collective-permute-start = (bf16[2,4,8,5120]{3,2,1,0:T(8,128)(2,1)}, bf16[2,4,8,5120]{3,2,1,0:T(8,128)(2,1)S(1)}, u32[]{:S(2)}, u32[]{:S(2)}) collective-permute-start(bf16[2,4,8,5120]{3,2,1,0:T(8,128)(2,1)} %bitcast.67), channel_id=1, source_target_pairs={{0,128},{16,144},{32,160},{48,176},{64,192},{80,208},{96,224},{112... | collective-permute-start | bytes 1966088 | tf_op jit(solution)/shard_map/ppermute | solution.py:30
  6.1 6.6 %collective-permute-start.1 = (f32[1,5248]{1,0:T(1,128)S(1)}, f32[1,5248]{1,0:T(1,128)S(1)}, u32[]{:S(2)}, u32[]{:S(2)}) collective-permute-start(f32[1,5248]{1,0:T(1,128)S(1)} %broadcast_in_dim.32), channel_id=1, source_target_pairs={{0,240},{16,0},{32,16},{48,32},{64,48},{80,64},{96,80},{112,96},{1... | collective-permute-start | bytes 62984 | tf_op jit(solution)/shard_map/ppermute | solution.py:34
  14.0 2.7 %shard_map.175.refs_5_ = bf16[8,8,5120]{2,1,0:T(8,128)(2,1)} custom-call(f32[24]{0:T(128)} %copy-done.15, bf16[4,8,5120]{2,1,0:T(8,128)(2,1)} %bitcast.68, f32[1,5120]{1,0:T(1,128)} %refs_3_.1), custom_call_target="tpu_custom_call" | custom-call | flops 2500000000 | bytes 1000 | tf_op jit(solution)/shard_map/pallas_call | solution.py:520
  16.7 3.3 %collective-permute-done.2.refs_1_ = f32[24]{0:T(128)S(1)} collective-permute-done((f32[24]{0:T(128)S(1)}, f32[24]{0:T(128)S(1)}, u32[]{:S(2)}, u32[]{:S(2)}) %collective-permute-start.2) | collective-permute-done | bytes 128 | tf_op jit(solution)/shard_map/ppermute | solution.py:34
  20.1 4.5 %all-to-all-start = ((bf16[8,8,5120]{2,1,0:T(8,128)(2,1)}), bf16[8,8,5120]{2,1,0:T(8,128)(2,1)S(1)}, u32[]{:S(2)}, u32[]{:S(2)}) async-start(bf16[8,8,5120]{2,1,0:T(8,128)(2,1)} %shard_map.175.refs_5_), calls=%async_computation | async-start | bytes 1310720 | tf_op jit(solution)/shard_map/all_to_all | solution.py:538
  24.5 2.7 %collective-permute-start.4 = (bf16[128,5120]{1,0:T(8,128)(2,1)}, bf16[128,5120]{1,0:T(8,128)(2,1)}, u32[]{:S(2)}, u32[]{:S(2)}) collective-permute-start(bf16[128,5120]{1,0:T(8,128)(2,1)} %bitcast.12.refs_3_.own_w), channel_id=1, source_target_pairs={{0,1},{1,0},{2,3},{3,2},{4,5},{5,4},{6,7},{7,6},{8,9},{9,8},{10,11... | collective-permute-start | bytes 3932168 | tf_op jit(solution)/shard_map/ppermute | solution.py:26
  27.8 4.6 %shard_map.176 = (bf16[8,8,15360]{2,1,0:T(8,128)(2,1)}, f32[8,5120]{1,0:T(8,128)}, f32[8,128]{1,0:T(8,128)}, f32[8,5120]{1,0:T(8,128)}, f32[8,128]{1,0:T(8,128)}) custom-call(f32[24]{0:T(128)} %copy-done.15, s32[1]{0:T(128)} %bitcast.17.refs_1_, bf16[2,4,8,5120]{3,2,1,0:T(8,128)(2,1)} %copy-done.16, bf16[4,8,5120]{2,1,0:T(8,128)(2,1)} %bitcast.71, ...), custom_call_target="tpu_custom_call" | custom-call | flops 2500000000 | bytes 1000 | tf_op jit(solution)/shard_map/pallas_call | solution.py:520
  33.3 5.4 %all-to-all-start.2 = ((bf16[8,8,15360]{2,1,0:T(8,128)(2,1)}), bf16[8,8,15360]{2,1,0:T(8,128)(2,1)S(1)}, u32[]{:S(2)}, u32[]{:S(2)}) async-start(bf16[8,8,15360]{2,1,0:T(8,128)(2,1)} %get-tuple-element.40.refs_8_), calls=%async_computation.2 | async-start | bytes 3932160 | tf_op jit(solution)/shard_map/all_to_all | solution.py:538
  43.0 8.7 %shard_map.177 = (bf16[64,5120]{1,0:T(8,128)(2,1)}, bf16[64,5120]{1,0:T(8,128)(2,1)}) custom-call(s32[1]{0:T(128)} %bitcast.2.parity, bf16[64,5120]{1,0:T(8,128)(2,1)} %bitcast.45, bf16[64,5120]{1,0:T(8,128)(2,1)} %collective-permute-done.3.refs_1_, bf16[5120,384]{1,0:T(8,128)(2,1)} %bitcast.58, bf16[128,5120]{1,0:T(8,128)(2,1)} %bitcast.12.refs_3_.own_w, ...), custom_call_target="tpu_custom_call" | custom-call | flops 8000000000 | bytes 1000 | tf_op jit(solution)/shard_map/pallas_call | solution.py:372
  56.9 6.2 %collective-permute-done.6.after = bf16[4,8,5120]{2,1,0:T(8,128)(2,1)} collective-permute-done((bf16[4,8,5120]{2,1,0:T(8,128)(2,1)}, bf16[4,8,5120]{2,1,0:T(8,128)(2,1)}, u32[]{:S(2)}, u32[]{:S(2)}) %collective-permute-start.6) | collective-permute-done | bytes 327712 | tf_op jit(solution)/shard_map/ppermute | solution.py:30
  64.3 5.0 %all-to-all-start.1 = ((bf16[8,8,5120]{2,1,0:T(8,128)(2,1)}), bf16[8,8,5120]{2,1,0:T(8,128)(2,1)}, u32[]{:S(2)}, u32[]{:S(2)}) async-start(bf16[8,8,5120]{2,1,0:T(8,128)(2,1)} %bitcast.19), calls=%async_computation.1 | async-start | bytes 1310720 | tf_op jit(solution)/shard_map/all_to_all | solution.py:548
  69.4 4.5 %shard_map.178.context_grad.after = f32[128,384]{1,0:T(8,128)} custom-call(bf16[64,15360]{1,0:T(8,128)(2,1)} %bitcast.41, bf16[64,15360]{1,0:T(8,128)(2,1)} %collective-permute-done.7.other, bf16[384,5120]{1,0:T(8,128)(2,1)} %bitcast.64, bf16[4,8,5120]{2,1,0:T(8,128)(2,1)} %collective-permute-done.6.after), custom_call_target="tpu_custom_call" | custom-call | flops 4000000000 | bytes 1000 | tf_op jit(solution)/shard_map/pallas_call | solution.py:372
  73.9 9.6 %shard_map.179 = (bf16[64,5120]{1,0:T(8,128)(2,1)}, bf16[64,5120]{1,0:T(8,128)(2,1)}) custom-call(s32[1]{0:T(128)} %bitcast.2.parity, bf16[64,15360]{1,0:T(8,128)(2,1)} %bitcast.42, bf16[64,15360]{1,0:T(8,128)(2,1)} %collective-permute-done.7.other, f32[128,384]{1,0:T(8,128)} %shard_map.178.context_grad.after, bf16[5120,384]{1,0:T(8,128)(2,1)} %bitcast.59, ...), custom_call_target="tpu_custom_call" | custom-call | flops 12000000000 | bytes 1000 | tf_op jit(solution)/shard_map/pallas_call | solution.py:372
  85.1 3.4 %shard_map.180 = (bf16[4,8,5120]{2,1,0:T(8,128)(2,1)}, bf16[8,5120]{1,0:T(8,128)(2,1)}) custom-call(f32[24]{0:T(128)} %copy-done.15, f32[24]{0:T(128)} %slice_bitcast_fusion.refs_1_, bf16[8,8,5120]{2,1,0:T(8,128)(2,1)} %all-to-all-done.1.refs_2_, bf16[4,8,5120]{2,1,0:T(8,128)(2,1)} %bitcast.70, f32[1,5120]{1,0:T(1,128)} %slice.7.refs_4_, ...), custom_call_target="tpu_custom_call" | custom-call | flops 2500000000 | bytes 1000 | tf_op jit(solution)/shard_map/pallas_call | solution.py:520
  88.5 2.8 %collective-permute-start.8 = (bf16[8,5120]{1,0:T(8,128)(2,1)}, bf16[8,5120]{1,0:T(8,128)(2,1)S(1)}, u32[]{:S(2)}, u32[]{:S(2)}) collective-permute-start(bf16[8,5120]{1,0:T(8,128)(2,1)} %get-tuple-element.45), channel_id=1, source_target_pairs={{0,16},{16,32},{32,48},{48,64},{64,80},{80,96},{96,112},{112,128},... | collective-permute-start | bytes 245768 | tf_op jit(solution)/shard_map/ppermute | solution.py:34
  92.3 6.9 %collective-permute-done.8.refs_2_ = bf16[8,5120]{1,0:T(8,128)(2,1)S(1)} collective-permute-done((bf16[8,5120]{1,0:T(8,128)(2,1)}, bf16[8,5120]{1,0:T(8,128)(2,1)S(1)}, u32[]{:S(2)}, u32[]{:S(2)}) %collective-permute-start.8) | collective-permute-done | bytes 81952 | tf_op jit(solution)/shard_map/ppermute | solution.py:34
  99.2 7.5 %all-to-all-start.4 = ((bf16[8,8,5120]{2,1,0:T(8,128)(2,1)}), bf16[8,8,5120]{2,1,0:T(8,128)(2,1)S(1)}, u32[]{:S(2)}, u32[]{:S(2)}) async-start(bf16[8,8,5120]{2,1,0:T(8,128)(2,1)} %bitcast.23), calls=%async_computation.4 | async-start | bytes 1310720 | tf_op jit(solution)/shard_map/all_to_all | solution.py:548
  106.7 2.8 %shard_map.181.after = bf16[8,8,5120]{2,1,0:T(8,128)(2,1)} custom-call(f32[24]{0:T(128)} %copy-done.15, s32[1]{0:T(128)} %bitcast.3.refs_1_, bf16[8,5120]{1,0:T(8,128)(2,1)} %copy-done.18, bf16[4,8,5120]{2,1,0:T(8,128)(2,1)} %bitcast.50, f32[1,5120]{1,0:T(1,128)} %refs_3_.1), custom_call_target="tpu_custom_call" | custom-call | flops 2500000000 | bytes 1000 | tf_op jit(solution)/shard_map/pallas_call | solution.py:520
  109.5 5.7 %shard_map.182.refs_7_.projected = bf16[128,640]{1,0:T(8,128)(2,1)} custom-call(s32[1]{0:T(128)} %bitcast.2.parity, bf16[64,15360]{1,0:T(8,128)(2,1)} %bitcast.43, bf16[64,15360]{1,0:T(8,128)(2,1)} %collective-permute-done.7.other, bf16[5120,384]{1,0:T(8,128)(2,1)} %bitcast.60, bf16[128,5120]{1,0:T(8,128)(2,1)} %bitcast.12.refs_3_.own_w, ...), custom_call_target="tpu_custom_call" | custom-call | flops 5000000000 | bytes 1000 | tf_op jit(solution)/shard_map/pallas_call | solution.py:372
  116.4 4.7 %all-to-all-start.3 = ((bf16[8,8,5120]{2,1,0:T(8,128)(2,1)}), bf16[8,8,5120]{2,1,0:T(8,128)(2,1)S(1)}, u32[]{:S(2)}, u32[]{:S(2)}) async-start(bf16[8,8,5120]{2,1,0:T(8,128)(2,1)} %shard_map.181.after), calls=%async_computation.3 | async-start | bytes 1310720 | tf_op jit(solution)/shard_map/all_to_all | solution.py:538
  121.1 3.4 %shard_map.183 = (bf16[4,8,5120]{2,1,0:T(8,128)(2,1)}, bf16[8,5120]{1,0:T(8,128)(2,1)}) custom-call(f32[24]{0:T(128)} %copy-done.15, f32[24]{0:T(128)} %copy-done.20, bf16[8,8,5120]{2,1,0:T(8,128)(2,1)} %copy-done.6, bf16[4,8,5120]{2,1,0:T(8,128)(2,1)} %bitcast.72, f32[1,5120]{1,0:T(1,128)} %refs_3_.1, f32[8,5120]{1,0:T(8,128)} %get-tuple-element.53.refs_5_, ...), custom_call_target="tpu_custom_call" | custom-call | flops 2500000000 | bytes 1000 | tf_op jit(solution)/shard_map/pallas_call | solution.py:520
  126.9 4.3 %all-to-all-done.3 = bf16[8,8,5120]{2,1,0:T(8,128)(2,1)S(1)} async-done(((bf16[8,8,5120]{2,1,0:T(8,128)(2,1)}), bf16[8,8,5120]{2,1,0:T(8,128)(2,1)S(1)}, u32[]{:S(2)}, u32[]{:S(2)}) %all-to-all-start.3) | async-done | bytes 655392 | tf_op jit(solution)/shard_map/all_to_all | solution.py:538
  131.2 3.2 %collective-permute-start.11 = (bf16[64,5120]{1,0:T(8,128)(2,1)S(1)}, bf16[64,5120]{1,0:T(8,128)(2,1)S(1)}, u32[]{:S(2)}, u32[]{:S(2)}) collective-permute-start(bf16[64,5120]{1,0:T(8,128)(2,1)S(1)} %bitcast.48), channel_id=1, source_target_pairs={{0,1},{1,0},{2,3},{3,2},{4,5},{5,4},{6,7},{7,6},{8,9},{9,8},{10,11... | collective-permute-start | bytes 1966088 | tf_op jit(solution)/shard_map/ppermute | solution.py:26
  134.3 2.7 %shard_map.184.refs_8_ = bf16[8,8,5120]{2,1,0:T(8,128)(2,1)} custom-call(f32[24]{0:T(128)} %copy-done.15, s32[1]{0:T(128)} %bitcast.24.refs_1_, bf16[8,5120]{1,0:T(8,128)(2,1)} %copy-done.19, bf16[4,8,5120]{2,1,0:T(8,128)(2,1)} %bitcast.51), custom_call_target="tpu_custom_call" | custom-call | flops 2500000000 | bytes 1000 | tf_op jit(solution)/shard_map/pallas_call | solution.py:520
  137.1 3.8 %all-to-all-start.5 = ((bf16[8,8,5120]{2,1,0:T(8,128)(2,1)}), bf16[8,8,5120]{2,1,0:T(8,128)(2,1)S(1)}, u32[]{:S(2)}, u32[]{:S(2)}) async-start(bf16[8,8,5120]{2,1,0:T(8,128)(2,1)} %shard_map.184.refs_8_), calls=%async_computation.5 | async-start | bytes 1310720 | tf_op jit(solution)/shard_map/all_to_all | solution.py:538
  141.7 8.6 %shard_map.185 = (bf16[64,5120]{1,0:T(8,128)(2,1)}, bf16[64,5120]{1,0:T(8,128)(2,1)}) custom-call(s32[1]{0:T(128)} %bitcast.2.parity, bf16[64,5120]{1,0:T(8,128)(2,1)} %bitcast.49, bf16[64,5120]{1,0:T(8,128)(2,1)} %copy-done.17, bf16[5120,384]{1,0:T(8,128)(2,1)} %bitcast.61, bf16[128,5120]{1,0:T(8,128)(2,1)} %bitcast.12.refs_3_.own_w, ...), custom_call_target="tpu_custom_call" | custom-call | flops 8000000000 | bytes 1000 | tf_op jit(solution)/shard_map/pallas_call | solution.py:372
  152.9 5.7 %collective-permute-start.15 = (bf16[4,8,5120]{2,1,0:T(8,128)(2,1)}, bf16[4,8,5120]{2,1,0:T(8,128)(2,1)S(1)}, u32[]{:S(2)}, u32[]{:S(2)}) collective-permute-start(bf16[4,8,5120]{2,1,0:T(8,128)(2,1)} %get-tuple-element.66), channel_id=1, source_target_pairs={{0,240},{16,0},{32,16},{48,32},{64,48},{80,64},{96,80},{112,96},{1... | collective-permute-start | bytes 983048 | tf_op jit(solution)/shard_map/ppermute | solution.py:34
  160.7 4.5 %all-to-all-start.6 = ((bf16[8,8,5120]{2,1,0:T(8,128)(2,1)}), bf16[8,8,5120]{2,1,0:T(8,128)(2,1)S(1)}, u32[]{:S(2)}, u32[]{:S(2)}) async-start(bf16[8,8,5120]{2,1,0:T(8,128)(2,1)} %bitcast.27), calls=%async_computation.6 | async-start | bytes 1310720 | tf_op jit(solution)/shard_map/all_to_all | solution.py:548
  165.2 12.8 %shard_map.186 = (bf16[64,5120]{1,0:T(8,128)(2,1)}, bf16[64,5120]{1,0:T(8,128)(2,1)}) custom-call(s32[1]{0:T(128)} %bitcast.2.parity, bf16[64,5120]{1,0:T(8,128)(2,1)} %bitcast.47, bf16[64,5120]{1,0:T(8,128)(2,1)} %collective-permute-done.14.other, bf16[128,640]{1,0:T(8,128)(2,1)} %shard_map.182.refs_7_.projected, bf16[5120,384]{1,0:T(8,128)(2,1)} %bitcast.62, ...), custom_call_target="tpu_custom_call" | custom-call | flops 12000000000 | bytes 1000 | tf_op jit(solution)/shard_map/pallas_call | solution.py:372
  182.1 5.4 %all-to-all-start.7 = ((bf16[8,8,5120]{2,1,0:T(8,128)(2,1)}), bf16[8,8,5120]{2,1,0:T(8,128)(2,1)S(1)}, u32[]{:S(2)}, u32[]{:S(2)}) async-start(bf16[8,8,5120]{2,1,0:T(8,128)(2,1)} %bitcast.29), calls=%async_computation.7 | async-start | bytes 1310720 | tf_op jit(solution)/shard_map/all_to_all | solution.py:548
  192.0 3.0 %shard_map.187.refs_6_ = bf16[4,8,5120]{2,1,0:T(8,128)(2,1)} custom-call(f32[24]{0:T(128)} %copy-done.15, bf16[8,8,5120]{2,1,0:T(8,128)(2,1)} %copy-done.3, bf16[4,8,5120]{2,1,0:T(8,128)(2,1)} %copy-done.12, bf16[64,5120]{1,0:T(8,128)(2,1)} %add_convert_fusion.refs_3_), custom_call_target="tpu_custom_call" | custom-call | flops 2500000000 | bytes 1000 | tf_op jit(solution)/shard_map/pallas_call | solution.py:520
  198.4 3.3 %shard_map.188 = bf16[4,8,5120]{2,1,0:T(8,128)(2,1)} custom-call(f32[24]{0:T(128)} %copy-done.15, bf16[8,8,5120]{2,1,0:T(8,128)(2,1)} %copy-done.7, bf16[4,8,5120]{2,1,0:T(8,128)(2,1)} %broadcast_select_fusion.refs_2_, f32[1,5120]{1,0:T(1,128)} %refs_3_.1, f32[8,5120]{1,0:T(8,128)} %get-tuple-element.69.refs_4_, f32[8,128]{1,0:T(8,128)} %get-tuple-element.70.refs_5_, ...), custom_call_target="tpu_custom_call" | custom-call | flops 2500000000 | bytes 1000 | tf_op jit(solution)/shard_map/pallas_call | solution.py:520
  (92 shorter events, 38.6 us)
Async XLA Ops:
  0.6 26.6 %copy-start = (s32[16,2]{0,1:T(2,128)S(1)}, s32[16,2]{0,1:T(2,128)}, u32[]{:S(2)}) copy-start(s32[16,2]{0,1:T(2,128)} %param.21) | copy-start | bytes 388
  0.6 19.4 %collective-permute-start = (bf16[2,4,8,5120]{3,2,1,0:T(8,128)(2,1)}, bf16[2,4,8,5120]{3,2,1,0:T(8,128)(2,1)S(1)}, u32[]{:S(2)}, u32[]{:S(2)}) collective-permute-start(bf16[2,4,8,5120]{3,2,1,0:T(8,128)(2,1)} %bitcast.67), channel_id=1, source_target_pairs={{0,128},{16,144},{32,160},{48,176},{64,192},{80,208},{96,224},{112... | collective-permute-start | bytes 1966088 | tf_op jit(solution)/shard_map/ppermute | solution.py:30
  6.1 14.0 %collective-permute-start.1 = (f32[1,5248]{1,0:T(1,128)S(1)}, f32[1,5248]{1,0:T(1,128)S(1)}, u32[]{:S(2)}, u32[]{:S(2)}) collective-permute-start(f32[1,5248]{1,0:T(1,128)S(1)} %broadcast_in_dim.32), channel_id=1, source_target_pairs={{0,240},{16,0},{32,16},{48,32},{64,48},{80,64},{96,80},{112,96},{1... | collective-permute-start | bytes 62984 | tf_op jit(solution)/shard_map/ppermute | solution.py:34
  13.4 6.6 %collective-permute-start.2 = (f32[24]{0:T(128)S(1)}, f32[24]{0:T(128)S(1)}, u32[]{:S(2)}, u32[]{:S(2)}) collective-permute-start(f32[24]{0:T(128)S(1)} %pad_maximum_fusion.refs_0_), channel_id=1, source_target_pairs={{0,16},{16,32},{32,48},{48,64},{64,80},{80,96},{96,112},{112,128},... | collective-permute-start | bytes 296 | tf_op jit(solution)/shard_map/ppermute | solution.py:34
  20.0 12.4 %copy-start.20 = (f32[24]{0:T(128)}, f32[24]{0:T(128)S(1)}, u32[]{:S(2)}) copy-start(f32[24]{0:T(128)S(1)} %collective-permute-done.2.refs_1_) | copy-start | bytes 292
  20.1 12.4 %all-to-all-start = ((bf16[8,8,5120]{2,1,0:T(8,128)(2,1)}), bf16[8,8,5120]{2,1,0:T(8,128)(2,1)S(1)}, u32[]{:S(2)}, u32[]{:S(2)}) async-start(bf16[8,8,5120]{2,1,0:T(8,128)(2,1)} %shard_map.175.refs_5_), calls=%async_computation | async-start | bytes 1310720 | tf_op jit(solution)/shard_map/all_to_all | solution.py:538
  24.5 17.2 %collective-permute-start.4 = (bf16[128,5120]{1,0:T(8,128)(2,1)}, bf16[128,5120]{1,0:T(8,128)(2,1)}, u32[]{:S(2)}, u32[]{:S(2)}) collective-permute-start(bf16[128,5120]{1,0:T(8,128)(2,1)} %bitcast.12.refs_3_.own_w), channel_id=1, source_target_pairs={{0,1},{1,0},{2,3},{3,2},{4,5},{5,4},{6,7},{7,6},{8,9},{9,8},{10,11... | collective-permute-start | bytes 3932168 | tf_op jit(solution)/shard_map/ppermute | solution.py:26
  32.5 8.5 %copy-start.13 = (f32[4,128,128]{2,1,0:T(8,128)S(1)}, f32[4,128,128]{2,1,0:T(8,128)}, u32[]{:S(2)}) copy-start(f32[4,128,128]{2,1,0:T(8,128)} %constant.31.clone) | copy-start | bytes 786436
  32.5 8.5 %copy-start.14 = (f32[4,128,128]{2,1,0:T(8,128)S(1)}, f32[4,128,128]{2,1,0:T(8,128)}, u32[]{:S(2)}) copy-start(f32[4,128,128]{2,1,0:T(8,128)} %constant.32.clone) | copy-start | bytes 786436
  33.3 30.3 %all-to-all-start.2 = ((bf16[8,8,15360]{2,1,0:T(8,128)(2,1)}), bf16[8,8,15360]{2,1,0:T(8,128)(2,1)S(1)}, u32[]{:S(2)}, u32[]{:S(2)}) async-start(bf16[8,8,15360]{2,1,0:T(8,128)(2,1)} %get-tuple-element.40.refs_8_), calls=%async_computation.2 | async-start | bytes 3932160 | tf_op jit(solution)/shard_map/all_to_all | solution.py:538
  38.7 4.3 %collective-permute-start.3 = (bf16[64,5120]{1,0:T(8,128)(2,1)}, bf16[64,5120]{1,0:T(8,128)(2,1)}, u32[]{:S(2)}, u32[]{:S(2)}) collective-permute-start(bf16[64,5120]{1,0:T(8,128)(2,1)} %bitcast.44), channel_id=1, source_target_pairs={{0,1},{1,0},{2,3},{3,2},{4,5},{5,4},{6,7},{7,6},{8,9},{9,8},{10,11... | collective-permute-start | bytes 1966088 | tf_op jit(solution)/shard_map/ppermute | solution.py:26
  51.7 3.1 %collective-permute-start.5 = (bf16[64,5120]{1,0:T(8,128)(2,1)}, bf16[64,5120]{1,0:T(8,128)(2,1)S(1)}, u32[]{:S(2)}, u32[]{:S(2)}) collective-permute-start(bf16[64,5120]{1,0:T(8,128)(2,1)} %get-tuple-element.42), channel_id=1, source_target_pairs={{0,1},{1,0},{2,3},{3,2},{4,5},{5,4},{6,7},{7,6},{8,9},{9,8},{10,11... | collective-permute-start | bytes 1966088 | tf_op jit(solution)/shard_map/ppermute | solution.py:26
  52.1 11.0 %collective-permute-start.6 = (bf16[4,8,5120]{2,1,0:T(8,128)(2,1)}, bf16[4,8,5120]{2,1,0:T(8,128)(2,1)}, u32[]{:S(2)}, u32[]{:S(2)}) collective-permute-start(bf16[4,8,5120]{2,1,0:T(8,128)(2,1)} %bitcast.69), channel_id=1, source_target_pairs={{0,128},{16,144},{32,160},{48,176},{64,192},{80,208},{96,224},{112... | collective-permute-start | bytes 983048 | tf_op jit(solution)/shard_map/ppermute | solution.py:30
  63.6 5.8 %collective-permute-start.7 = (bf16[64,15360]{1,0:T(8,128)(2,1)S(1)}, bf16[64,15360]{1,0:T(8,128)(2,1)}, u32[]{:S(2)}, u32[]{:S(2)}) collective-permute-start(bf16[64,15360]{1,0:T(8,128)(2,1)S(1)} %bitcast.40), channel_id=1, source_target_pairs={{0,1},{1,0},{2,3},{3,2},{4,5},{5,4},{6,7},{7,6},{8,9},{9,8},{10,11... | collective-permute-start | bytes 5898248 | tf_op jit(solution)/shard_map/ppermute | solution.py:26
  64.3 20.8 %all-to-all-start.1 = ((bf16[8,8,5120]{2,1,0:T(8,128)(2,1)}), bf16[8,8,5120]{2,1,0:T(8,128)(2,1)}, u32[]{:S(2)}, u32[]{:S(2)}) async-start(bf16[8,8,5120]{2,1,0:T(8,128)(2,1)} %bitcast.19), calls=%async_computation.1 | async-start | bytes 1310720 | tf_op jit(solution)/shard_map/all_to_all | solution.py:548
  83.6 7.7 %collective-permute-start.9 = (bf16[64,5120]{1,0:T(8,128)(2,1)}, bf16[64,5120]{1,0:T(8,128)(2,1)S(1)}, u32[]{:S(2)}, u32[]{:S(2)}) collective-permute-start(bf16[64,5120]{1,0:T(8,128)(2,1)} %get-tuple-element.48), channel_id=1, source_target_pairs={{0,1},{1,0},{2,3},{3,2},{4,5},{5,4},{6,7},{7,6},{8,9},{9,8},{10,11... | collective-permute-start | bytes 1966088 | tf_op jit(solution)/shard_map/ppermute | solution.py:26
  88.5 10.7 %collective-permute-start.8 = (bf16[8,5120]{1,0:T(8,128)(2,1)}, bf16[8,5120]{1,0:T(8,128)(2,1)S(1)}, u32[]{:S(2)}, u32[]{:S(2)}) collective-permute-start(bf16[8,5120]{1,0:T(8,128)(2,1)} %get-tuple-element.45), channel_id=1, source_target_pairs={{0,16},{16,32},{32,48},{48,64},{64,80},{80,96},{96,112},{112,128},... | collective-permute-start | bytes 245768 | tf_op jit(solution)/shard_map/ppermute | solution.py:34
  99.2 17.2 %all-to-all-start.4 = ((bf16[8,8,5120]{2,1,0:T(8,128)(2,1)}), bf16[8,8,5120]{2,1,0:T(8,128)(2,1)S(1)}, u32[]{:S(2)}, u32[]{:S(2)}) async-start(bf16[8,8,5120]{2,1,0:T(8,128)(2,1)} %bitcast.23), calls=%async_computation.4 | async-start | bytes 1310720 | tf_op jit(solution)/shard_map/all_to_all | solution.py:548
  116.4 14.8 %all-to-all-start.3 = ((bf16[8,8,5120]{2,1,0:T(8,128)(2,1)}), bf16[8,8,5120]{2,1,0:T(8,128)(2,1)S(1)}, u32[]{:S(2)}, u32[]{:S(2)}) async-start(bf16[8,8,5120]{2,1,0:T(8,128)(2,1)} %shard_map.181.after), calls=%async_computation.3 | async-start | bytes 1310720 | tf_op jit(solution)/shard_map/all_to_all | solution.py:538
  124.5 6.7 %collective-permute-start.10 = (bf16[8,5120]{1,0:T(8,128)(2,1)}, bf16[8,5120]{1,0:T(8,128)(2,1)S(1)}, u32[]{:S(2)}, u32[]{:S(2)}) collective-permute-start(bf16[8,5120]{1,0:T(8,128)(2,1)} %get-tuple-element.55), channel_id=1, source_target_pairs={{0,240},{16,0},{32,16},{48,32},{64,48},{80,64},{96,80},{112,96},{1... | collective-permute-start | bytes 245768 | tf_op jit(solution)/shard_map/ppermute | solution.py:34
  131.2 9.7 %collective-permute-start.11 = (bf16[64,5120]{1,0:T(8,128)(2,1)S(1)}, bf16[64,5120]{1,0:T(8,128)(2,1)S(1)}, u32[]{:S(2)}, u32[]{:S(2)}) collective-permute-start(bf16[64,5120]{1,0:T(8,128)(2,1)S(1)} %bitcast.48), channel_id=1, source_target_pairs={{0,1},{1,0},{2,3},{3,2},{4,5},{5,4},{6,7},{7,6},{8,9},{9,8},{10,11... | collective-permute-start | bytes 1966088 | tf_op jit(solution)/shard_map/ppermute | solution.py:26
  137.1 15.5 %all-to-all-start.5 = ((bf16[8,8,5120]{2,1,0:T(8,128)(2,1)}), bf16[8,8,5120]{2,1,0:T(8,128)(2,1)S(1)}, u32[]{:S(2)}, u32[]{:S(2)}) async-start(bf16[8,8,5120]{2,1,0:T(8,128)(2,1)} %shard_map.184.refs_8_), calls=%async_computation.5 | async-start | bytes 1310720 | tf_op jit(solution)/shard_map/all_to_all | solution.py:538
  150.3 8.3 %collective-permute-start.12 = (bf16[64,5120]{1,0:T(8,128)(2,1)}, bf16[64,5120]{1,0:T(8,128)(2,1)S(1)}, u32[]{:S(2)}, u32[]{:S(2)}) collective-permute-start(bf16[64,5120]{1,0:T(8,128)(2,1)} %get-tuple-element.59), channel_id=1, source_target_pairs={{0,1},{1,0},{2,3},{3,2},{4,5},{5,4},{6,7},{7,6},{8,9},{9,8},{10,11... | collective-permute-start | bytes 1966088 | tf_op jit(solution)/shard_map/ppermute | solution.py:26
  151.2 26.9 %collective-permute-start.13 = (bf16[4,8,5120]{2,1,0:T(8,128)(2,1)}, bf16[4,8,5120]{2,1,0:T(8,128)(2,1)}, u32[]{:S(2)}, u32[]{:S(2)}) collective-permute-start(bf16[4,8,5120]{2,1,0:T(8,128)(2,1)} %get-tuple-element.62), channel_id=1, source_target_pairs={{0,16},{16,32},{32,48},{48,64},{64,80},{80,96},{96,112},{112,128},... | collective-permute-start | bytes 983048 | tf_op jit(solution)/shard_map/ppermute | solution.py:34
  152.6 12.7 %collective-permute-start.14 = (bf16[64,5120]{1,0:T(8,128)(2,1)S(1)}, bf16[64,5120]{1,0:T(8,128)(2,1)}, u32[]{:S(2)}, u32[]{:S(2)}) collective-permute-start(bf16[64,5120]{1,0:T(8,128)(2,1)S(1)} %bitcast.46), channel_id=1, source_target_pairs={{0,1},{1,0},{2,3},{3,2},{4,5},{5,4},{6,7},{7,6},{8,9},{9,8},{10,11... | collective-permute-start | bytes 1966088 | tf_op jit(solution)/shard_map/ppermute | solution.py:26
  152.9 26.2 %collective-permute-start.15 = (bf16[4,8,5120]{2,1,0:T(8,128)(2,1)}, bf16[4,8,5120]{2,1,0:T(8,128)(2,1)S(1)}, u32[]{:S(2)}, u32[]{:S(2)}) collective-permute-start(bf16[4,8,5120]{2,1,0:T(8,128)(2,1)} %get-tuple-element.66), channel_id=1, source_target_pairs={{0,240},{16,0},{32,16},{48,32},{64,48},{80,64},{96,80},{112,96},{1... | collective-permute-start | bytes 983048 | tf_op jit(solution)/shard_map/ppermute | solution.py:34
  160.7 21.4 %all-to-all-start.6 = ((bf16[8,8,5120]{2,1,0:T(8,128)(2,1)}), bf16[8,8,5120]{2,1,0:T(8,128)(2,1)S(1)}, u32[]{:S(2)}, u32[]{:S(2)}) async-start(bf16[8,8,5120]{2,1,0:T(8,128)(2,1)} %bitcast.27), calls=%async_computation.6 | async-start | bytes 1310720 | tf_op jit(solution)/shard_map/all_to_all | solution.py:548
  165.2 13.9 %copy-start.10 = (bf16[1,4,8,5120]{3,2,1,0:T(8,128)(2,1)S(1)}, bf16[1,4,8,5120]{3,2,1,0:T(8,128)(2,1)}, u32[]{:S(2)}) copy-start(bf16[1,4,8,5120]{3,2,1,0:T(8,128)(2,1)} %param.18) | copy-start | bytes 983044
  178.1 3.0 %collective-permute-start.16 = (bf16[64,5120]{1,0:T(8,128)(2,1)}, bf16[64,5120]{1,0:T(8,128)(2,1)S(1)}, u32[]{:S(2)}, u32[]{:S(2)}) collective-permute-start(bf16[64,5120]{1,0:T(8,128)(2,1)} %get-tuple-element.68), channel_id=1, source_target_pairs={{0,1},{1,0},{2,3},{3,2},{4,5},{5,4},{6,7},{7,6},{8,9},{9,8},{10,11... | collective-permute-start | bytes 1966088 | tf_op jit(solution)/shard_map/ppermute | solution.py:26
  179.2 10.9 %collective-permute-start.17 = (bf16[4,8,5120]{2,1,0:T(8,128)(2,1)S(1)}, bf16[4,8,5120]{2,1,0:T(8,128)(2,1)S(1)}, u32[]{:S(2)}, u32[]{:S(2)}) collective-permute-start(bf16[4,8,5120]{2,1,0:T(8,128)(2,1)S(1)} %broadcast_select_fusion.1.refs_2_), channel_id=1, source_target_pairs={{0,128},{16,144},{32,160},{48,176},{64,192},{80,208},{96,224},{112... | collective-permute-start | bytes 983048 | tf_op jit(solution)/shard_map/ppermute | solution.py:30
  182.1 9.9 %copy-start.3 = (bf16[8,8,5120]{2,1,0:T(8,128)(2,1)}, bf16[8,8,5120]{2,1,0:T(8,128)(2,1)S(1)}, u32[]{:S(2)}) copy-start(bf16[8,8,5120]{2,1,0:T(8,128)(2,1)S(1)} %all-to-all-done.6.refs_1_) | copy-start | bytes 1966084
  182.1 15.5 %all-to-all-start.7 = ((bf16[8,8,5120]{2,1,0:T(8,128)(2,1)}), bf16[8,8,5120]{2,1,0:T(8,128)(2,1)S(1)}, u32[]{:S(2)}, u32[]{:S(2)}) async-start(bf16[8,8,5120]{2,1,0:T(8,128)(2,1)} %bitcast.29), calls=%async_computation.7 | async-start | bytes 1310720 | tf_op jit(solution)/shard_map/all_to_all | solution.py:548
  (15 other events, 66.4 us)
